TPU v7x, 512 devices: a whole 4x8x8 slice. The times are simulated.
512 devices in a mesh: slab: 64 (over z, y_hi, core), chaos: 8 (over y_lo, x).
Axes of the slice: x: 4, y: 8 (y_hi: 4, y_lo: 2; y = y_hi * 2 + y_lo), z: 8, core: 2. Of those that a mesh axis runs over, the one named last changes fastest.
Arguments:
- rhs: float32 [120, 64, 8, 128], P('chaos', 'slab'), may hold values from -6 to 6
- guess: float32 [120, 64, 8, 128], P('chaos', 'slab'), may hold values from -6 to 6
- coef: float32 [36, 64, 8, 128], P(None, 'slab'), may hold values from 0.1 to 1
- block_triples: int32 [48, 3], replicated, may hold values from 0 to 7, as said below
- offsets: int32 [9], replicated, may hold values from 0 to 36, as said below
- values: float32 [48, 15, 12, 15], replicated, may hold values from -0.1875 to 0.1875
Outputs:
- solution: float32 [120, 64, 8, 128], P('chaos', 'slab')
- residual: float32 [120, 64, 8, 128], P('chaos', 'slab')
Inputs may be any that keep to these rules, and one draw needn't show every extreme that they name: `block_triples`: rows offsets[I] to offsets[I+1]-1 have first entry I, and within one output block the pairs of second and third entries are distinct; third entries are below 3. Each output block has 3 to 6 rows, exactly 6 for some block; blocks 2p and 2p + 1 together have 6 // 2 + 6 rows. Rows from offsets[8] on are zero and unused. offsets[0] = 0, offsets rise by 3 to 6 from block to block, and offsets[8] = 36.
All inputs are finite; a program needn't handle non-finite values.
Results may differ from a plain program's by a relative error of at most 0.0001.
Values sent between devices are 32-bit elements; how exact they have to be, the bound alone decides.
No kernel may reach another device: no remote copies, remote signals or barrier semaphores. Data moves between devices by JAX's collectives and lax.ppermute only.
A program may use at most 64 MiB of HBM per device.

v0:
```python
import jax
import jax.numpy as jnp
from jax import lax
from jax.sharding import PartitionSpec as P

MODE_BLK = 15
COEF_BLK = 12
ITERS = 3


relax = 0.1


def extended(x, sides, width):
    for axis, dim in sides:
        peers, length = (lax.axis_size(axis), x.shape[dim])
        up = [(i, (i + 1) % peers) for i in range(peers - 1)]
        down = [(j, i) for i, j in up]
        last = lax.slice_in_dim(x, length - width, length, axis=dim)
        initial = lax.slice_in_dim(x, 0, width, axis=dim)
        before = lax.ppermute(last, axis, up)
        after = lax.ppermute(initial, axis, down)
        x = jnp.concatenate([before, x, after], axis=dim)
    return x


def face_coefs(padded):
    core = padded[:, 1:-1]
    count = padded.shape[0]
    along_x = 0.5 * (core + jnp.roll(core, -1, axis=3))
    along_y = 0.5 * (core + jnp.roll(core, -1, axis=2))
    along_z = 0.5 * (padded[:, :-1] + padded[:, 1:])
    return jnp.concatenate(
        [along_x.reshape(count, -1), along_y.reshape(count, -1), along_z.reshape(count, -1)], axis=1
    )


def gradients(padded):
    core = padded[:, 1:-1]
    count = padded.shape[0]
    grad_x = jnp.roll(core, -1, axis=3) - core
    grad_y = jnp.roll(core, -1, axis=2) - core
    grad_z = padded[:, 1:] - padded[:, :-1]
    return jnp.concatenate(
        [grad_x.reshape(count, -1), grad_y.reshape(count, -1), grad_z.reshape(count, -1)], axis=1
    )


def divergence(flux, planes, rows, cols):
    count = flux.shape[0]
    cells = planes * rows * cols
    flux_x = flux[:, :cells].reshape(count, planes, rows, cols)
    flux_y = flux[:, cells : 2 * cells].reshape(count, planes, rows, cols)
    flux_z = flux[:, 2 * cells :].reshape(count, planes + 1, rows, cols)
    return (
        jnp.roll(flux_x, 1, axis=3)
        - flux_x
        + (jnp.roll(flux_y, 1, axis=2) - flux_y)
        + (flux_z[:, :-1] - flux_z[:, 1:])
    )


def coupling(table, grads_block, coef_block):
    mixed = jnp.dot(
        table.reshape(-1, table.shape[-1]),
        grads_block,
        precision=lax.Precision.HIGHEST,
        preferred_element_type=jnp.float32,
    )
    mixed = mixed.reshape(table.shape[0], table.shape[1], -1)
    return jnp.sum(mixed * coef_block[None], axis=1)


def gathered_image(field, a_faces, block_triples, offsets, values, first):
    whole = lax.all_gather(field, "chaos", axis=0, tiled=True)
    padded = extended(whole, (("slab", 1),), 1)
    grads = gradients(padded)

    def add_triple(index, flux):
        triple = block_triples[index]
        grads_block = lax.dynamic_slice_in_dim(grads, triple[1] * MODE_BLK, MODE_BLK, 0)
        coef_block = lax.dynamic_slice_in_dim(a_faces, triple[2] * COEF_BLK, COEF_BLK, 0)
        return flux + coupling(values[index], grads_block, coef_block)

    block_out = first + 0
    start_flux = jnp.zeros((MODE_BLK, grads.shape[1]), jnp.float32)
    pieces = lax.fori_loop(offsets[block_out], offsets[block_out + 1], add_triple, start_flux)
    flux = pieces
    return divergence(flux, field.shape[1], field.shape[2], field.shape[3])


def body(rhs, guess, coef, block_triples, offsets, values):
    local_blocks = rhs.shape[0] // MODE_BLK
    coef_padded = extended(coef, (("slab", 1),), 1)
    a_faces = face_coefs(coef_padded)
    first = lax.axis_index("chaos") * local_blocks
    solution = guess
    residual = rhs
    for step in range(ITERS):
        image = gathered_image(solution, a_faces, block_triples, offsets, values, first)
        residual = rhs - image
        solution = solution + relax * residual
    return (solution, residual)


def solution(mesh):
    placed = (
        P("chaos", "slab", None, None),
        P("chaos", "slab", None, None),
        P(None, "slab", None, None),
        P(),
        P(),
        P(),
    )
    return jax.shard_map(
        body,
        mesh=mesh,
        in_specs=placed,
        out_specs=(P("chaos", "slab", None, None), P("chaos", "slab", None, None)),
        check_vma=False,
    )
```

profile of v0, /device:TPU:270, one launch (start us, length us, event | category | flops | bytes accessed | tf_op | source)
XLA Modules:
  0.0 297.5 jit_solution(17128256986682455426)
XLA Ops:
  0.6 29.1 %all_gather.9 = f32[120,1,8,128]{3,2,1,0:T(8,128)S(1)} all-gather(f32[15,1,8,128]{3,2,1,0:T(8,128)} %param.13), channel_id=1, replica_groups=mesh['slab'=64,'chaos'=8] {'chaos'}, dimensions={0}, use_global_device_ids=true | all-gather | bytes 552960 | tf_op jit(solution)/shard_map/all_gather | solution.py:75
  29.8 1.9 collective-permute-start
  31.7 2.4 collective-permute-start.1
  34.1 4.1 %collective-permute-start.2 = (f32[36,1,8,128]{3,2,1,0:T(8,128)}, f32[36,1,8,128]{3,2,1,0:T(8,128)}, u32[]{:S(2)}, u32[]{:S(2)}) collective-permute-start(f32[36,1,8,128]{3,2,1,0:T(8,128)} %param.14), channel_id=1, source_target_pairs={{0,8},{8,16},{16,24},{24,32},{32,40},{40,48},{48,56},{56,64},{64,7... | collective-permute-start | bytes 442376 | tf_op jit(solution)/shard_map/ppermute | solution.py:21
  38.2 5.7 %collective-permute-start.3 = (f32[36,1,8,128]{3,2,1,0:T(8,128)}, f32[36,1,8,128]{3,2,1,0:T(8,128)}, u32[]{:S(2)}, u32[]{:S(2)}) collective-permute-start(f32[36,1,8,128]{3,2,1,0:T(8,128)} %param.14), channel_id=1, source_target_pairs={{8,0},{16,8},{24,16},{32,24},{40,32},{48,40},{56,48},{64,56},{72,6... | collective-permute-start | bytes 442376 | tf_op jit(solution)/shard_map/ppermute | solution.py:22
  44.8 1.2 copy_bitcast_fusion.7
  46.0 0.6 fusion.44
  47.3 5.1 %copy.11 = f32[48,15,12,15]{3,1,2,0:T(8,128)} copy(f32[48,15,12,15]{0,3,2,1:T(8,128)S(1)} %copy-done.3) | data formatting | bytes 1036800 | tf_op jit(solution)/shard_map/while | solution.py:87
  52.4 2.2 collective-permute-done.2
  54.6 1.0 fusion.19
  55.8 1.2 maximum_subtract_fusion
  58.0 38.4 %while.30 = (s32[]{:T(128)}, f32[15,4096]{1,0:T(8,128)S(1)}, s32[]{:T(128)}, f32[48,15,12,15]{3,1,2,0:T(8,128)}, s32[48,3]{0,1:T(4,128)S(1)}, /*index=5*/f32[120...) while((s32[]{:T(128)}, f32[15,4096]{1,0:T(8,128)S(1)}, ...), condition=%wide.region_2.3_spmd, body=%wide.region_0.2_spmd.sunk | while | flops 134184976 | bytes 1999163 | solution.py:87
  58.8 0.5 fusion.59
  60.6 3.6 %fusion.60 = f32[15,4096]{1,0:T(8,128)S(1)} fusion(f32[12,4096]{1,0:T(8,128)S(1)} %constant_dynamic-slice_fusion.13, f32[120,4096]{1,0:T(8,128)S(1)} %get-tuple-element.406, s32[]{:T(128)S(6)} %select_n.53, f32[48,15,12,15]{3,1,2,0:T(8,128)} %get-tuple-element.404, s32[]{:T(128)S(6)} %select_n.51), kind=kOutput, calls=%fused_computation.1.clone.1 | convolution fusion | flops 134123520 | bytes 868360 | tf_op jit(solution)/shard_map/while/body/dot_general | solution.py:64
  65.0 0.5 fusion.59
  66.9 3.6 %fusion.60 = f32[15,4096]{1,0:T(8,128)S(1)} fusion(f32[12,4096]{1,0:T(8,128)S(1)} %constant_dynamic-slice_fusion.13, f32[120,4096]{1,0:T(8,128)S(1)} %get-tuple-element.406, s32[]{:T(128)S(6)} %select_n.53, f32[48,15,12,15]{3,1,2,0:T(8,128)} %get-tuple-element.404, s32[]{:T(128)S(6)} %select_n.51), kind=kOutput, calls=%fused_computation.1.clone.1 | convolution fusion | flops 134123520 | bytes 868360 | tf_op jit(solution)/shard_map/while/body/dot_general | solution.py:64
  71.3 0.5 fusion.59
  73.2 3.6 %fusion.60 = f32[15,4096]{1,0:T(8,128)S(1)} fusion(f32[12,4096]{1,0:T(8,128)S(1)} %constant_dynamic-slice_fusion.13, f32[120,4096]{1,0:T(8,128)S(1)} %get-tuple-element.406, s32[]{:T(128)S(6)} %select_n.53, f32[48,15,12,15]{3,1,2,0:T(8,128)} %get-tuple-element.404, s32[]{:T(128)S(6)} %select_n.51), kind=kOutput, calls=%fused_computation.1.clone.1 | convolution fusion | flops 134123520 | bytes 868360 | tf_op jit(solution)/shard_map/while/body/dot_general | solution.py:64
  77.6 0.5 fusion.59
  79.5 3.6 %fusion.60 = f32[15,4096]{1,0:T(8,128)S(1)} fusion(f32[12,4096]{1,0:T(8,128)S(1)} %constant_dynamic-slice_fusion.13, f32[120,4096]{1,0:T(8,128)S(1)} %get-tuple-element.406, s32[]{:T(128)S(6)} %select_n.53, f32[48,15,12,15]{3,1,2,0:T(8,128)} %get-tuple-element.404, s32[]{:T(128)S(6)} %select_n.51), kind=kOutput, calls=%fused_computation.1.clone.1 | convolution fusion | flops 134123520 | bytes 868360 | tf_op jit(solution)/shard_map/while/body/dot_general | solution.py:64
  83.9 0.5 fusion.59
  85.8 3.6 %fusion.60 = f32[15,4096]{1,0:T(8,128)S(1)} fusion(f32[12,4096]{1,0:T(8,128)S(1)} %constant_dynamic-slice_fusion.13, f32[120,4096]{1,0:T(8,128)S(1)} %get-tuple-element.406, s32[]{:T(128)S(6)} %select_n.53, f32[48,15,12,15]{3,1,2,0:T(8,128)} %get-tuple-element.404, s32[]{:T(128)S(6)} %select_n.51), kind=kOutput, calls=%fused_computation.1.clone.1 | convolution fusion | flops 134123520 | bytes 868360 | tf_op jit(solution)/shard_map/while/body/dot_general | solution.py:64
  92.1 3.6 %fusion.60 = f32[15,4096]{1,0:T(8,128)S(1)} fusion(f32[12,4096]{1,0:T(8,128)S(1)} %constant_dynamic-slice_fusion.13, f32[120,4096]{1,0:T(8,128)S(1)} %get-tuple-element.406, s32[]{:T(128)S(6)} %select_n.53, f32[48,15,12,15]{3,1,2,0:T(8,128)} %get-tuple-element.404, s32[]{:T(128)S(6)} %select_n.51), kind=kOutput, calls=%fused_computation.1.clone.1 | convolution fusion | flops 134123520 | bytes 868360 | tf_op jit(solution)/shard_map/while/body/dot_general | solution.py:64
  96.8 28.9 %all_gather.10 = f32[120,1,8,128]{3,2,1,0:T(8,128)S(1)} all-gather(f32[15,1,8,128]{3,2,1,0:T(8,128)S(1)} %fusion.33), channel_id=1, replica_groups=mesh['slab'=64,'chaos'=8] {'chaos'}, dimensions={0}, use_global_device_ids=true | all-gather | bytes 552960 | tf_op jit(solution)/shard_map/all_gather | solution.py:75
  125.7 1.9 collective-permute-start.4
  127.6 2.4 collective-permute-start.5
  131.3 4.8 %collective-permute-done.4 = f32[120,1,8,128]{3,2,1,0:T(8,128)S(1)} collective-permute-done((f32[120,1,8,128]{3,2,1,0:T(8,128)S(1)}, f32[120,1,8,128]{3,2,1,0:T(8,128)S(1)}, u32[]{:S(2)}, u32[]{:S(2)}) %collective-permute-start.4) | collective-permute-done | bytes 491552 | tf_op jit(solution)/shard_map/ppermute | solution.py:22
  136.2 8.6 %collective-permute-done.5 = f32[120,1,8,128]{3,2,1,0:T(8,128)S(1)} collective-permute-done((f32[120,1,8,128]{3,2,1,0:T(8,128)S(1)}, f32[120,1,8,128]{3,2,1,0:T(8,128)S(1)}, u32[]{:S(2)}, u32[]{:S(2)}) %collective-permute-start.5) | collective-permute-done | bytes 491552 | tf_op jit(solution)/shard_map/ppermute | solution.py:21
  145.3 38.4 %while.31 = (s32[]{:T(128)}, f32[15,4096]{1,0:T(8,128)S(1)}, s32[]{:T(128)}, f32[48,15,12,15]{3,1,2,0:T(8,128)}, s32[48,3]{0,1:T(4,128)S(1)}, /*index=5*/f32[120...) while((s32[]{:T(128)}, f32[15,4096]{1,0:T(8,128)S(1)}, ...), condition=%wide.region_5.6_spmd, body=%wide.region_3.5_spmd.sunk | while | flops 134184976 | bytes 1999163 | solution.py:87
  147.9 3.6 %fusion.64 = f32[15,4096]{1,0:T(8,128)S(1)} fusion(f32[12,4096]{1,0:T(8,128)S(1)} %constant_dynamic-slice_fusion.15, f32[120,4096]{1,0:T(8,128)S(1)} %get-tuple-element.448, s32[]{:T(128)S(6)} %select_n.56, f32[48,15,12,15]{3,1,2,0:T(8,128)} %get-tuple-element.446, s32[]{:T(128)S(6)} %select_n.54), kind=kOutput, calls=%fused_computation.10.clone.1 | convolution fusion | flops 134123520 | bytes 868360 | tf_op jit(solution)/shard_map/while/body/dot_general | solution.py:64
  154.2 3.6 %fusion.64 = f32[15,4096]{1,0:T(8,128)S(1)} fusion(f32[12,4096]{1,0:T(8,128)S(1)} %constant_dynamic-slice_fusion.15, f32[120,4096]{1,0:T(8,128)S(1)} %get-tuple-element.448, s32[]{:T(128)S(6)} %select_n.56, f32[48,15,12,15]{3,1,2,0:T(8,128)} %get-tuple-element.446, s32[]{:T(128)S(6)} %select_n.54), kind=kOutput, calls=%fused_computation.10.clone.1 | convolution fusion | flops 134123520 | bytes 868360 | tf_op jit(solution)/shard_map/while/body/dot_general | solution.py:64
  160.5 3.6 %fusion.64 = f32[15,4096]{1,0:T(8,128)S(1)} fusion(f32[12,4096]{1,0:T(8,128)S(1)} %constant_dynamic-slice_fusion.15, f32[120,4096]{1,0:T(8,128)S(1)} %get-tuple-element.448, s32[]{:T(128)S(6)} %select_n.56, f32[48,15,12,15]{3,1,2,0:T(8,128)} %get-tuple-element.446, s32[]{:T(128)S(6)} %select_n.54), kind=kOutput, calls=%fused_computation.10.clone.1 | convolution fusion | flops 134123520 | bytes 868360 | tf_op jit(solution)/shard_map/while/body/dot_general | solution.py:64
  166.8 3.6 %fusion.64 = f32[15,4096]{1,0:T(8,128)S(1)} fusion(f32[12,4096]{1,0:T(8,128)S(1)} %constant_dynamic-slice_fusion.15, f32[120,4096]{1,0:T(8,128)S(1)} %get-tuple-element.448, s32[]{:T(128)S(6)} %select_n.56, f32[48,15,12,15]{3,1,2,0:T(8,128)} %get-tuple-element.446, s32[]{:T(128)S(6)} %select_n.54), kind=kOutput, calls=%fused_computation.10.clone.1 | convolution fusion | flops 134123520 | bytes 868360 | tf_op jit(solution)/shard_map/while/body/dot_general | solution.py:64
  173.1 3.6 %fusion.64 = f32[15,4096]{1,0:T(8,128)S(1)} fusion(f32[12,4096]{1,0:T(8,128)S(1)} %constant_dynamic-slice_fusion.15, f32[120,4096]{1,0:T(8,128)S(1)} %get-tuple-element.448, s32[]{:T(128)S(6)} %select_n.56, f32[48,15,12,15]{3,1,2,0:T(8,128)} %get-tuple-element.446, s32[]{:T(128)S(6)} %select_n.54), kind=kOutput, calls=%fused_computation.10.clone.1 | convolution fusion | flops 134123520 | bytes 868360 | tf_op jit(solution)/shard_map/while/body/dot_general | solution.py:64
  179.4 3.6 %fusion.64 = f32[15,4096]{1,0:T(8,128)S(1)} fusion(f32[12,4096]{1,0:T(8,128)S(1)} %constant_dynamic-slice_fusion.15, f32[120,4096]{1,0:T(8,128)S(1)} %get-tuple-element.448, s32[]{:T(128)S(6)} %select_n.56, f32[48,15,12,15]{3,1,2,0:T(8,128)} %get-tuple-element.446, s32[]{:T(128)S(6)} %select_n.54), kind=kOutput, calls=%fused_computation.10.clone.1 | convolution fusion | flops 134123520 | bytes 868360 | tf_op jit(solution)/shard_map/while/body/dot_general | solution.py:64
  184.1 28.9 %all_gather.11 = f32[120,1,8,128]{3,2,1,0:T(8,128)S(1)} all-gather(f32[15,1,8,128]{3,2,1,0:T(8,128)S(1)} %fusion.29), channel_id=1, replica_groups=mesh['slab'=64,'chaos'=8] {'chaos'}, dimensions={0}, use_global_device_ids=true | all-gather | bytes 552960 | tf_op jit(solution)/shard_map/all_gather | solution.py:75
  212.9 1.9 collective-permute-start.6
  214.9 2.6 collective-permute-start.7
  218.2 3.1 %collective-permute-done.6 = f32[120,1,8,128]{3,2,1,0:T(8,128)S(1)} collective-permute-done((f32[120,1,8,128]{3,2,1,0:T(8,128)S(1)}, f32[120,1,8,128]{3,2,1,0:T(8,128)S(1)}, u32[]{:S(2)}, u32[]{:S(2)}) %collective-permute-start.6) | collective-permute-done | bytes 491552 | tf_op jit(solution)/shard_map/ppermute | solution.py:22
  221.2 13.2 %collective-permute-done.7 = f32[120,1,8,128]{3,2,1,0:T(8,128)S(1)} collective-permute-done((f32[120,1,8,128]{3,2,1,0:T(8,128)S(1)}, f32[120,1,8,128]{3,2,1,0:T(8,128)S(1)}, u32[]{:S(2)}, u32[]{:S(2)}) %collective-permute-start.7) | collective-permute-done | bytes 491552 | tf_op jit(solution)/shard_map/ppermute | solution.py:21
  235.0 61.4 %while.32 = (s32[]{:T(128)}, f32[15,4096]{1,0:T(8,128)S(1)}, s32[]{:T(128)}, f32[48,15,12,15]{3,1,2,0:T(8,128)}, s32[48,3]{0,1:T(4,128)S(1)}, /*index=5*/f32[120...) while((s32[]{:T(128)}, f32[15,4096]{1,0:T(8,128)S(1)}, ...), condition=%wide.region_8.9_spmd, body=%wide.region_6.8_spmd.sunk | while | flops 134184976 | bytes 1999163 | solution.py:87
  240.2 3.6 %fusion.68 = f32[15,4096]{1,0:T(8,128)S(1)} fusion(f32[12,4096]{1,0:T(8,128)S(1)} %constant_dynamic-slice_fusion.17, f32[120,4096]{1,0:T(8,128)S(1)} %get-tuple-element.490, s32[]{:T(128)S(6)} %select_n.59, f32[48,15,12,15]{3,1,2,0:T(8,128)} %get-tuple-element.488, s32[]{:T(128)S(6)} %select_n.57), kind=kOutput, calls=%fused_computation.19.clone.1 | convolution fusion | flops 134123520 | bytes 868360 | tf_op jit(solution)/shard_map/while/body/dot_general | solution.py:64
  250.2 3.6 %fusion.68 = f32[15,4096]{1,0:T(8,128)S(1)} fusion(f32[12,4096]{1,0:T(8,128)S(1)} %constant_dynamic-slice_fusion.17, f32[120,4096]{1,0:T(8,128)S(1)} %get-tuple-element.490, s32[]{:T(128)S(6)} %select_n.59, f32[48,15,12,15]{3,1,2,0:T(8,128)} %get-tuple-element.488, s32[]{:T(128)S(6)} %select_n.57), kind=kOutput, calls=%fused_computation.19.clone.1 | convolution fusion | flops 134123520 | bytes 868360 | tf_op jit(solution)/shard_map/while/body/dot_general | solution.py:64
  260.3 3.6 %fusion.68 = f32[15,4096]{1,0:T(8,128)S(1)} fusion(f32[12,4096]{1,0:T(8,128)S(1)} %constant_dynamic-slice_fusion.17, f32[120,4096]{1,0:T(8,128)S(1)} %get-tuple-element.490, s32[]{:T(128)S(6)} %select_n.59, f32[48,15,12,15]{3,1,2,0:T(8,128)} %get-tuple-element.488, s32[]{:T(128)S(6)} %select_n.57), kind=kOutput, calls=%fused_computation.19.clone.1 | convolution fusion | flops 134123520 | bytes 868360 | tf_op jit(solution)/shard_map/while/body/dot_general | solution.py:64
  270.3 3.6 %fusion.68 = f32[15,4096]{1,0:T(8,128)S(1)} fusion(f32[12,4096]{1,0:T(8,128)S(1)} %constant_dynamic-slice_fusion.17, f32[120,4096]{1,0:T(8,128)S(1)} %get-tuple-element.490, s32[]{:T(128)S(6)} %select_n.59, f32[48,15,12,15]{3,1,2,0:T(8,128)} %get-tuple-element.488, s32[]{:T(128)S(6)} %select_n.57), kind=kOutput, calls=%fused_computation.19.clone.1 | convolution fusion | flops 134123520 | bytes 868360 | tf_op jit(solution)/shard_map/while/body/dot_general | solution.py:64
  280.3 3.6 %fusion.68 = f32[15,4096]{1,0:T(8,128)S(1)} fusion(f32[12,4096]{1,0:T(8,128)S(1)} %constant_dynamic-slice_fusion.17, f32[120,4096]{1,0:T(8,128)S(1)} %get-tuple-element.490, s32[]{:T(128)S(6)} %select_n.59, f32[48,15,12,15]{3,1,2,0:T(8,128)} %get-tuple-element.488, s32[]{:T(128)S(6)} %select_n.57), kind=kOutput, calls=%fused_computation.19.clone.1 | convolution fusion | flops 134123520 | bytes 868360 | tf_op jit(solution)/shard_map/while/body/dot_general | solution.py:64
  290.3 3.6 %fusion.68 = f32[15,4096]{1,0:T(8,128)S(1)} fusion(f32[12,4096]{1,0:T(8,128)S(1)} %constant_dynamic-slice_fusion.17, f32[120,4096]{1,0:T(8,128)S(1)} %get-tuple-element.490, s32[]{:T(128)S(6)} %select_n.59, f32[48,15,12,15]{3,1,2,0:T(8,128)} %get-tuple-element.488, s32[]{:T(128)S(6)} %select_n.57), kind=kOutput, calls=%fused_computation.19.clone.1 | convolution fusion | flops 134123520 | bytes 868360 | tf_op jit(solution)/shard_map/while/body/dot_general | solution.py:64
  296.7 0.7 multiply_add_fusion
  (158 shorter events, 15.2 us)
Async XLA Ops:
  0.6 43.6 %copy-start = (f32[36,1,8,128]{3,2,1,0:T(8,128)S(1)}, f32[36,1,8,128]{3,2,1,0:T(8,128)}, u32[]{:S(2)}) copy-start(f32[36,1,8,128]{3,2,1,0:T(8,128)} %param.14) | copy-start | bytes 442372
  29.8 26.0 %collective-permute-start = (f32[120,1,8,128]{3,2,1,0:T(8,128)S(1)}, f32[120,1,8,128]{3,2,1,0:T(8,128)S(1)}, u32[]{:S(2)}, u32[]{:S(2)}) collective-permute-start(f32[120,1,8,128]{3,2,1,0:T(8,128)S(1)} %all_gather.9), channel_id=1, source_target_pairs={{8,0},{16,8},{24,16},{32,24},{40,32},{48,40},{56,48},{64,56},{72,6... | collective-permute-start | bytes 1474568 | tf_op jit(solution)/shard_map/ppermute | solution.py:22
  31.7 24.1 %collective-permute-start.1 = (f32[120,1,8,128]{3,2,1,0:T(8,128)S(1)}, f32[120,1,8,128]{3,2,1,0:T(8,128)}, u32[]{:S(2)}, u32[]{:S(2)}) collective-permute-start(f32[120,1,8,128]{3,2,1,0:T(8,128)S(1)} %all_gather.9), channel_id=1, source_target_pairs={{0,8},{8,16},{16,24},{24,32},{32,40},{40,48},{48,56},{56,64},{64,7... | collective-permute-start | bytes 1474568 | tf_op jit(solution)/shard_map/ppermute | solution.py:21
  34.1 20.5 %collective-permute-start.2 = (f32[36,1,8,128]{3,2,1,0:T(8,128)}, f32[36,1,8,128]{3,2,1,0:T(8,128)}, u32[]{:S(2)}, u32[]{:S(2)}) collective-permute-start(f32[36,1,8,128]{3,2,1,0:T(8,128)} %param.14), channel_id=1, source_target_pairs={{0,8},{8,16},{16,24},{24,32},{32,40},{40,48},{48,56},{56,64},{64,7... | collective-permute-start | bytes 442376 | tf_op jit(solution)/shard_map/ppermute | solution.py:21
  38.2 16.3 %collective-permute-start.3 = (f32[36,1,8,128]{3,2,1,0:T(8,128)}, f32[36,1,8,128]{3,2,1,0:T(8,128)}, u32[]{:S(2)}, u32[]{:S(2)}) collective-permute-start(f32[36,1,8,128]{3,2,1,0:T(8,128)} %param.14), channel_id=1, source_target_pairs={{8,0},{16,8},{24,16},{32,24},{40,32},{48,40},{56,48},{64,56},{72,6... | collective-permute-start | bytes 442376 | tf_op jit(solution)/shard_map/ppermute | solution.py:22
  44.5 1.4 copy-start.7
  44.7 2.5 copy-start.3
  55.7 1.6 copy-start.1
  55.8 1.6 copy-start.2
  57.3 0.7 copy-start.5
  58.0 38.7 %copy-start.4 = (f32[15,1,8,128]{3,2,1,0:T(8,128)S(1)}, f32[15,1,8,128]{3,2,1,0:T(8,128)}, u32[]{:S(2)}) copy-start(f32[15,1,8,128]{3,2,1,0:T(8,128)} %param.12) | copy-start | bytes 184324
  58.0 38.7 %copy-start.6 = (f32[15,1,8,128]{3,2,1,0:T(8,128)S(1)}, f32[15,1,8,128]{3,2,1,0:T(8,128)}, u32[]{:S(2)}) copy-start(f32[15,1,8,128]{3,2,1,0:T(8,128)} %param.13) | copy-start | bytes 184324
  125.7 10.5 %collective-permute-start.4 = (f32[120,1,8,128]{3,2,1,0:T(8,128)S(1)}, f32[120,1,8,128]{3,2,1,0:T(8,128)S(1)}, u32[]{:S(2)}, u32[]{:S(2)}) collective-permute-start(f32[120,1,8,128]{3,2,1,0:T(8,128)S(1)} %all_gather.10), channel_id=1, source_target_pairs={{8,0},{16,8},{24,16},{32,24},{40,32},{48,40},{56,48},{64,56},{72,6... | collective-permute-start | bytes 1474568 | tf_op jit(solution)/shard_map/ppermute | solution.py:22
  127.6 17.2 %collective-permute-start.5 = (f32[120,1,8,128]{3,2,1,0:T(8,128)S(1)}, f32[120,1,8,128]{3,2,1,0:T(8,128)S(1)}, u32[]{:S(2)}, u32[]{:S(2)}) collective-permute-start(f32[120,1,8,128]{3,2,1,0:T(8,128)S(1)} %all_gather.10), channel_id=1, source_target_pairs={{0,8},{8,16},{16,24},{24,32},{32,40},{40,48},{48,56},{56,64},{64,7... | collective-permute-start | bytes 1474568 | tf_op jit(solution)/shard_map/ppermute | solution.py:21
  212.9 8.3 %collective-permute-start.6 = (f32[120,1,8,128]{3,2,1,0:T(8,128)S(1)}, f32[120,1,8,128]{3,2,1,0:T(8,128)S(1)}, u32[]{:S(2)}, u32[]{:S(2)}) collective-permute-start(f32[120,1,8,128]{3,2,1,0:T(8,128)S(1)} %all_gather.11), channel_id=1, source_target_pairs={{8,0},{16,8},{24,16},{32,24},{40,32},{48,40},{56,48},{64,56},{72,6... | collective-permute-start | bytes 1474568 | tf_op jit(solution)/shard_map/ppermute | solution.py:22
  214.9 19.6 %collective-permute-start.7 = (f32[120,1,8,128]{3,2,1,0:T(8,128)S(1)}, f32[120,1,8,128]{3,2,1,0:T(8,128)S(1)}, u32[]{:S(2)}, u32[]{:S(2)}) collective-permute-start(f32[120,1,8,128]{3,2,1,0:T(8,128)S(1)} %all_gather.11), channel_id=1, source_target_pairs={{0,8},{8,16},{16,24},{24,32},{32,40},{40,48},{48,56},{56,64},{64,7... | collective-permute-start | bytes 1474568 | tf_op jit(solution)/shard_map/ppermute | solution.py:21
where the time goes:
time: 299 us; the launch traced here: 297 us
  blocking collectives  86.8 us (29%)
  matrix products  65 us (22%)
  loops' own time  60.5 us (20%)
  waiting for transfers between devices  31.9 us (11%)
  starting transfers between devices  22.9 us (8%)
  local copies, waits for them, and re-layouts  22.3 us (7%)
  other arithmetic  5.47 us (2%)
    all_gather x3, blocking collectives, gathered_image(): whole = lax.all_gather(field, 'chaos', axis=0, tiled=True)  86.8 us
    dot_general x18, matrix products, coupling(): jnp.dot(table.reshape(-1, table.shape[-1]), grads_block, precision=lax.Pr...  65 us
    another operation x3, loops' own time, gathered_image(): lax.fori_loop(offsets[block_out], offsets[block_out + 1], add_triple, sta...  60.5 us
    ppermute x4, waiting for transfers between devices, extended(): before = lax.ppermute(last, axis, up)  24 us
    ppermute x4, starting transfers between devices, extended(): before = lax.ppermute(last, axis, up)  11.5 us
    ppermute x4, starting transfers between devices, extended(): after = lax.ppermute(initial, axis, down)  11.4 us
    slice x18, local copies, waits for them, and re-layouts, add_triple(): triple[1] * MODE_BLK  9.81 us
    ppermute x4, waiting for transfers between devices, extended(): after = lax.ppermute(initial, axis, down)  7.89 us
  transfers between devices with their start and end apart: 8, of which 5 were waited for; matrix products, arithmetic and copies ran while one was open for 3% of the time, Pallas kernels for 0%

commit v1 on v0

v1 whole, which is shorter than its diff:
```python
import functools

import jax
import jax.numpy as jnp
from jax import lax
from jax.experimental import pallas as pl
from jax.experimental.pallas import tpu as pltpu
from jax.sharding import PartitionSpec as P

MB = 15
MP = 16
NB = 8
CB = 12
NK = 36
KC = 3
NTRIP = 36
ROWS = NB * MP
NX = 128
CP = 40
RELAX = 0.1
f32 = jnp.float32
bf16 = jnp.bfloat16

VM = pl.BlockSpec(memory_space=pltpu.VMEM)
SM = pl.BlockSpec(memory_space=pltpu.SMEM)
PARAMS = pltpu.CompilerParams(vmem_limit_bytes=44 * 2**20)


def call(kernel, outs, ins, scratch=(), specs=None, name=None):
    return pl.pallas_call(
        kernel,
        out_shape=outs,
        in_specs=specs or [VM] * len(ins),
        out_specs=jax.tree.map(lambda _: VM, outs),
        scratch_shapes=scratch,
        compiler_params=PARAMS,
        name=name,
    )(*ins)


def struct(*shape, dtype=f32):
    return jax.ShapeDtypeStruct(shape, dtype)


def table_kernel(trip, values, table, dense, piece):
    dense[...] = jnp.zeros_like(dense)
    piece[...] = jnp.zeros_like(piece)

    def place(t, carry):
        piece[:, :CB, :MB] = values[t]
        block = piece[...].reshape(MB * MP, ROWS)
        block = pltpu.roll(block, trip[t, 1] * MP, 1)
        base = pl.multiple_of((trip[t, 2] * NB + trip[t, 0]) * (MP * MP), MP * MP)
        dense[pl.ds(base, MB * MP), :] += block
        return carry

    lax.fori_loop(0, NTRIP, place, 0)

    for c in range(KC):
        for b in range(NB):
            for k in range(CB):
                x = dense[pl.ds((c * NB + b) * MP * MP + k, MP, stride=MP), :]
                high = x.astype(bf16)
                low = (x - high.astype(f32)).astype(bf16)
                at = pl.ds((c * CB + k) * ROWS + b * MP, MP)
                table[at, 0:128] = high
                table[at, 128:256] = high
                table[at, 256:384] = low


def pack_kernel(guess, rhs, send):
    zero = jnp.zeros((1, NX), f32)
    for y in range(NB):
        g = jnp.concatenate([guess[pl.ds(y, MB, stride=NB), :], zero], axis=0)
        r = jnp.concatenate([rhs[pl.ds(y, MB, stride=NB), :], zero], axis=0)
        for p in range(5):
            send[(y + 2 - p) % NB, p] = g
        for p in range(3):
            send[(y + 1 - p) % NB, 5 + p] = r


def side_kernel(me, got, coef, side, own):
    y = me[0]
    zero = jnp.zeros((CP - NK, NX), f32)
    for q in range(5):
        row = lax.rem(y + q + NB - 2, NB)
        c = jnp.concatenate([coef[pl.ds(row, NK, stride=NB), :], zero], axis=0)
        own[q] = c
        if 1 <= q <= 3:
            side[q - 1, ROWS:, :] = c
            for b in range(NB):
                side[q - 1, b * MP : (b + 1) * MP, :] = got[b, q]


def column(g):
    high = g.astype(bf16)
    low = (g - high.astype(f32)).astype(bf16)
    return jnp.concatenate([high, low, high], axis=0)


def tile_flux(table, grad, weight, extra=None):
    width = grad.shape[1]

    def chunk(c, sums):
        w = jnp.dot(
            table[pl.ds(pl.multiple_of(c * CB * ROWS, CB * ROWS), CB * ROWS), :],
            grad[...],
            preferred_element_type=f32,
        )
        main, more = sums
        for k in range(CB):
            part = w[k * ROWS : (k + 1) * ROWS, :]
            main = main + weight[c, k : k + 1, :] * part
            if extra is not None:
                more = more + extra[c, k : k + 1, :] * part[:, NX:]
        return main, more

    zero = jnp.zeros((ROWS, width), f32)
    none = jnp.zeros((ROWS, NX), f32) if extra is not None else 0
    main, more = lax.fori_loop(0, KC, chunk, (zero, none))
    return main if extra is None else (main, more)


def put_weight(ref, tile, half, a):
    for c in range(KC):
        ref[tile, c, :CB, half * NX : (half + 1) * NX] = a[c * CB : (c + 1) * CB]


def to_right(x):
    return pltpu.roll(x, 1, 1)


def from_right(x):
    return pltpu.roll(x, NX - 1, 1)


def fluxes(table, grad, weight, flux, faces):
    for n, (g, a) in enumerate(faces):
        grad[n // 2, :, (n % 2) * NX : (n % 2 + 1) * NX] = column(g)
        put_weight(weight, n // 2, n % 2, a)
    if len(faces) % 2:
        grad[len(faces) // 2, :, NX:] = jnp.zeros((3 * ROWS, NX), bf16)
        weight[len(faces) // 2, :, :, NX:] = jnp.zeros((KC, MP, NX), f32)

    def tile(n, carry):
        flux[n] = tile_flux(table, grad.at[n], weight.at[n])
        return carry

    lax.fori_loop(0, (len(faces) + 1) // 2, tile, 0)
    return [flux[n // 2, :, (n % 2) * NX : (n % 2 + 1) * NX] for n in range(len(faces))]


def half_sum(a, b):
    return 0.5 * (a + b)


def first_kernel(got, below, above, own, table, three, one, right, grad, weight, flux):
    v = [jnp.concatenate([got[b, p] for b in range(NB)], axis=0) for p in range(5)]
    faces = []
    for r in (1, 2, 3):
        faces.append((from_right(v[r]) - v[r], half_sum(own[r], from_right(own[r]))))
        faces.append((v[r] - below[r - 1, :ROWS], half_sum(below[r - 1, ROWS:], own[r])))
        faces.append((above[r - 1, :ROWS] - v[r], half_sum(own[r], above[r - 1, ROWS:])))
    for r in range(4):
        faces.append((v[r + 1] - v[r], half_sum(own[r], own[r + 1])))
    out = fluxes(table, grad, weight, flux, faces)
    for r in (1, 2, 3):
        fx, low, high = out[3 * (r - 1) : 3 * r]
        image = (to_right(fx) - fx) + (out[9 + r - 1] - out[9 + r]) + (low - high)
        rhs = jnp.concatenate([got[b, 4 + r] for b in range(NB)], axis=0)
        new = v[r] + RELAX * (rhs - image)
        three[r - 1] = new
        if r == 2:
            one[...] = new
            right[...] = rhs


def second_kernel(three, low_v, high_v, below, above, own, right, table, one, grad, weight, flux):
    v = three[1]
    c = own[2]
    faces = [
        (from_right(v) - v, half_sum(c, from_right(c))),
        (v - low_v[...], half_sum(below[1, ROWS:], c)),
        (high_v[...] - v, half_sum(c, above[1, ROWS:])),
        (v - three[0], half_sum(own[1], c)),
        (three[2] - v, half_sum(c, own[3])),
    ]
    fx, zl, zh, yl, yh = fluxes(table, grad, weight, flux, faces)
    image = (to_right(fx) - fx) + (yl - yh) + (zl - zh)
    one[...] = v + RELAX * (right[...] - image)


def third_kernel(mid, low_v, high_v, below, above, own, right, table, send, grad, weight):
    v = mid[...]
    c = own[2]
    columns = [
        (from_right(v) - v, half_sum(c, from_right(c))),
        (v - low_v[...], half_sum(below[1, ROWS:], c)),
        (high_v[...] - v, half_sum(c, above[1, ROWS:])),
        (v, half_sum(c, own[3])),
    ]
    for n, (g, a) in enumerate(columns):
        grad[n // 2, :, (n % 2) * NX : (n % 2 + 1) * NX] = column(g)
        put_weight(weight, n // 2, n % 2, a)
    put_weight(weight, 2, 0, half_sum(own[1], c))
    one = tile_flux(table, grad.at[0], weight.at[0])
    two, y_low = tile_flux(table, grad.at[1], weight.at[1], weight.at[2, :, :, :NX])
    fx, zl = one[:, :NX], one[:, NX:]
    zh, y_high = two[:, :NX], two[:, NX:]
    rest = right[...] - (to_right(fx) - fx) - (zl - zh) - (y_low + y_high)
    for b in range(NB):
        rows = slice(b * MP, (b + 1) * MP)
        send[b, 0] = v[rows]
        send[b, 1] = rest[rows]
        send[b, 2] = y_high[rows]
        send[b, 3] = y_low[rows]


def last_kernel(got, out, residual):
    for y in range(NB):
        res = got[y, 1] + got[(y - 1) % NB, 2] + got[(y + 1) % NB, 3]
        new = got[y, 0] + RELAX * res
        residual[pl.ds(y, MB, stride=NB), :] = res[:MB]
        out[pl.ds(y, MB, stride=NB), :] = new[:MB]


def body(rhs, guess, coef, block_triples, offsets, values):
    slabs = lax.axis_size("slab")
    up = [(i, i + 1) for i in range(slabs - 1)]
    down = [(j, i) for i, j in up]

    def beside(x):
        return lax.ppermute(x, "slab", up), lax.ppermute(x, "slab", down)

    def scratch(tiles, weights):
        return [
            pltpu.VMEM((tiles, 3 * ROWS, 2 * NX), bf16),
            pltpu.VMEM((weights, KC, MP, 2 * NX), f32),
        ]

    me = lax.axis_index("chaos").astype(jnp.int32).reshape(1)
    send = call(
        pack_kernel,
        struct(NB, 8, MP, NX),
        (guess.reshape(MB * NB, NX), rhs.reshape(MB * NB, NX)),
        name="pack",
    )
    got = lax.all_to_all(send, "chaos", 0, 0, tiled=True)
    side, own = call(
        side_kernel,
        (struct(3, ROWS + CP, NX), struct(5, CP, NX)),
        (me, got, coef.reshape(NK * NB, NX)),
        specs=[SM, VM, VM],
        name="side",
    )
    below, above = beside(side)
    table = call(
        table_kernel,
        struct(NK * ROWS, 3 * ROWS, dtype=bf16),
        (block_triples, values),
        scratch=[pltpu.VMEM((KC * NB * MP * MP, ROWS), f32), pltpu.VMEM((MB, MP, ROWS), f32)],
        specs=[SM, VM],
        name="table",
    )
    flat = struct(ROWS, NX)
    three, one, right = call(
        first_kernel,
        (struct(3, ROWS, NX), flat, flat),
        (got, below, above, own, table),
        scratch=scratch(7, 7) + [pltpu.VMEM((7, ROWS, 2 * NX), f32)],
        name="first",
    )
    low_v, high_v = beside(one)
    mid = call(
        second_kernel,
        flat,
        (three, low_v, high_v, below, above, own, right, table),
        scratch=scratch(3, 3) + [pltpu.VMEM((3, ROWS, 2 * NX), f32)],
        name="second",
    )
    low_v, high_v = beside(mid)
    send = call(
        third_kernel,
        struct(NB, 4, MP, NX),
        (mid, low_v, high_v, below, above, own, right, table),
        scratch=scratch(2, 3),
        name="third",
    )
    got = lax.all_to_all(send, "chaos", 0, 0, tiled=True)
    out, residual = call(
        last_kernel, (struct(MB * NB, NX), struct(MB * NB, NX)), (got,), name="last"
    )
    return out.reshape(rhs.shape), residual.reshape(rhs.shape)


def solution(mesh):
    field = P("chaos", "slab", None, None)
    placed = (field, field, P(None, "slab", None, None), P(), P(), P())
    return jax.shard_map(
        body, mesh=mesh, in_specs=placed, out_specs=(field, field), check_vma=False
    )
```

time: 299 us -> 102 us (0.34)
  the two profiles are of different devices: /device:TPU:270 before, /device:TPU:256 now
where the time goes in v1:
time: 102 us; the launch traced here: 101 us
  Pallas kernels  28.7 us (28%)
  waiting for transfers between devices  24.9 us (24%)
  starting transfers between devices  23.3 us (23%)
  blocking collectives  12.2 us (12%)
  local copies, waits for them, and re-layouts  11.2 us (11%)
    pallas_call x7, Pallas kernels, call(): pl.pallas_call(kernel, out_shape=outs, in_specs=specs or [VM] * len(ins),...  28.7 us
    ppermute x6, starting transfers between devices, beside(): return (lax.ppermute(x, 'slab', up), lax.ppermute(x, 'slab', down))  17.9 us
    ppermute x6, waiting for transfers between devices, beside(): return (lax.ppermute(x, 'slab', up), lax.ppermute(x, 'slab', down))  15.4 us
    all_to_all x1, blocking collectives, body(): got = lax.all_to_all(send, 'chaos', 0, 0, tiled=True)  12.2 us
    unnamed x10, local copies, waits for them, and re-layouts  11.2 us
    all_to_all x1, waiting for transfers between devices, body(): got = lax.all_to_all(send, 'chaos', 0, 0, tiled=True)  9.58 us
    all_to_all x1, starting transfers between devices, body(): got = lax.all_to_all(send, 'chaos', 0, 0, tiled=True)  5.31 us
  transfers between devices with their start and end apart: 7, of which 3 were waited for; matrix products, arithmetic and copies ran while one was open for 6% of the time, Pallas kernels for 6%

profile of v1, /device:TPU:256, one launch (start us, length us, event | category | flops | bytes accessed | tf_op | source)
XLA Modules:
  0.0 101.1 jit_solution(6874246481617166720)
XLA Ops:
  0.6 0.0 copy-start.2
  0.6 0.8 copy-done.2
  1.5 0.0 copy-start.3
  1.5 0.8 copy-done.3
  2.3 0.8 pack.1
  3.1 5.3 %all-to-all-start = ((f32[8,8,16,128]{3,2,1,0:T(8,128)}), f32[8,8,16,128]{3,2,1,0:T(8,128)S(1)}, u32[]{:S(2)}, u32[]{:S(2)}) async-start(f32[8,8,16,128]{3,2,1,0:T(8,128)} %pack.1), calls=%async_computation | async-start | bytes 1048576 | tf_op jit(solution)/shard_map/all_to_all | solution.py:248
  8.4 9.6 %all-to-all-done.got = f32[8,8,16,128]{3,2,1,0:T(8,128)S(1)} async-done(((f32[8,8,16,128]{3,2,1,0:T(8,128)}), f32[8,8,16,128]{3,2,1,0:T(8,128)S(1)}, u32[]{:S(2)}, u32[]{:S(2)}) %all-to-all-start) | async-done | bytes 524320 | tf_op jit(solution)/shard_map/all_to_all | solution.py:248
  18.0 0.0 copy-start.1
  18.0 0.9 copy-done.1
  19.0 1.9 %collective-permute-start.1 = (f32[3,168,128]{2,1,0:T(8,128)S(1)}, f32[3,168,128]{2,1,0:T(8,128)S(1)}, u32[]{:S(2)}, u32[]{:S(2)}) collective-permute-start(f32[3,168,128]{2,1,0:T(8,128)S(1)} %get-tuple-element.9), channel_id=1, source_target_pairs={{8,0},{16,8},{24,16},{32,24},{40,32},{48,40},{56,48},{64,56},{72,6... | collective-permute-start | bytes 774152 | tf_op jit(solution)/shard_map/ppermute | solution.py:233
  20.9 2.4 %collective-permute-start = (f32[3,168,128]{2,1,0:T(8,128)S(1)}, f32[3,168,128]{2,1,0:T(8,128)S(1)}, u32[]{:S(2)}, u32[]{:S(2)}) collective-permute-start(f32[3,168,128]{2,1,0:T(8,128)S(1)} %get-tuple-element.9), channel_id=1, source_target_pairs={{0,8},{8,16},{16,24},{24,32},{32,40},{40,48},{48,56},{56,64},{64,7... | collective-permute-start | bytes 774152 | tf_op jit(solution)/shard_map/ppermute | solution.py:233
  23.3 0.8 copy.7.trip
  24.1 5.2 %copy.8.values = f32[48,15,12,15]{3,2,1,0:T(8,128)} copy(f32[48,15,12,15]{0,3,2,1:T(8,128)} %param.10) | data formatting | bytes 1036800 | tf_op args[5]
  29.3 0.0 copy-start
  29.3 2.7 %copy-done = f32[48,15,12,15]{3,2,1,0:T(8,128)S(1)} copy-done((f32[48,15,12,15]{3,2,1,0:T(8,128)S(1)}, f32[48,15,12,15]{3,2,1,0:T(8,128)}, u32[]{:S(2)}) %copy-start) | copy-done | bytes 518424
  32.0 5.9 %table.1 = bf16[4608,384]{1,0:T(8,128)(2,1)S(1)} custom-call(s32[48,3]{1,0:T(8,128)S(1)} %copy.7.trip, f32[48,15,12,15]{3,2,1,0:T(8,128)S(1)} %copy-done), custom_call_target="tpu_custom_call" | custom-call | tf_op jit(solution)/shard_map/table/pallas_call | solution.py:30
  37.9 0.0 collective-permute-done.1.above
  37.9 0.0 collective-permute-done.below
  37.9 12.4 %first.1 = (f32[3,128,128]{2,1,0:T(8,128)S(1)}, f32[128,128]{1,0:T(8,128)S(1)}, f32[128,128]{1,0:T(8,128)S(1)}) custom-call(f32[8,8,16,128]{3,2,1,0:T(8,128)S(1)} %all-to-all-done.got, f32[3,168,128]{2,1,0:T(8,128)S(1)} %collective-permute-done.below, f32[3,168,128]{2,1,0:T(8,128)S(1)} %collective-permute-done.1.above, ...), custom_call_target="tpu_custom_call" | custom-call | tf_op jit(solution)/shard_map/first/pallas_call | solution.py:30
  50.2 7.4 %collective-permute-start.3 = (f32[128,128]{1,0:T(8,128)S(1)}, f32[128,128]{1,0:T(8,128)S(1)}, u32[]{:S(2)}, u32[]{:S(2)}) collective-permute-start(f32[128,128]{1,0:T(8,128)S(1)} %get-tuple-element.12), channel_id=1, source_target_pairs={{8,0},{16,8},{24,16},{32,24},{40,32},{48,40},{56,48},{64,56},{72,6... | collective-permute-start | bytes 196616 | tf_op jit(solution)/shard_map/ppermute | solution.py:233
  57.6 1.9 %collective-permute-start.2 = (f32[128,128]{1,0:T(8,128)S(1)}, f32[128,128]{1,0:T(8,128)S(1)}, u32[]{:S(2)}, u32[]{:S(2)}) collective-permute-start(f32[128,128]{1,0:T(8,128)S(1)} %get-tuple-element.12), channel_id=1, source_target_pairs={{0,8},{8,16},{16,24},{24,32},{32,40},{40,48},{48,56},{56,64},{64,7... | collective-permute-start | bytes 196616 | tf_op jit(solution)/shard_map/ppermute | solution.py:233
  59.6 0.0 collective-permute-done.3.high_v
  59.6 8.0 %collective-permute-done.2.low_v = f32[128,128]{1,0:T(8,128)S(1)} collective-permute-done((f32[128,128]{1,0:T(8,128)S(1)}, f32[128,128]{1,0:T(8,128)S(1)}, u32[]{:S(2)}, u32[]{:S(2)}) %collective-permute-start.2) | collective-permute-done | bytes 65568 | tf_op jit(solution)/shard_map/ppermute | solution.py:233
  67.5 5.3 %second.1.mid = f32[128,128]{1,0:T(8,128)S(1)} custom-call(f32[3,128,128]{2,1,0:T(8,128)S(1)} %get-tuple-element.11.three, f32[128,128]{1,0:T(8,128)S(1)} %collective-permute-done.2.low_v, f32[128,128]{1,0:T(8,128)S(1)} %collective-permute-done.3.high_v, f32[3,168,128]{2,1,0:T(8,128)S(1)} %collective-permute-done.below, ...), custom_call_target="tpu_custom_call" | custom-call | tf_op jit(solution)/shard_map/second/pallas_call | solution.py:30
  72.9 1.9 %collective-permute-start.5 = (f32[128,128]{1,0:T(8,128)S(1)}, f32[128,128]{1,0:T(8,128)S(1)}, u32[]{:S(2)}, u32[]{:S(2)}) collective-permute-start(f32[128,128]{1,0:T(8,128)S(1)} %second.1.mid), channel_id=1, source_target_pairs={{8,0},{16,8},{24,16},{32,24},{40,32},{48,40},{56,48},{64,56},{72,6... | collective-permute-start | bytes 196616 | tf_op jit(solution)/shard_map/ppermute | solution.py:233
  74.8 2.4 %collective-permute-start.4 = (f32[128,128]{1,0:T(8,128)S(1)}, f32[128,128]{1,0:T(8,128)S(1)}, u32[]{:S(2)}, u32[]{:S(2)}) collective-permute-start(f32[128,128]{1,0:T(8,128)S(1)} %second.1.mid), channel_id=1, source_target_pairs={{0,8},{8,16},{16,24},{24,32},{32,40},{40,48},{48,56},{56,64},{64,7... | collective-permute-start | bytes 196616 | tf_op jit(solution)/shard_map/ppermute | solution.py:233
  77.2 0.0 collective-permute-done.5.high_v
  77.2 7.4 %collective-permute-done.4.low_v = f32[128,128]{1,0:T(8,128)S(1)} collective-permute-done((f32[128,128]{1,0:T(8,128)S(1)}, f32[128,128]{1,0:T(8,128)S(1)}, u32[]{:S(2)}, u32[]{:S(2)}) %collective-permute-start.4) | collective-permute-done | bytes 65568 | tf_op jit(solution)/shard_map/ppermute | solution.py:233
  84.6 3.6 %third.1 = f32[8,4,16,128]{3,2,1,0:T(8,128)S(1)} custom-call(f32[128,128]{1,0:T(8,128)S(1)} %second.1.mid, f32[128,128]{1,0:T(8,128)S(1)} %collective-permute-done.4.low_v, f32[128,128]{1,0:T(8,128)S(1)} %collective-permute-done.5.high_v, f32[3,168,128]{2,1,0:T(8,128)S(1)} %collective-permute-done.below, f32[3,168,128]{2,1,0:T(8,128)S(1)} %collective-permute-done.1.above, ...), custom_call_target="tpu_custom_call" | custom-call | tf_op jit(solution)/shard_map/third/pallas_call | solution.py:30
  88.3 12.2 %all_to_all.10.got = f32[8,4,16,128]{3,2,1,0:T(8,128)S(1)} all-to-all(f32[8,4,16,128]{3,2,1,0:T(8,128)S(1)} %third.1), channel_id=1, replica_groups=mesh['slab'=64,'chaos'=8] {'chaos'}, dimensions={0} | all-to-all | bytes 524288 | tf_op jit(solution)/shard_map/all_to_all | solution.py:289
  100.5 0.7 last.1
  (1 shorter events, 0.0 us)
Async XLA Ops:
  0.6 0.8 copy-start.2
  1.5 0.8 copy-start.3
  3.1 14.9 %all-to-all-start = ((f32[8,8,16,128]{3,2,1,0:T(8,128)}), f32[8,8,16,128]{3,2,1,0:T(8,128)S(1)}, u32[]{:S(2)}, u32[]{:S(2)}) async-start(f32[8,8,16,128]{3,2,1,0:T(8,128)} %pack.1), calls=%async_computation | async-start | bytes 1048576 | tf_op jit(solution)/shard_map/all_to_all | solution.py:248
  18.0 0.9 copy-start.1
  19.0 18.9 %collective-permute-start.1 = (f32[3,168,128]{2,1,0:T(8,128)S(1)}, f32[3,168,128]{2,1,0:T(8,128)S(1)}, u32[]{:S(2)}, u32[]{:S(2)}) collective-permute-start(f32[3,168,128]{2,1,0:T(8,128)S(1)} %get-tuple-element.9), channel_id=1, source_target_pairs={{8,0},{16,8},{24,16},{32,24},{40,32},{48,40},{56,48},{64,56},{72,6... | collective-permute-start | bytes 774152 | tf_op jit(solution)/shard_map/ppermute | solution.py:233
  20.9 17.0 %collective-permute-start = (f32[3,168,128]{2,1,0:T(8,128)S(1)}, f32[3,168,128]{2,1,0:T(8,128)S(1)}, u32[]{:S(2)}, u32[]{:S(2)}) collective-permute-start(f32[3,168,128]{2,1,0:T(8,128)S(1)} %get-tuple-element.9), channel_id=1, source_target_pairs={{0,8},{8,16},{16,24},{24,32},{32,40},{40,48},{48,56},{56,64},{64,7... | collective-permute-start | bytes 774152 | tf_op jit(solution)/shard_map/ppermute | solution.py:233
  29.3 2.7 %copy-start = (f32[48,15,12,15]{3,2,1,0:T(8,128)S(1)}, f32[48,15,12,15]{3,2,1,0:T(8,128)}, u32[]{:S(2)}) copy-start(f32[48,15,12,15]{3,2,1,0:T(8,128)} %copy.8.values) | copy-start | bytes 1555204
  50.2 9.3 %collective-permute-start.3 = (f32[128,128]{1,0:T(8,128)S(1)}, f32[128,128]{1,0:T(8,128)S(1)}, u32[]{:S(2)}, u32[]{:S(2)}) collective-permute-start(f32[128,128]{1,0:T(8,128)S(1)} %get-tuple-element.12), channel_id=1, source_target_pairs={{8,0},{16,8},{24,16},{32,24},{40,32},{48,40},{56,48},{64,56},{72,6... | collective-permute-start | bytes 196616 | tf_op jit(solution)/shard_map/ppermute | solution.py:233
  57.6 9.9 %collective-permute-start.2 = (f32[128,128]{1,0:T(8,128)S(1)}, f32[128,128]{1,0:T(8,128)S(1)}, u32[]{:S(2)}, u32[]{:S(2)}) collective-permute-start(f32[128,128]{1,0:T(8,128)S(1)} %get-tuple-element.12), channel_id=1, source_target_pairs={{0,8},{8,16},{16,24},{24,32},{32,40},{40,48},{48,56},{56,64},{64,7... | collective-permute-start | bytes 196616 | tf_op jit(solution)/shard_map/ppermute | solution.py:233
  72.9 4.3 %collective-permute-start.5 = (f32[128,128]{1,0:T(8,128)S(1)}, f32[128,128]{1,0:T(8,128)S(1)}, u32[]{:S(2)}, u32[]{:S(2)}) collective-permute-start(f32[128,128]{1,0:T(8,128)S(1)} %second.1.mid), channel_id=1, source_target_pairs={{8,0},{16,8},{24,16},{32,24},{40,32},{48,40},{56,48},{64,56},{72,6... | collective-permute-start | bytes 196616 | tf_op jit(solution)/shard_map/ppermute | solution.py:233
  74.8 9.8 %collective-permute-start.4 = (f32[128,128]{1,0:T(8,128)S(1)}, f32[128,128]{1,0:T(8,128)S(1)}, u32[]{:S(2)}, u32[]{:S(2)}) collective-permute-start(f32[128,128]{1,0:T(8,128)S(1)} %second.1.mid), channel_id=1, source_target_pairs={{0,8},{8,16},{16,24},{24,32},{32,40},{40,48},{48,56},{56,64},{64,7... | collective-permute-start | bytes 196616 | tf_op jit(solution)/shard_map/ppermute | solution.py:233

commit v2 on v1

v2 whole, which is shorter than its diff:
```python
import jax
import jax.numpy as jnp
from jax import lax
from jax.experimental import pallas as pl
from jax.experimental.pallas import tpu as pltpu
from jax.sharding import PartitionSpec as P

MB = 15
MP = 16
NB = 8
CB = 12
KC = 3
NK = 36
NTRIP = 36
ROWS = NB * MP
PART = 4
CHUNK = ROWS // PART
NX = 128
CP = 40
RELAX = 0.1
f32 = jnp.float32
bf16 = jnp.bfloat16

VM = pl.BlockSpec(memory_space=pltpu.VMEM)
SM = pl.BlockSpec(memory_space=pltpu.SMEM)
HBM = pl.BlockSpec(memory_space=pltpu.HBM)
LIMIT = 20 * 2**20
FULL = 60 * 2**20


def call(kernel, name, outs, ins, scratch=(), specs=None, cost=None, limit=LIMIT):
    estimate = None
    if cost is not None:
        estimate = pl.CostEstimate(flops=cost, bytes_accessed=4 * 2**20, transcendentals=0)
    return pl.pallas_call(
        kernel,
        out_shape=outs,
        in_specs=specs or [VM] * len(ins),
        out_specs=jax.tree.map(lambda _: VM, outs),
        scratch_shapes=scratch,
        compiler_params=pltpu.CompilerParams(vmem_limit_bytes=limit),
        cost_estimate=estimate,
        name=name,
    )(*ins)


def struct(*shape, dtype=f32):
    return jax.ShapeDtypeStruct(shape, dtype)


def table_kernel(trip, values, table, dense, piece, turned):
    dense[...] = jnp.zeros_like(dense)
    piece[...] = jnp.zeros_like(piece)
    for half in range(2):
        count = min(8, MB - 8 * half)
        for k in range(CB):
            piece[half, :count, :MB, :] = values[8 * half : 8 * half + count, k]
            block = piece[half].reshape(ROWS, 48)
            turned[half, k * 48 : (k + 1) * 48, :] = block.T

    lane_block = lax.broadcasted_iota(jnp.int32, (CB, ROWS), 1) // MP

    def place(t, carry):
        out, inner, coef = trip[0, t], trip[1, t], trip[2, t]
        base = (out // 2) * (NK * CHUNK) + coef * (CB * CHUNK) + lax.rem(out, 2) * MP
        here = lane_block == inner
        for half in range(2):
            x = turned[half, pl.ds(t, CB, stride=48), :]
            for q in range(8 if half == 0 else MB - 8):
                y = pltpu.roll(x, lax.rem(inner + NB - q, NB) * MP, 1)
                at = pl.ds(base + half * 8 + q, CB, stride=CHUNK)
                dense[at, :] += jnp.where(here, y, 0.0)
        return carry

    lax.fori_loop(0, NTRIP, place, 0)

    def cut(n, carry):
        at = pl.ds(pl.multiple_of(n * ROWS, ROWS), ROWS)
        x = dense[at, :]
        high = x.astype(bf16)
        table[at, 0:128] = high
        table[at, 128:256] = high
        table[at, 256:384] = (x - high.astype(f32)).astype(bf16)
        return carry

    lax.fori_loop(0, NK, cut, 0)


def pack_kernel(me, guess_hbm, rhs_hbm, coef_hbm, send, own, guess, rhs, coef, sem):
    pairs = ((guess_hbm, guess), (rhs_hbm, rhs), (coef_hbm, coef))
    copies = [pltpu.make_async_copy(a, b, sem.at[n]) for n, (a, b) in enumerate(pairs)]
    for copy in copies:
        copy.start()
    zero = jnp.zeros((1, NX), f32)
    copies[0].wait()
    for y in range(NB):
        g = jnp.concatenate([guess[pl.ds(y, MB, stride=NB), :], zero], axis=0)
        for p in range(5):
            send[(y + 2 - p) % NB, p] = g
    copies[1].wait()
    for y in range(NB):
        r = jnp.concatenate([rhs[pl.ds(y, MB, stride=NB), :], zero], axis=0)
        for p in range(3):
            send[(y + 1 - p) % NB, 5 + p] = r
    copies[2].wait()
    for q in range(5):
        row = lax.rem(me[0] + q + NB - 2, NB)
        own[q, :NK] = coef[pl.ds(row, NK, stride=NB), :]
        own[q, NK:] = jnp.zeros((CP - NK, NX), f32)


def side_kernel(got, own, side):
    for q in range(1, 4):
        side[q - 1, ROWS:, :] = own[q]
        for b in range(NB):
            side[q - 1, b * MP : (b + 1) * MP, :] = got[b, q]


def put_columns(grad, tile, columns):
    for n, g in enumerate(columns):
        high = g.astype(bf16)
        low = (g - high.astype(f32)).astype(bf16)
        lanes = slice(n * NX, (n + 1) * NX)
        grad[tile, 0:128, lanes] = high
        grad[tile, 128:256, lanes] = low
        grad[tile, 256:384, lanes] = high


def put_weights(weight, place, halves):
    for n, a in enumerate(halves):
        weight[place, :, n * NX : (n + 1) * NX] = a


def sums(table, grad, tile, width, weight, places):
    rows = []
    for part in range(PART):
        w = jnp.dot(
            table[part * NK * CHUNK : (part + 1) * NK * CHUNK, :],
            grad[tile, :, :width],
            preferred_element_type=f32,
        )
        total = [jnp.zeros((CHUNK, width), f32) for _ in places]
        for k in range(NK):
            here = w[k * CHUNK : (k + 1) * CHUNK]
            for n, p in enumerate(places):
                total[n] = total[n] + weight[p, k : k + 1, :width] * here
        rows.append(total)
    return [jnp.concatenate([r[n] for r in rows], axis=0) for n in range(len(places))]


def to_right(x):
    return pltpu.roll(x, 1, 1)


def from_right(x):
    return pltpu.roll(x, NX - 1, 1)


def mean(a, b):
    return 0.5 * (a + b)


def along_x(plus, minus):
    return minus + plus - to_right(plus) - from_right(minus)


def blocks(got, p):
    return jnp.concatenate([got[b, p] for b in range(NB)], axis=0)


def plane_kernel(got, own, table, base, grad, weight):
    v = [blocks(got, p) for p in range(5)]
    put_columns(grad, 0, [v[1], v[2]])
    put_columns(grad, 1, [v[0], v[4]])
    put_columns(grad, 2, [v[3]])
    ax = [mean(own[r], from_right(own[r])) for r in range(5)]
    ay = [mean(own[r], own[r + 1]) for r in range(4)]
    put_weights(weight, 0, [ax[1], ax[2]])
    put_weights(weight, 1, [to_right(ax[1]), to_right(ax[2])])
    put_weights(weight, 2, [ay[1], ay[2]])
    put_weights(weight, 3, [ay[0], ay[1]])
    put_weights(weight, 4, [ay[0], ay[3]])
    put_weights(weight, 5, [ax[3]])
    put_weights(weight, 6, [to_right(ax[3])])
    put_weights(weight, 7, [ay[3]])
    put_weights(weight, 8, [ay[2]])
    xp, xm, yp, ym = sums(table, grad, 0, 2 * NX, weight, (0, 1, 2, 3))
    (edge,) = sums(table, grad, 1, 2 * NX, weight, (4,))
    xp3, xm3, yp3, ym3 = sums(table, grad, 2, NX, weight, (5, 6, 7, 8))
    plus = [edge[:, :NX], yp[:, :NX], yp[:, NX:], yp3]
    minus = [None, ym[:, :NX], ym[:, NX:], ym3, edge[:, NX:]]
    xs = [None, (xp[:, :NX], xm[:, :NX]), (xp[:, NX:], xm[:, NX:]), (xp3, xm3)]
    for r in (1, 2, 3):
        image = along_x(*xs[r]) + (minus[r] + plus[r] - plus[r - 1] - minus[r + 1])
        base[r - 1] = blocks(got, 4 + r) - image


def put_six(weight, own, low_coef, high_coef):
    c = own[2]
    ax = mean(c, from_right(c))
    six = (ax, to_right(ax), mean(c, own[3]), mean(own[1], c), mean(c, high_coef), mean(low_coef, c))
    for n, a in enumerate(six):
        put_weights(weight, n, [a])


def first_kernel(got, below, above, own, base, table, three, up, down, rest, grad, weight, six):
    for r in range(3):
        v = blocks(got, r + 1)
        put_columns(grad, r, [v - below[r, :ROWS], above[r, :ROWS] - v])
        low, high = mean(below[r, ROWS:], own[r + 1]), mean(own[r + 1], above[r, ROWS:])
        put_weights(weight, r, [low, high])
    put_six(six, own, below[1, ROWS:], above[1, ROWS:])
    for r in range(3):
        (flux,) = sums(table, grad, r, 2 * NX, weight, (r,))
        image = flux[:, :NX] - flux[:, NX:]
        three[r] = blocks(got, r + 1) + RELAX * (base[r] - image)
    put_columns(grad, 3, [three[1]])
    xp, xm, yp, ym, zp, zm = sums(table, grad, 3, NX, six, range(6))
    up[...] = zp
    down[...] = zm
    rest[...] = blocks(got, 6) - along_x(xp, xm) - ((yp + ym) + (zp + zm))


def second_kernel(three, own, table, rest, full, grad, weight):
    put_columns(grad, 0, [three[0], three[2]])
    put_weights(weight, 0, [mean(own[1], own[2]), mean(own[2], own[3])])
    (y,) = sums(table, grad, 0, 2 * NX, weight, (0,))
    full[...] = rest[...] + (y[:, :NX] + y[:, NX:])


def third_kernel(
    three, from_low, from_high, full, got, below, above, own, table, mid, up, down, y_up, y_down, rest, grad, six
):
    v = three[1] + RELAX * (full[...] + (from_low[...] + from_high[...]))
    mid[...] = v
    put_six(six, own, below[1, ROWS:], above[1, ROWS:])
    put_columns(grad, 0, [v])
    xp, xm, yp, ym, zp, zm = sums(table, grad, 0, NX, six, range(6))
    up[...] = zp
    down[...] = zm
    y_up[...] = yp
    y_down[...] = ym
    rest[...] = blocks(got, 6) - along_x(xp, xm) - ((yp + ym) + (zp + zm))


def back_kernel(mid, rest, from_low, from_high, y_up, y_down, send):
    whole = rest[...] + (from_low[...] + from_high[...])
    for b in range(NB):
        rows = slice(b * MP, (b + 1) * MP)
        send[b, 0] = mid[rows]
        send[b, 1] = whole[rows]
        send[b, 2] = y_up[rows]
        send[b, 3] = y_down[rows]


def last_kernel(got, out, residual):
    for y in range(NB):
        res = got[y, 1] + got[(y - 1) % NB, 2] + got[(y + 1) % NB, 3]
        new = got[y, 0] + RELAX * res
        residual[pl.ds(y, MB, stride=NB), :] = res[:MB]
        out[pl.ds(y, MB, stride=NB), :] = new[:MB]


def body(rhs, guess, coef, block_triples, offsets, values):
    slabs = lax.axis_size("slab")
    up = [(i, i + 1) for i in range(slabs - 1)]
    down = [(j, i) for i, j in up]

    def grads(tiles, width=2 * NX):
        return pltpu.VMEM((tiles, 3 * ROWS, width), bf16)

    def weights(count, width=2 * NX):
        return pltpu.VMEM((count, CP, width), f32)

    tile_flops = 2 * NK * ROWS * 3 * ROWS * 2 * NX
    flat = struct(ROWS, NX)
    me = lax.axis_index("chaos").astype(jnp.int32).reshape(1)
    send, own = call(
        pack_kernel,
        "pack",
        (struct(NB, 8, MP, NX), struct(5, CP, NX)),
        (me, guess.reshape(MB * NB, NX), rhs.reshape(MB * NB, NX), coef.reshape(NK * NB, NX)),
        scratch=[
            pltpu.VMEM((MB * NB, NX), f32),
            pltpu.VMEM((MB * NB, NX), f32),
            pltpu.VMEM((NK * NB, NX), f32),
            pltpu.SemaphoreType.DMA((3,)),
        ],
        specs=[SM, HBM, HBM, HBM],
        limit=FULL,
    )
    got = lax.all_to_all(send, "chaos", 0, 0, tiled=True)
    table = call(
        table_kernel,
        "table",
        struct(NK * ROWS, 3 * ROWS, dtype=bf16),
        (block_triples.T, values.transpose(1, 2, 3, 0)),
        scratch=[
            pltpu.VMEM((NK * ROWS, ROWS), f32),
            pltpu.VMEM((2, 8, MP, 48), f32),
            pltpu.VMEM((2, CB * 48, ROWS), f32),
        ],
        specs=[SM, VM],
        cost=6 * tile_flops,
    )
    got, table = lax.optimization_barrier((got, table))
    side = call(side_kernel, "side", struct(3, ROWS + CP, NX), (got, own))
    below = lax.ppermute(side, "slab", up)
    above = lax.ppermute(side, "slab", down)
    base = call(
        plane_kernel,
        "plane",
        struct(3, ROWS, NX),
        (got, own, table),
        scratch=[grads(3), weights(9)],
        cost=3 * tile_flops,
    )
    three, to_up, to_down, rest = call(
        first_kernel,
        "first",
        (struct(3, ROWS, NX), flat, flat, flat),
        (got, below, above, own, base, table),
        scratch=[grads(4), weights(3), weights(6, NX)],
        cost=4 * tile_flops,
    )
    from_low = lax.ppermute(to_up, "slab", up)
    from_high = lax.ppermute(to_down, "slab", down)
    full = call(
        second_kernel,
        "second",
        flat,
        (three, own, table, rest),
        scratch=[grads(1), weights(1)],
        cost=tile_flops,
    )
    mid, to_up, to_down, y_up, y_down, rest = call(
        third_kernel,
        "third",
        (flat,) * 6,
        (three, from_low, from_high, full, got, below, above, own, table),
        scratch=[grads(1, NX), weights(6, NX)],
        cost=tile_flops,
    )
    from_low = lax.ppermute(to_up, "slab", up)
    from_high = lax.ppermute(to_down, "slab", down)
    send = call(
        back_kernel,
        "back",
        struct(NB, 4, MP, NX),
        (mid, rest, from_low, from_high, y_up, y_down),
    )
    got = lax.all_to_all(send, "chaos", 0, 0, tiled=True)
    out, residual = call(
        last_kernel, "last", (struct(MB * NB, NX), struct(MB * NB, NX)), (got,)
    )
    return out.reshape(rhs.shape), residual.reshape(rhs.shape)


def solution(mesh):
    field = P("chaos", "slab", None, None)
    placed = (field, field, P(None, "slab", None, None), P(), P(), P())
    return jax.shard_map(
        body, mesh=mesh, in_specs=placed, out_specs=(field, field), check_vma=False
    )
```

time: 102 us -> 84.8 us (0.83)
  the two profiles are of different devices: /device:TPU:256 before, /device:TPU:241 now
where the time goes in v2:
time: 84.8 us; the launch traced here: 84.2 us
  starting transfers between devices  29 us (34%)
  Pallas kernels  27.2 us (32%)
  waiting for transfers between devices  14.2 us (17%)
  blocking collectives  10.1 us (12%)
  local copies, waits for them, and re-layouts  2.94 us (3%)
    pallas_call x9, Pallas kernels, call(): pl.pallas_call(kernel, out_shape=outs, in_specs=specs or [VM] * len(ins),...  27.2 us
    ppermute x2, waiting for transfers between devices, body(): from_high = lax.ppermute(to_down, 'slab', down)  13.7 us
    ppermute x2, starting transfers between devices, body(): from_low = lax.ppermute(to_up, 'slab', up)  10.6 us
    all_to_all x1, blocking collectives, body(): got = lax.all_to_all(send, 'chaos', 0, 0, tiled=True)  10.1 us
    ppermute x1, starting transfers between devices, body(): below = lax.ppermute(side, 'slab', up)  6.94 us
    ppermute x2, starting transfers between devices, body(): from_high = lax.ppermute(to_down, 'slab', down)  4.51 us
    all_to_all x1, starting transfers between devices, body(): got = lax.all_to_all(send, 'chaos', 0, 0, tiled=True)  4.15 us
    unnamed x6, local copies, waits for them, and re-layouts  2.94 us
  transfers between devices with their start and end apart: 7, of which 3 were waited for; matrix products, arithmetic and copies ran while one was open for 0% of the time, Pallas kernels for 18%

profile of v2, /device:TPU:241, one launch (start us, length us, event | category | flops | bytes accessed | tf_op | source)
XLA Modules:
  0.0 84.2 jit_solution(8792918372499694401)
XLA Ops:
  0.6 1.9 %pack.1 = (f32[8,8,16,128]{3,2,1,0:T(8,128)}, f32[5,40,128]{2,1,0:T(8,128)}) custom-call(s32[1]{0:T(128)} %bitcast.me, f32[120,128]{1,0:T(8,128)} %bitcast.15, f32[120,128]{1,0:T(8,128)} %bitcast.16, f32[288,128]{1,0:T(8,128)} %bitcast.14), custom_call_target="tpu_custom_call" | custom-call | tf_op jit(solution)/shard_map/pack/pallas_call | solution.py:35
  2.5 4.2 %all-to-all-start = ((f32[8,8,16,128]{3,2,1,0:T(8,128)}), f32[8,8,16,128]{3,2,1,0:T(8,128)}, u32[]{:S(2)}, u32[]{:S(2)}) async-start(f32[8,8,16,128]{3,2,1,0:T(8,128)} %get-tuple-element.18), calls=%async_computation | async-start | bytes 1048576 | tf_op jit(solution)/shard_map/all_to_all | solution.py:292
  6.7 0.0 copy-start.1
  6.7 1.4 %copy-done.1 = f32[48,15,12,15]{0,3,2,1:T(8,128)S(1)} copy-done((f32[48,15,12,15]{0,3,2,1:T(8,128)S(1)}, f32[48,15,12,15]{0,3,2,1:T(8,128)}, u32[]{:S(2)}) %copy-start.1) | copy-done | bytes 518424
  8.0 0.0 copy-start.2
  8.0 0.7 copy-done.2
  8.7 8.1 %table.1 = bf16[4608,384]{1,0:T(8,128)(2,1)S(1)} custom-call(s32[3,48]{1,0:T(4,128)S(1)} %bitcast.13, f32[15,12,15,48]{3,2,1,0:T(8,128)S(1)} %bitcast.12), custom_call_target="tpu_custom_call" | custom-call | flops 5435817984 | bytes 4194304 | tf_op jit(solution)/shard_map/table/pallas_call | solution.py:35
  16.8 0.0 all-to-all-done.got
  16.8 0.0 copy-start
  16.8 0.9 %copy-done = f32[5,40,128]{2,1,0:T(8,128)S(1)} copy-done((f32[5,40,128]{2,1,0:T(8,128)S(1)}, f32[5,40,128]{2,1,0:T(8,128)}, u32[]{:S(2)}) %copy-start) | copy-done | bytes 102424
  17.7 1.1 %side.1 = f32[3,168,128]{2,1,0:T(8,128)S(1)} custom-call(f32[8,8,16,128]{3,2,1,0:T(8,128)} %all-to-all-done.got, f32[5,40,128]{2,1,0:T(8,128)S(1)} %copy-done), custom_call_target="tpu_custom_call" | custom-call | tf_op jit(solution)/shard_map/side/pallas_call | solution.py:35
  18.8 2.8 %collective-permute-start.1 = (f32[3,168,128]{2,1,0:T(8,128)S(1)}, f32[3,168,128]{2,1,0:T(8,128)S(1)}, u32[]{:S(2)}, u32[]{:S(2)}) collective-permute-start(f32[3,168,128]{2,1,0:T(8,128)S(1)} %side.1), channel_id=1, source_target_pairs={{8,0},{16,8},{24,16},{32,24},{40,32},{48,40},{56,48},{64,56},{72,6... | collective-permute-start | bytes 774152 | tf_op jit(solution)/shard_map/ppermute | solution.py:309
  21.6 6.9 %collective-permute-start = (f32[3,168,128]{2,1,0:T(8,128)S(1)}, f32[3,168,128]{2,1,0:T(8,128)S(1)}, u32[]{:S(2)}, u32[]{:S(2)}) collective-permute-start(f32[3,168,128]{2,1,0:T(8,128)S(1)} %side.1), channel_id=1, source_target_pairs={{0,8},{8,16},{16,24},{24,32},{32,40},{40,48},{48,56},{56,64},{64,7... | collective-permute-start | bytes 774152 | tf_op jit(solution)/shard_map/ppermute | solution.py:308
  28.6 5.5 %plane.1.base = f32[3,128,128]{2,1,0:T(8,128)S(1)} custom-call(f32[8,8,16,128]{3,2,1,0:T(8,128)} %all-to-all-done.got, f32[5,40,128]{2,1,0:T(8,128)S(1)} %copy-done, bf16[4608,384]{1,0:T(8,128)(2,1)S(1)} %table.1), custom_call_target="tpu_custom_call" | custom-call | flops 2717908992 | bytes 4194304 | tf_op jit(solution)/shard_map/plane/pallas_call | solution.py:35
  34.1 0.0 collective-permute-done.1.above
  34.1 0.4 collective-permute-done.below
  34.5 6.1 %first.1 = (f32[3,128,128]{2,1,0:T(8,128)S(1)}, f32[128,128]{1,0:T(8,128)S(1)}, f32[128,128]{1,0:T(8,128)S(1)}, f32[128,128]{1,0:T(8,128)S(1)}) custom-call(f32[8,8,16,128]{3,2,1,0:T(8,128)} %all-to-all-done.got, f32[3,168,128]{2,1,0:T(8,128)S(1)} %collective-permute-done.below, f32[3,168,128]{2,1,0:T(8,128)S(1)} %collective-permute-done.1.above, ...), custom_call_target="tpu_custom_call" | custom-call | flops 3623878656 | bytes 4194304 | tf_op jit(solution)/shard_map/first/pallas_call | solution.py:35
  40.7 8.7 %collective-permute-start.2 = (f32[128,128]{1,0:T(8,128)S(1)}, f32[128,128]{1,0:T(8,128)S(1)}, u32[]{:S(2)}, u32[]{:S(2)}) collective-permute-start(f32[128,128]{1,0:T(8,128)S(1)} %get-tuple-element.23), channel_id=1, source_target_pairs={{0,8},{8,16},{16,24},{24,32},{32,40},{40,48},{48,56},{56,64},{64,7... | collective-permute-start | bytes 196616 | tf_op jit(solution)/shard_map/ppermute | solution.py:326
  49.3 2.1 %collective-permute-start.3 = (f32[128,128]{1,0:T(8,128)S(1)}, f32[128,128]{1,0:T(8,128)S(1)}, u32[]{:S(2)}, u32[]{:S(2)}) collective-permute-start(f32[128,128]{1,0:T(8,128)S(1)} %get-tuple-element.24), channel_id=1, source_target_pairs={{8,0},{16,8},{24,16},{32,24},{40,32},{48,40},{56,48},{64,56},{72,6... | collective-permute-start | bytes 196616 | tf_op jit(solution)/shard_map/ppermute | solution.py:327
  51.5 1.4 %second.1.full = f32[128,128]{1,0:T(8,128)S(1)} custom-call(f32[3,128,128]{2,1,0:T(8,128)S(1)} %get-tuple-element.22.three, f32[5,40,128]{2,1,0:T(8,128)S(1)} %copy-done, bf16[4608,384]{1,0:T(8,128)(2,1)S(1)} %table.1, f32[128,128]{1,0:T(8,128)S(1)} %get-tuple-element.25.rest), custom_call_target="tpu_custom_call" | custom-call | flops 905969664 | bytes 4194304 | tf_op jit(solution)/shard_map/second/pallas_call | solution.py:35
  52.9 0.0 collective-permute-done.2.from_low
  52.9 6.3 %collective-permute-done.3.from_high = f32[128,128]{1,0:T(8,128)S(1)} collective-permute-done((f32[128,128]{1,0:T(8,128)S(1)}, f32[128,128]{1,0:T(8,128)S(1)}, u32[]{:S(2)}, u32[]{:S(2)}) %collective-permute-start.3) | collective-permute-done | bytes 65568 | tf_op jit(solution)/shard_map/ppermute | solution.py:327
  59.2 2.4 %third.1 = (f32[128,128]{1,0:T(8,128)S(1)}, f32[128,128]{1,0:T(8,128)S(1)}, f32[128,128]{1,0:T(8,128)S(1)}, f32[128,128]{1,0:T(8,128)S(1)}, f32[128,128]{1,0:T(8,128)S(1)}, /*index=5*/f32[128,128]{1,0:T(8,128)S(1)}) custom-call(f32[3,128,128]{2,1,0:T(8,128)S(1)} %get-tuple-element.22.three, f32[128,128]{1,0:T(8,128)S(1)} %collective-permute-done.2.from_low, ...), custom_call_target="tpu_custom_call" | custom-call | flops 905969664 | bytes 4194304 | tf_op jit(solution)/shard_map/third/pallas_call | solution.py:35
  61.6 1.9 %collective-permute-start.4 = (f32[128,128]{1,0:T(8,128)S(1)}, f32[128,128]{1,0:T(8,128)S(1)}, u32[]{:S(2)}, u32[]{:S(2)}) collective-permute-start(f32[128,128]{1,0:T(8,128)S(1)} %get-tuple-element.28), channel_id=1, source_target_pairs={{0,8},{8,16},{16,24},{24,32},{32,40},{40,48},{48,56},{56,64},{64,7... | collective-permute-start | bytes 196616 | tf_op jit(solution)/shard_map/ppermute | solution.py:344
  63.6 2.4 %collective-permute-start.5 = (f32[128,128]{1,0:T(8,128)S(1)}, f32[128,128]{1,0:T(8,128)S(1)}, u32[]{:S(2)}, u32[]{:S(2)}) collective-permute-start(f32[128,128]{1,0:T(8,128)S(1)} %get-tuple-element.29), channel_id=1, source_target_pairs={{8,0},{16,8},{24,16},{32,24},{40,32},{48,40},{56,48},{64,56},{72,6... | collective-permute-start | bytes 196616 | tf_op jit(solution)/shard_map/ppermute | solution.py:345
  66.0 0.0 collective-permute-done.4.from_low
  66.0 7.4 %collective-permute-done.5.from_high = f32[128,128]{1,0:T(8,128)S(1)} collective-permute-done((f32[128,128]{1,0:T(8,128)S(1)}, f32[128,128]{1,0:T(8,128)S(1)}, u32[]{:S(2)}, u32[]{:S(2)}) %collective-permute-start.5) | collective-permute-done | bytes 65568 | tf_op jit(solution)/shard_map/ppermute | solution.py:345
  73.4 10.1 %all_to_all.10.got = f32[8,4,16,128]{3,2,1,0:T(8,128)S(1)} all-to-all(f32[8,4,16,128]{3,2,1,0:T(8,128)S(1)} %back.1), channel_id=1, replica_groups=mesh['slab'=64,'chaos'=8] {'chaos'}, dimensions={0} | all-to-all | bytes 524288 | tf_op jit(solution)/shard_map/all_to_all | solution.py:352
  83.5 0.7 last.1
  (1 shorter events, 0.0 us)
Async XLA Ops:
  2.5 14.3 %all-to-all-start = ((f32[8,8,16,128]{3,2,1,0:T(8,128)}), f32[8,8,16,128]{3,2,1,0:T(8,128)}, u32[]{:S(2)}, u32[]{:S(2)}) async-start(f32[8,8,16,128]{3,2,1,0:T(8,128)} %get-tuple-element.18), calls=%async_computation | async-start | bytes 1048576 | tf_op jit(solution)/shard_map/all_to_all | solution.py:292
  6.7 1.4 %copy-start.1 = (f32[48,15,12,15]{0,3,2,1:T(8,128)S(1)}, f32[48,15,12,15]{0,3,2,1:T(8,128)}, u32[]{:S(2)}) copy-start(f32[48,15,12,15]{0,3,2,1:T(8,128)} %param.10) | copy-start | bytes 1555204
  8.0 0.7 copy-start.2
  16.8 0.9 %copy-start = (f32[5,40,128]{2,1,0:T(8,128)S(1)}, f32[5,40,128]{2,1,0:T(8,128)}, u32[]{:S(2)}) copy-start(f32[5,40,128]{2,1,0:T(8,128)} %get-tuple-element.20.own) | copy-start | bytes 307204
  18.8 15.3 %collective-permute-start.1 = (f32[3,168,128]{2,1,0:T(8,128)S(1)}, f32[3,168,128]{2,1,0:T(8,128)S(1)}, u32[]{:S(2)}, u32[]{:S(2)}) collective-permute-start(f32[3,168,128]{2,1,0:T(8,128)S(1)} %side.1), channel_id=1, source_target_pairs={{8,0},{16,8},{24,16},{32,24},{40,32},{48,40},{56,48},{64,56},{72,6... | collective-permute-start | bytes 774152 | tf_op jit(solution)/shard_map/ppermute | solution.py:309
  21.6 12.9 %collective-permute-start = (f32[3,168,128]{2,1,0:T(8,128)S(1)}, f32[3,168,128]{2,1,0:T(8,128)S(1)}, u32[]{:S(2)}, u32[]{:S(2)}) collective-permute-start(f32[3,168,128]{2,1,0:T(8,128)S(1)} %side.1), channel_id=1, source_target_pairs={{0,8},{8,16},{16,24},{24,32},{32,40},{40,48},{48,56},{56,64},{64,7... | collective-permute-start | bytes 774152 | tf_op jit(solution)/shard_map/ppermute | solution.py:308
  40.7 12.2 %collective-permute-start.2 = (f32[128,128]{1,0:T(8,128)S(1)}, f32[128,128]{1,0:T(8,128)S(1)}, u32[]{:S(2)}, u32[]{:S(2)}) collective-permute-start(f32[128,128]{1,0:T(8,128)S(1)} %get-tuple-element.23), channel_id=1, source_target_pairs={{0,8},{8,16},{16,24},{24,32},{32,40},{40,48},{48,56},{56,64},{64,7... | collective-permute-start | bytes 196616 | tf_op jit(solution)/shard_map/ppermute | solution.py:326
  49.3 9.9 %collective-permute-start.3 = (f32[128,128]{1,0:T(8,128)S(1)}, f32[128,128]{1,0:T(8,128)S(1)}, u32[]{:S(2)}, u32[]{:S(2)}) collective-permute-start(f32[128,128]{1,0:T(8,128)S(1)} %get-tuple-element.24), channel_id=1, source_target_pairs={{8,0},{16,8},{24,16},{32,24},{40,32},{48,40},{56,48},{64,56},{72,6... | collective-permute-start | bytes 196616 | tf_op jit(solution)/shard_map/ppermute | solution.py:327
  61.6 4.3 %collective-permute-start.4 = (f32[128,128]{1,0:T(8,128)S(1)}, f32[128,128]{1,0:T(8,128)S(1)}, u32[]{:S(2)}, u32[]{:S(2)}) collective-permute-start(f32[128,128]{1,0:T(8,128)S(1)} %get-tuple-element.28), channel_id=1, source_target_pairs={{0,8},{8,16},{16,24},{24,32},{32,40},{40,48},{48,56},{56,64},{64,7... | collective-permute-start | bytes 196616 | tf_op jit(solution)/shard_map/ppermute | solution.py:344
  63.6 9.8 %collective-permute-start.5 = (f32[128,128]{1,0:T(8,128)S(1)}, f32[128,128]{1,0:T(8,128)S(1)}, u32[]{:S(2)}, u32[]{:S(2)}) collective-permute-start(f32[128,128]{1,0:T(8,128)S(1)} %get-tuple-element.29), channel_id=1, source_target_pairs={{8,0},{16,8},{24,16},{32,24},{40,32},{48,40},{56,48},{64,56},{72,6... | collective-permute-start | bytes 196616 | tf_op jit(solution)/shard_map/ppermute | solution.py:345

commit v3 on v2

v3 whole, which is shorter than its diff:
```python
import jax
import jax.numpy as jnp
from jax import lax
from jax.experimental import pallas as pl
from jax.experimental.pallas import tpu as pltpu
from jax.sharding import PartitionSpec as P

MB = 15
MP = 16
NB = 8
CB = 12
KC = 3
NK = 36
NTRIP = 36
LIST = 40
ROWS = NB * MP
PART = 4
CHUNK = ROWS // PART
NX = 128
CP = 40
RELAX = 0.1
f32 = jnp.float32
bf16 = jnp.bfloat16

VM = pl.BlockSpec(memory_space=pltpu.VMEM)
SM = pl.BlockSpec(memory_space=pltpu.SMEM)
ANY = pl.BlockSpec(memory_space=pl.ANY)
HBM = pl.BlockSpec(memory_space=pltpu.HBM)
LIMIT = 20 * 2**20
FULL = 60 * 2**20


def call(kernel, name, outs, ins, scratch=(), specs=None, cost=None, limit=LIMIT):
    estimate = None
    if cost is not None:
        estimate = pl.CostEstimate(flops=cost, bytes_accessed=4 * 2**20, transcendentals=0)
    return pl.pallas_call(
        kernel,
        out_shape=outs,
        in_specs=specs or [VM] * len(ins),
        out_specs=jax.tree.map(lambda _: VM, outs),
        scratch_shapes=scratch,
        compiler_params=pltpu.CompilerParams(vmem_limit_bytes=limit),
        cost_estimate=estimate,
        name=name,
    )(*ins)


def struct(*shape, dtype=f32):
    return jax.ShapeDtypeStruct(shape, dtype)


def table_kernel(trip, values, table, dense, piece, spread):
    dense[...] = jnp.zeros_like(dense)
    piece[...] = jnp.zeros_like(piece)
    first_block = lax.broadcasted_iota(jnp.int32, (LIST, ROWS), 1) < MP
    for half in range(2):
        count = min(8, MB - 8 * half)
        for k in range(CB):
            piece[half, :count, :MB, :] = values[8 * half : 8 * half + count, k]
            block = piece[half].reshape(ROWS, 48).T[:LIST]
            for q in range(8):
                y = pltpu.roll(block, (NB - q) % NB * MP, 1) if q else block
                at = pl.ds(k * LIST * 8 + q, LIST, stride=8)
                spread[half, at, :] = jnp.where(first_block, y, 0.0)

    def place(t, carry):
        out, inner, coef = trip[0, t], trip[1, t], trip[2, t]
        base = (out // 2) * (NK * CHUNK) + coef * (CB * CHUNK) + lax.rem(out, 2) * MP
        for half in range(2):
            for k in range(CB):
                x = spread[half, pl.ds(pl.multiple_of((k * LIST + t) * 8, 8), 8), :]
                at = pl.ds(pl.multiple_of(base + k * CHUNK + half * 8, 8), 8)
                dense[at, :] += pltpu.roll(x, inner * MP, 1)
        return carry

    lax.fori_loop(0, NTRIP, place, 0)

    def cut(n, carry):
        at = pl.ds(pl.multiple_of(n * ROWS, ROWS), ROWS)
        x = dense[at, :]
        high = x.astype(bf16)
        table[at, 0:128] = high
        table[at, 128:256] = high
        table[at, 256:384] = (x - high.astype(f32)).astype(bf16)
        return carry

    lax.fori_loop(0, NK, cut, 0)


def pack_kernel(guess_hbm, rhs_hbm, send, guess, rhs, sem):
    pairs = ((guess_hbm, guess), (rhs_hbm, rhs))
    copies = [pltpu.make_async_copy(a, b, sem.at[n]) for n, (a, b) in enumerate(pairs)]
    for copy in copies:
        copy.start()
    zero = jnp.zeros((1, NX), f32)
    copies[0].wait()
    for y in range(NB):
        g = jnp.concatenate([guess[pl.ds(y, MB, stride=NB), :], zero], axis=0)
        for p in range(5):
            send[(y + 2 - p) % NB, p] = g
    copies[1].wait()
    for y in range(NB):
        r = jnp.concatenate([rhs[pl.ds(y, MB, stride=NB), :], zero], axis=0)
        for p in range(3):
            send[(y + 1 - p) % NB, 5 + p] = r


def side_kernel(me, got, coef, table, side, own, rows):
    del table
    for q in range(5):
        row = lax.rem(me[0] + q + NB - 2, NB)
        c = jnp.concatenate(
            [coef[pl.ds(row, NK, stride=NB), :], jnp.zeros((CP - NK, NX), f32)], axis=0
        )
        own[q] = c
        if 1 <= q <= 3:
            side[q - 1, ROWS:, :] = c
    for q in range(8):
        for b in range(NB):
            x = got[b, q]
            rows[q, b * MP : (b + 1) * MP, :] = x
            if 1 <= q <= 3:
                side[q - 1, b * MP : (b + 1) * MP, :] = x


def put_columns(grad, tile, columns):
    for n, g in enumerate(columns):
        high = g.astype(bf16)
        low = (g - high.astype(f32)).astype(bf16)
        lanes = slice(n * NX, (n + 1) * NX)
        grad[tile, 0:128, lanes] = high
        grad[tile, 128:256, lanes] = low
        grad[tile, 256:384, lanes] = high


def put_weights(weight, place, halves):
    for n, a in enumerate(halves):
        weight[place, :, n * NX : (n + 1) * NX] = a


def sums(table, grad, tile, width, weight, places):
    rows = []
    for part in range(PART):
        w = jnp.dot(
            table[part * NK * CHUNK : (part + 1) * NK * CHUNK, :],
            grad[tile, :, :width],
            preferred_element_type=f32,
        )
        total = [jnp.zeros((CHUNK, width), f32) for _ in places]
        for k in range(NK):
            here = w[k * CHUNK : (k + 1) * CHUNK]
            for n, p in enumerate(places):
                total[n] = total[n] + weight[p, k : k + 1, :width] * here
        rows.append(total)
    return [jnp.concatenate([r[n] for r in rows], axis=0) for n in range(len(places))]


def to_right(x):
    return pltpu.roll(x, 1, 1)


def from_right(x):
    return pltpu.roll(x, NX - 1, 1)


def mean(a, b):
    return 0.5 * (a + b)


def along_x(plus, minus):
    return minus + plus - to_right(plus) - from_right(minus)


def plane_kernel(line, own, table, base, grad, weight, single):
    v = [line[p] for p in range(5)]
    put_columns(grad, 0, [v[1], v[2]])
    put_columns(grad, 1, [v[0], v[4]])
    put_columns(single, 0, [v[3]])
    ax = [mean(own[r], from_right(own[r])) for r in range(5)]
    ay = [mean(own[r], own[r + 1]) for r in range(4)]
    put_weights(weight, 0, [ax[1], ax[2]])
    put_weights(weight, 1, [to_right(ax[1]), to_right(ax[2])])
    put_weights(weight, 2, [ay[1], ay[2]])
    put_weights(weight, 3, [ay[0], ay[1]])
    put_weights(weight, 4, [ay[0], ay[3]])
    put_weights(weight, 5, [ax[3]])
    put_weights(weight, 6, [to_right(ax[3])])
    put_weights(weight, 7, [ay[3]])
    put_weights(weight, 8, [ay[2]])
    xp, xm, yp, ym = sums(table, grad, 0, 2 * NX, weight, (0, 1, 2, 3))
    (edge,) = sums(table, grad, 1, 2 * NX, weight, (4,))
    xp3, xm3, yp3, ym3 = sums(table, single, 0, NX, weight, (5, 6, 7, 8))
    plus = [edge[:, :NX], yp[:, :NX], yp[:, NX:], yp3]
    minus = [None, ym[:, :NX], ym[:, NX:], ym3, edge[:, NX:]]
    xs = [None, (xp[:, :NX], xm[:, :NX]), (xp[:, NX:], xm[:, NX:]), (xp3, xm3)]
    for r in (1, 2, 3):
        image = along_x(*xs[r]) + (minus[r] + plus[r] - plus[r - 1] - minus[r + 1])
        base[r - 1] = line[4 + r] - image


def put_six(six, own, low_coef, high_coef):
    c = own[2]
    ax = mean(c, from_right(c))
    weights = (ax, to_right(ax), mean(c, own[3]), mean(own[1], c), mean(c, high_coef), mean(low_coef, c))
    for n, a in enumerate(weights):
        six[n] = a


def row_sums(odd, v, right, table, single, six, first_out, second_out):
    put_columns(single, 0, [v])
    xp, xm, yp, ym, zp, zm = sums(table, single, 0, NX, six, range(6))
    first_out[...] = jnp.where(odd, zm, zp)
    second_out[...] = jnp.where(odd, zp, zm)
    return yp, ym, right - along_x(xp, xm) - ((yp + ym) + (zp + zm))


def first_kernel(
    me, line, side_a, side_b, own, base, table, three, first_out, second_out, rest, six, grad, weight, single
):
    odd = me[1] == 1
    rows = []
    for r in range(3):
        below = jnp.where(odd, side_a[r], side_b[r])
        above = jnp.where(odd, side_b[r], side_a[r])
        v = line[r + 1]
        put_columns(grad, r, [v - below[:ROWS], above[:ROWS] - v])
        low, high = mean(below[ROWS:], own[r + 1]), mean(own[r + 1], above[ROWS:])
        put_weights(weight, r, [low, high])
        if r == 1:
            put_six(six, own, below[ROWS:], above[ROWS:])
    for r in range(3):
        (flux,) = sums(table, grad, r, 2 * NX, weight, (r,))
        image = flux[:, :NX] - flux[:, NX:]
        three[r] = line[r + 1] + RELAX * (base[r] - image)
    _, _, left = row_sums(odd, three[1], line[6], table, single, six, first_out, second_out)
    rest[...] = left


def second_kernel(three, own, table, rest, full, grad, weight):
    put_columns(grad, 0, [three[0], three[2]])
    put_weights(weight, 0, [mean(own[1], own[2]), mean(own[2], own[3])])
    (y,) = sums(table, grad, 0, 2 * NX, weight, (0,))
    full[...] = rest[...] + (y[:, :NX] + y[:, NX:])


def third_kernel(
    me, three, from_a, from_b, full, line, six, table, mid, first_out, second_out, y_up, y_down, rest, single
):
    odd = me[1] == 1
    v = three[1] + RELAX * (full[...] + (from_a[...] + from_b[...]))
    mid[...] = v
    y_up[...], y_down[...], rest[...] = row_sums(
        odd, v, line[6], table, single, six, first_out, second_out
    )


def back_kernel(mid, rest, from_a, from_b, y_up, y_down, send):
    whole = rest[...] + (from_a[...] + from_b[...])
    for b in range(NB):
        rows = slice(b * MP, (b + 1) * MP)
        send[b, 0] = mid[rows]
        send[b, 1] = whole[rows]
        send[b, 2] = y_up[rows]
        send[b, 3] = y_down[rows]


def last_kernel(got, out, residual):
    for y in range(NB):
        res = got[y, 1] + got[(y - 1) % NB, 2] + got[(y + 1) % NB, 3]
        new = got[y, 0] + RELAX * res
        residual[pl.ds(y, MB, stride=NB), :] = res[:MB]
        out[pl.ds(y, MB, stride=NB), :] = new[:MB]


def body(rhs, guess, coef, block_triples, offsets, values):
    slabs = lax.axis_size("slab")
    pairs_a = [(i, i ^ 1) for i in range(slabs) if i ^ 1 < slabs]
    pairs_b = [(i, ((i + 1) ^ 1) - 1) for i in range(1, slabs) if ((i + 1) ^ 1) - 1 < slabs]

    def swap(a, b):
        return lax.ppermute(a, "slab", pairs_a), lax.ppermute(b, "slab", pairs_b)

    def grads(tiles):
        return pltpu.VMEM((tiles, 3 * ROWS, 2 * NX), bf16)

    def weights(count):
        return pltpu.VMEM((count, CP, 2 * NX), f32)

    single = pltpu.VMEM((1, 3 * ROWS, NX), bf16)
    tile_flops = 2 * NK * ROWS * 3 * ROWS * 2 * NX
    flat = struct(ROWS, NX)
    me = jnp.stack([lax.axis_index("chaos"), lax.rem(lax.axis_index("slab"), 2)]).astype(jnp.int32)
    send = call(
        pack_kernel,
        "pack",
        struct(NB, 8, MP, NX),
        (guess.reshape(MB * NB, NX), rhs.reshape(MB * NB, NX)),
        scratch=[
            pltpu.VMEM((MB * NB, NX), f32),
            pltpu.VMEM((MB * NB, NX), f32),
            pltpu.SemaphoreType.DMA((2,)),
        ],
        specs=[HBM, HBM],
        limit=FULL,
    )
    got = lax.all_to_all(send, "chaos", 0, 0, tiled=True)
    table = call(
        table_kernel,
        "table",
        struct(NK * ROWS, 3 * ROWS, dtype=bf16),
        (block_triples.T, values.transpose(1, 2, 3, 0)),
        scratch=[
            pltpu.VMEM((NK * ROWS, ROWS), f32),
            pltpu.VMEM((2, 8, MP, 48), f32),
            pltpu.VMEM((2, CB * LIST * 8, ROWS), f32),
        ],
        specs=[SM, VM],
        cost=6 * tile_flops,
    )
    side, own, line = call(
        side_kernel,
        "side",
        (struct(3, ROWS + CP, NX), struct(5, CP, NX), struct(8, ROWS, NX)),
        (me, got, coef.reshape(NK * NB, NX), table),
        specs=[SM, VM, VM, ANY],
    )
    side_a, side_b = swap(side, side)
    base = call(
        plane_kernel,
        "plane",
        struct(3, ROWS, NX),
        (line, own, table),
        scratch=[grads(2), weights(9), single],
        cost=3 * tile_flops,
    )
    three, to_a, to_b, rest, six = call(
        first_kernel,
        "first",
        (struct(3, ROWS, NX), flat, flat, flat, struct(6, CP, NX)),
        (me, line, side_a, side_b, own, base, table),
        scratch=[grads(3), weights(3), single],
        specs=[SM] + [VM] * 6,
        cost=4 * tile_flops,
    )
    from_a, from_b = swap(to_a, to_b)
    full = call(
        second_kernel,
        "second",
        flat,
        (three, own, table, rest),
        scratch=[grads(1), weights(1)],
        cost=tile_flops,
    )
    mid, to_a, to_b, y_up, y_down, rest = call(
        third_kernel,
        "third",
        (flat,) * 6,
        (me, three, from_a, from_b, full, line, six, table),
        scratch=[single],
        specs=[SM] + [VM] * 7,
        cost=tile_flops,
    )
    from_a, from_b = swap(to_a, to_b)
    send = call(
        back_kernel, "back", struct(NB, 4, MP, NX), (mid, rest, from_a, from_b, y_up, y_down)
    )
    got = lax.all_to_all(send, "chaos", 0, 0, tiled=True)
    out, residual = call(
        last_kernel, "last", (struct(MB * NB, NX), struct(MB * NB, NX)), (got,)
    )
    return out.reshape(rhs.shape), residual.reshape(rhs.shape)


def solution(mesh):
    field = P("chaos", "slab", None, None)
    placed = (field, field, P(None, "slab", None, None), P(), P(), P())
    return jax.shard_map(
        body, mesh=mesh, in_specs=placed, out_specs=(field, field), check_vma=False
    )
```

time: 84.8 us -> 77 us (0.908)
  the two profiles are of different devices: /device:TPU:241 before, /device:TPU:256 now
where the time goes in v3:
time: 77 us; the launch traced here: 76.5 us
  Pallas kernels  23.7 us (31%)
  starting transfers between devices  21.4 us (28%)
  waiting for transfers between devices  16.7 us (22%)
  blocking collectives  11 us (14%)
  local copies, waits for them, and re-layouts  2.96 us (4%)
    pallas_call x9, Pallas kernels, call(): pl.pallas_call(kernel, out_shape=outs, in_specs=specs or [VM] * len(ins),...  23.7 us
    ppermute x6, starting transfers between devices, swap(): return (lax.ppermute(a, 'slab', pairs_a), lax.ppermute(b, 'slab', pairs_b))  16.1 us
    ppermute x6, waiting for transfers between devices, swap(): return (lax.ppermute(a, 'slab', pairs_a), lax.ppermute(b, 'slab', pairs_b))  15.4 us
    all_to_all x1, blocking collectives, body(): got = lax.all_to_all(send, 'chaos', 0, 0, tiled=True)  11 us
    all_to_all x1, starting transfers between devices, body(): got = lax.all_to_all(send, 'chaos', 0, 0, tiled=True)  5.32 us
    unnamed x6, local copies, waits for them, and re-layouts  2.96 us
  transfers between devices with their start and end apart: 7, of which 4 were waited for; matrix products, arithmetic and copies ran while one was open for 0% of the time, Pallas kernels for 16%

profile of v3, /device:TPU:256, one launch (start us, length us, event | category | flops | bytes accessed | tf_op | source)
XLA Modules:
  0.0 76.5 jit_solution(14062781819574687044)
XLA Ops:
  0.6 1.7 %pack.1 = f32[8,8,16,128]{3,2,1,0:T(8,128)} custom-call(f32[120,128]{1,0:T(8,128)} %bitcast.16, f32[120,128]{1,0:T(8,128)} %bitcast.17), custom_call_target="tpu_custom_call" | custom-call | tf_op jit(solution)/shard_map/pack/pallas_call | solution.py:37
  2.3 5.3 %all-to-all-start = ((f32[8,8,16,128]{3,2,1,0:T(8,128)}), f32[8,8,16,128]{3,2,1,0:T(8,128)}, u32[]{:S(2)}, u32[]{:S(2)}) async-start(f32[8,8,16,128]{3,2,1,0:T(8,128)} %pack.1), calls=%async_computation | async-start | bytes 1048576 | tf_op jit(solution)/shard_map/all_to_all | solution.py:307
  7.7 0.1 pad_add_fusion.me
  7.7 0.0 copy-start.1
  7.7 1.4 %copy-done.1 = f32[48,15,12,15]{0,3,2,1:T(8,128)S(1)} copy-done((f32[48,15,12,15]{0,3,2,1:T(8,128)S(1)}, f32[48,15,12,15]{0,3,2,1:T(8,128)}, u32[]{:S(2)}) %copy-start.1) | copy-done | bytes 518424
  9.1 0.0 copy-start.2
  9.1 0.7 copy-done.2
  9.8 6.3 %table.1 = bf16[4608,384]{1,0:T(8,128)(2,1)S(1)} custom-call(s32[3,48]{1,0:T(4,128)S(1)} %bitcast.15, f32[15,12,15,48]{3,2,1,0:T(8,128)S(1)} %bitcast.14), custom_call_target="tpu_custom_call" | custom-call | flops 5435817984 | bytes 4194304 | tf_op jit(solution)/shard_map/table/pallas_call | solution.py:37
  16.1 1.3 %all-to-all-done.got = f32[8,8,16,128]{3,2,1,0:T(8,128)} async-done(((f32[8,8,16,128]{3,2,1,0:T(8,128)}), f32[8,8,16,128]{3,2,1,0:T(8,128)}, u32[]{:S(2)}, u32[]{:S(2)}) %all-to-all-start) | async-done | bytes 524320 | tf_op jit(solution)/shard_map/all_to_all | solution.py:307
  17.3 0.0 copy-start
  17.3 0.9 %copy-done = f32[36,1,8,128]{3,2,1,0:T(8,128)S(1)} copy-done((f32[36,1,8,128]{3,2,1,0:T(8,128)S(1)}, f32[36,1,8,128]{3,2,1,0:T(8,128)}, u32[]{:S(2)}) %copy-start) | copy-done | bytes 147480
  18.3 1.1 %side.1 = (f32[3,168,128]{2,1,0:T(8,128)S(1)}, f32[5,40,128]{2,1,0:T(8,128)S(1)}, f32[8,128,128]{2,1,0:T(8,128)S(1)}) custom-call(s32[2]{0:T(128)S(1)} %pad_add_fusion.me, f32[8,8,16,128]{3,2,1,0:T(8,128)} %all-to-all-done.got, f32[288,128]{1,0:T(8,128)S(1)} %bitcast.13, bf16[4608,384]{1,0:T(8,128)(2,1)S(1)} %table.1), custom_call_target="tpu_custom_call" | custom-call | tf_op jit(solution)/shard_map/side/pallas_call | solution.py:37
  19.4 2.3 %collective-permute-start.1 = (f32[3,168,128]{2,1,0:T(8,128)S(1)}, f32[3,168,128]{2,1,0:T(8,128)S(1)}, u32[]{:S(2)}, u32[]{:S(2)}) collective-permute-start(f32[3,168,128]{2,1,0:T(8,128)S(1)} %get-tuple-element.19), channel_id=1, source_target_pairs={{8,16},{16,8},{24,32},{32,24},{40,48},{48,40},{56,64},{64,56},{72,... | collective-permute-start | bytes 774152 | tf_op jit(solution)/shard_map/ppermute | solution.py:282
  21.7 4.2 %collective-permute-start = (f32[3,168,128]{2,1,0:T(8,128)S(1)}, f32[3,168,128]{2,1,0:T(8,128)S(1)}, u32[]{:S(2)}, u32[]{:S(2)}) collective-permute-start(f32[3,168,128]{2,1,0:T(8,128)S(1)} %get-tuple-element.19), channel_id=1, source_target_pairs={{0,8},{8,0},{16,24},{24,16},{32,40},{40,32},{48,56},{56,48},{64,72... | collective-permute-start | bytes 774152 | tf_op jit(solution)/shard_map/ppermute | solution.py:282
  25.9 4.7 %plane.1.base = f32[3,128,128]{2,1,0:T(8,128)S(1)} custom-call(f32[8,128,128]{2,1,0:T(8,128)S(1)} %get-tuple-element.18.line, f32[5,40,128]{2,1,0:T(8,128)S(1)} %get-tuple-element.20.own, bf16[4608,384]{1,0:T(8,128)(2,1)S(1)} %table.1), custom_call_target="tpu_custom_call" | custom-call | flops 2717908992 | bytes 4194304 | tf_op jit(solution)/shard_map/plane/pallas_call | solution.py:37
  30.6 3.0 %collective-permute-done.1.side_b = f32[3,168,128]{2,1,0:T(8,128)S(1)} collective-permute-done((f32[3,168,128]{2,1,0:T(8,128)S(1)}, f32[3,168,128]{2,1,0:T(8,128)S(1)}, u32[]{:S(2)}, u32[]{:S(2)}) %collective-permute-start.1) | collective-permute-done | bytes 258080 | tf_op jit(solution)/shard_map/ppermute | solution.py:282
  33.6 0.0 collective-permute-done.side_a
  33.6 5.8 %first.1 = (f32[3,128,128]{2,1,0:T(8,128)S(1)}, f32[128,128]{1,0:T(8,128)S(1)}, f32[128,128]{1,0:T(8,128)S(1)}, f32[128,128]{1,0:T(8,128)S(1)}, f32[6,40,128]{2,1,0:T(8,128)S(1)}) custom-call(s32[2]{0:T(128)S(1)} %pad_add_fusion.me, f32[8,128,128]{2,1,0:T(8,128)S(1)} %get-tuple-element.18.line, f32[3,168,128]{2,1,0:T(8,128)S(1)} %collective-permute-done.side_a, ...), custom_call_target="tpu_custom_call" | custom-call | flops 3623878656 | bytes 4194304 | tf_op jit(solution)/shard_map/first/pallas_call | solution.py:37
  39.4 1.9 %collective-permute-start.2 = (f32[128,128]{1,0:T(8,128)S(1)}, f32[128,128]{1,0:T(8,128)S(1)}, u32[]{:S(2)}, u32[]{:S(2)}) collective-permute-start(f32[128,128]{1,0:T(8,128)S(1)} %get-tuple-element.22), channel_id=1, source_target_pairs={{0,8},{8,0},{16,24},{24,16},{32,40},{40,32},{48,56},{56,48},{64,72... | collective-permute-start | bytes 196616 | tf_op jit(solution)/shard_map/ppermute | solution.py:282
  41.3 2.9 %collective-permute-start.3 = (f32[128,128]{1,0:T(8,128)S(1)}, f32[128,128]{1,0:T(8,128)S(1)}, u32[]{:S(2)}, u32[]{:S(2)}) collective-permute-start(f32[128,128]{1,0:T(8,128)S(1)} %get-tuple-element.23), channel_id=1, source_target_pairs={{8,16},{16,8},{24,32},{32,24},{40,48},{48,40},{56,64},{64,56},{72,... | collective-permute-start | bytes 196616 | tf_op jit(solution)/shard_map/ppermute | solution.py:282
  44.2 1.4 %second.1.full = f32[128,128]{1,0:T(8,128)S(1)} custom-call(f32[3,128,128]{2,1,0:T(8,128)S(1)} %get-tuple-element.21.three, f32[5,40,128]{2,1,0:T(8,128)S(1)} %get-tuple-element.20.own, bf16[4608,384]{1,0:T(8,128)(2,1)S(1)} %table.1, f32[128,128]{1,0:T(8,128)S(1)} %get-tuple-element.24.rest), custom_call_target="tpu_custom_call" | custom-call | flops 905969664 | bytes 4194304 | tf_op jit(solution)/shard_map/second/pallas_call | solution.py:37
  45.6 0.0 collective-permute-done.2.from_a
  45.6 5.5 %collective-permute-done.3.from_b = f32[128,128]{1,0:T(8,128)S(1)} collective-permute-done((f32[128,128]{1,0:T(8,128)S(1)}, f32[128,128]{1,0:T(8,128)S(1)}, u32[]{:S(2)}, u32[]{:S(2)}) %collective-permute-start.3) | collective-permute-done | bytes 65568 | tf_op jit(solution)/shard_map/ppermute | solution.py:282
  51.1 2.0 %third.1 = (f32[128,128]{1,0:T(8,128)S(1)}, f32[128,128]{1,0:T(8,128)S(1)}, f32[128,128]{1,0:T(8,128)S(1)}, f32[128,128]{1,0:T(8,128)S(1)}, f32[128,128]{1,0:T(8,128)S(1)}, /*index=5*/f32[128,128]{1,0:T(8,128)S(1)}) custom-call(s32[2]{0:T(128)S(1)} %pad_add_fusion.me, f32[3,128,128]{2,1,0:T(8,128)S(1)} %get-tuple-element.21.three, ...), custom_call_target="tpu_custom_call" | custom-call | flops 905969664 | bytes 4194304 | tf_op jit(solution)/shard_map/third/pallas_call | solution.py:37
  53.1 1.9 %collective-permute-start.4 = (f32[128,128]{1,0:T(8,128)S(1)}, f32[128,128]{1,0:T(8,128)S(1)}, u32[]{:S(2)}, u32[]{:S(2)}) collective-permute-start(f32[128,128]{1,0:T(8,128)S(1)} %get-tuple-element.28), channel_id=1, source_target_pairs={{0,8},{8,0},{16,24},{24,16},{32,40},{40,32},{48,56},{56,48},{64,72... | collective-permute-start | bytes 196616 | tf_op jit(solution)/shard_map/ppermute | solution.py:282
  55.0 2.8 %collective-permute-start.5 = (f32[128,128]{1,0:T(8,128)S(1)}, f32[128,128]{1,0:T(8,128)S(1)}, u32[]{:S(2)}, u32[]{:S(2)}) collective-permute-start(f32[128,128]{1,0:T(8,128)S(1)} %get-tuple-element.29), channel_id=1, source_target_pairs={{8,16},{16,8},{24,32},{32,24},{40,48},{48,40},{56,64},{64,56},{72,... | collective-permute-start | bytes 196616 | tf_op jit(solution)/shard_map/ppermute | solution.py:282
  57.9 0.0 collective-permute-done.4.from_a
  57.9 7.0 %collective-permute-done.5.from_b = f32[128,128]{1,0:T(8,128)S(1)} collective-permute-done((f32[128,128]{1,0:T(8,128)S(1)}, f32[128,128]{1,0:T(8,128)S(1)}, u32[]{:S(2)}, u32[]{:S(2)}) %collective-permute-start.5) | collective-permute-done | bytes 65568 | tf_op jit(solution)/shard_map/ppermute | solution.py:282
  64.9 11.0 %all_to_all.10.got = f32[8,4,16,128]{3,2,1,0:T(8,128)S(1)} all-to-all(f32[8,4,16,128]{3,2,1,0:T(8,128)S(1)} %back.1), channel_id=1, replica_groups=mesh['slab'=64,'chaos'=8] {'chaos'}, dimensions={0} | all-to-all | bytes 524288 | tf_op jit(solution)/shard_map/all_to_all | solution.py:368
  75.8 0.7 last.1
  (1 shorter events, 0.0 us)
Async XLA Ops:
  2.3 15.0 %all-to-all-start = ((f32[8,8,16,128]{3,2,1,0:T(8,128)}), f32[8,8,16,128]{3,2,1,0:T(8,128)}, u32[]{:S(2)}, u32[]{:S(2)}) async-start(f32[8,8,16,128]{3,2,1,0:T(8,128)} %pack.1), calls=%async_computation | async-start | bytes 1048576 | tf_op jit(solution)/shard_map/all_to_all | solution.py:307
  7.7 1.4 %copy-start.1 = (f32[48,15,12,15]{0,3,2,1:T(8,128)S(1)}, f32[48,15,12,15]{0,3,2,1:T(8,128)}, u32[]{:S(2)}) copy-start(f32[48,15,12,15]{0,3,2,1:T(8,128)} %param.10) | copy-start | bytes 1555204
  9.1 0.7 copy-start.2
  17.3 0.9 %copy-start = (f32[36,1,8,128]{3,2,1,0:T(8,128)S(1)}, f32[36,1,8,128]{3,2,1,0:T(8,128)}, u32[]{:S(2)}) copy-start(f32[36,1,8,128]{3,2,1,0:T(8,128)} %param.8) | copy-start | bytes 442372
  19.4 14.2 %collective-permute-start.1 = (f32[3,168,128]{2,1,0:T(8,128)S(1)}, f32[3,168,128]{2,1,0:T(8,128)S(1)}, u32[]{:S(2)}, u32[]{:S(2)}) collective-permute-start(f32[3,168,128]{2,1,0:T(8,128)S(1)} %get-tuple-element.19), channel_id=1, source_target_pairs={{8,16},{16,8},{24,32},{32,24},{40,48},{48,40},{56,64},{64,56},{72,... | collective-permute-start | bytes 774152 | tf_op jit(solution)/shard_map/ppermute | solution.py:282
  21.7 12.0 %collective-permute-start = (f32[3,168,128]{2,1,0:T(8,128)S(1)}, f32[3,168,128]{2,1,0:T(8,128)S(1)}, u32[]{:S(2)}, u32[]{:S(2)}) collective-permute-start(f32[3,168,128]{2,1,0:T(8,128)S(1)} %get-tuple-element.19), channel_id=1, source_target_pairs={{0,8},{8,0},{16,24},{24,16},{32,40},{40,32},{48,56},{56,48},{64,72... | collective-permute-start | bytes 774152 | tf_op jit(solution)/shard_map/ppermute | solution.py:282
  39.4 6.3 %collective-permute-start.2 = (f32[128,128]{1,0:T(8,128)S(1)}, f32[128,128]{1,0:T(8,128)S(1)}, u32[]{:S(2)}, u32[]{:S(2)}) collective-permute-start(f32[128,128]{1,0:T(8,128)S(1)} %get-tuple-element.22), channel_id=1, source_target_pairs={{0,8},{8,0},{16,24},{24,16},{32,40},{40,32},{48,56},{56,48},{64,72... | collective-permute-start | bytes 196616 | tf_op jit(solution)/shard_map/ppermute | solution.py:282
  41.3 9.8 %collective-permute-start.3 = (f32[128,128]{1,0:T(8,128)S(1)}, f32[128,128]{1,0:T(8,128)S(1)}, u32[]{:S(2)}, u32[]{:S(2)}) collective-permute-start(f32[128,128]{1,0:T(8,128)S(1)} %get-tuple-element.23), channel_id=1, source_target_pairs={{8,16},{16,8},{24,32},{32,24},{40,48},{48,40},{56,64},{64,56},{72,... | collective-permute-start | bytes 196616 | tf_op jit(solution)/shard_map/ppermute | solution.py:282
  53.1 4.7 %collective-permute-start.4 = (f32[128,128]{1,0:T(8,128)S(1)}, f32[128,128]{1,0:T(8,128)S(1)}, u32[]{:S(2)}, u32[]{:S(2)}) collective-permute-start(f32[128,128]{1,0:T(8,128)S(1)} %get-tuple-element.28), channel_id=1, source_target_pairs={{0,8},{8,0},{16,24},{24,16},{32,40},{40,32},{48,56},{56,48},{64,72... | collective-permute-start | bytes 196616 | tf_op jit(solution)/shard_map/ppermute | solution.py:282
  55.0 9.8 %collective-permute-start.5 = (f32[128,128]{1,0:T(8,128)S(1)}, f32[128,128]{1,0:T(8,128)S(1)}, u32[]{:S(2)}, u32[]{:S(2)}) collective-permute-start(f32[128,128]{1,0:T(8,128)S(1)} %get-tuple-element.29), channel_id=1, source_target_pairs={{8,16},{16,8},{24,32},{32,24},{40,48},{48,40},{56,64},{64,56},{72,... | collective-permute-start | bytes 196616 | tf_op jit(solution)/shard_map/ppermute | solution.py:282

commit v4 on v3

--- a/solution.py
+++ b/solution.py
@@ -215,40 +215,46 @@
     return yp, ym, right - along_x(xp, xm) - ((yp + ym) + (zp + zm))
 
 
+def new_row(odd, line, side_a, side_b, own, base, table, grad, weight, tile, r):
+    below = jnp.where(odd, side_a[r], side_b[r])
+    above = jnp.where(odd, side_b[r], side_a[r])
+    v = line[r + 1]
+    put_columns(grad, tile, [v - below[:ROWS], above[:ROWS] - v])
+    low, high = mean(below[ROWS:], own[r + 1]), mean(own[r + 1], above[ROWS:])
+    put_weights(weight, tile, [low, high])
+    (flux,) = sums(table, grad, tile, 2 * NX, weight, (tile,))
+    new = v + RELAX * (base[r] - (flux[:, :NX] - flux[:, NX:]))
+    return new, below[ROWS:], above[ROWS:]
+
+
 def first_kernel(
-    me, line, side_a, side_b, own, base, table, three, first_out, second_out, rest, six, grad, weight, single
+    me, line, side_a, side_b, own, base, table, one, first_out, second_out, rest, six, grad, weight, single
 ):
     odd = me[1] == 1
-    rows = []
-    for r in range(3):
-        below = jnp.where(odd, side_a[r], side_b[r])
-        above = jnp.where(odd, side_b[r], side_a[r])
-        v = line[r + 1]
-        put_columns(grad, r, [v - below[:ROWS], above[:ROWS] - v])
-        low, high = mean(below[ROWS:], own[r + 1]), mean(own[r + 1], above[ROWS:])
-        put_weights(weight, r, [low, high])
-        if r == 1:
-            put_six(six, own, below[ROWS:], above[ROWS:])
-    for r in range(3):
-        (flux,) = sums(table, grad, r, 2 * NX, weight, (r,))
-        image = flux[:, :NX] - flux[:, NX:]
-        three[r] = line[r + 1] + RELAX * (base[r] - image)
-    _, _, left = row_sums(odd, three[1], line[6], table, single, six, first_out, second_out)
+    v, low, high = new_row(odd, line, side_a, side_b, own, base, table, grad, weight, 0, 1)
+    one[...] = v
+    put_six(six, own, low, high)
+    _, _, left = row_sums(odd, v, line[6], table, single, six, first_out, second_out)
     rest[...] = left
 
 
-def second_kernel(three, own, table, rest, full, grad, weight):
-    put_columns(grad, 0, [three[0], three[2]])
-    put_weights(weight, 0, [mean(own[1], own[2]), mean(own[2], own[3])])
-    (y,) = sums(table, grad, 0, 2 * NX, weight, (0,))
+def second_kernel(me, line, side_a, side_b, own, base, table, rest, full, grad, weight):
+    odd = me[1] == 1
+    beside = [
+        new_row(odd, line, side_a, side_b, own, base, table, grad, weight, n, r)[0]
+        for n, r in enumerate((0, 2))
+    ]
+    put_columns(grad, 2, beside)
+    put_weights(weight, 2, [mean(own[1], own[2]), mean(own[2], own[3])])
+    (y,) = sums(table, grad, 2, 2 * NX, weight, (2,))
     full[...] = rest[...] + (y[:, :NX] + y[:, NX:])
 
 
 def third_kernel(
-    me, three, from_a, from_b, full, line, six, table, mid, first_out, second_out, y_up, y_down, rest, single
+    me, one, from_a, from_b, full, line, six, table, mid, first_out, second_out, y_up, y_down, rest, single
 ):
     odd = me[1] == 1
-    v = three[1] + RELAX * (full[...] + (from_a[...] + from_b[...]))
+    v = one[...] + RELAX * (full[...] + (from_a[...] + from_b[...]))
     mid[...] = v
     y_up[...], y_down[...], rest[...] = row_sums(
         odd, v, line[6], table, single, six, first_out, second_out
@@ -334,29 +340,30 @@
         scratch=[grads(2), weights(9), single],
         cost=3 * tile_flops,
     )
-    three, to_a, to_b, rest, six = call(
+    one, to_a, to_b, rest, six = call(
         first_kernel,
         "first",
-        (struct(3, ROWS, NX), flat, flat, flat, struct(6, CP, NX)),
+        (flat, flat, flat, flat, struct(6, CP, NX)),
         (me, line, side_a, side_b, own, base, table),
-        scratch=[grads(3), weights(3), single],
+        scratch=[grads(1), weights(1), single],
         specs=[SM] + [VM] * 6,
-        cost=4 * tile_flops,
+        cost=2 * tile_flops,
     )
     from_a, from_b = swap(to_a, to_b)
     full = call(
         second_kernel,
         "second",
         flat,
-        (three, own, table, rest),
-        scratch=[grads(1), weights(1)],
-        cost=tile_flops,
+        (me, line, side_a, side_b, own, base, table, rest),
+        scratch=[grads(3), weights(3)],
+        specs=[SM] + [VM] * 7,
+        cost=3 * tile_flops,
     )
     mid, to_a, to_b, y_up, y_down, rest = call(
         third_kernel,
         "third",
         (flat,) * 6,
-        (me, three, from_a, from_b, full, line, six, table),
+        (me, one, from_a, from_b, full, line, six, table),
         scratch=[single],
         specs=[SM] + [VM] * 7,
         cost=tile_flops,

time: 77 us -> 74.7 us (0.970)
  waiting for transfers between devices: 16.7 us -> 11.4 us
  starting transfers between devices: 21.4 us -> 23.4 us
  Pallas kernels: 23.7 us -> 24.6 us
    ppermute x6, waiting for transfers between devices: 15.4 us -> 10.1 us  [swap(): return (lax.ppermute(a, 'slab', pairs_a), lax.ppermute(b, 'slab', pairs_b))]
    ppermute x6, starting transfers between devices: 16.1 us -> 18.1 us  [swap(): return (lax.ppermute(a, 'slab', pairs_a), lax.ppermute(b, 'slab', pairs_b))]
    pallas_call x9, Pallas kernels: 23.7 us -> 24.6 us  [call(): pl.pallas_call(kernel, out_shape=outs, in_specs=specs or [VM] * len(ins),...]
  transfers between devices with their start and end apart: 7 -> 7, of which waited for: 4 -> 4; matrix products, arithmetic and copies ran while one was open for 0% -> 0% of each run, Pallas kernels for 16% -> 21%
where the time goes in v4:
time: 74.7 us; the launch traced here: 74.1 us
  Pallas kernels  24.6 us (33%)
  starting transfers between devices  23.4 us (31%)
  waiting for transfers between devices  11.4 us (15%)
  blocking collectives  11 us (15%)
  local copies, waits for them, and re-layouts  2.96 us (4%)
    pallas_call x9, Pallas kernels, call(): pl.pallas_call(kernel, out_shape=outs, in_specs=specs or [VM] * len(ins),...  24.6 us
    ppermute x6, starting transfers between devices, swap(): return (lax.ppermute(a, 'slab', pairs_a), lax.ppermute(b, 'slab', pairs_b))  18.1 us
    all_to_all x1, blocking collectives, body(): got = lax.all_to_all(send, 'chaos', 0, 0, tiled=True)  11 us
    ppermute x6, waiting for transfers between devices, swap(): return (lax.ppermute(a, 'slab', pairs_a), lax.ppermute(b, 'slab', pairs_b))  10.1 us
    all_to_all x1, starting transfers between devices, body(): got = lax.all_to_all(send, 'chaos', 0, 0, tiled=True)  5.32 us
    unnamed x6, local copies, waits for them, and re-layouts  2.96 us
  transfers between devices with their start and end apart: 7, of which 4 were waited for; matrix products, arithmetic and copies ran while one was open for 0% of the time, Pallas kernels for 21%

profile of v4, /device:TPU:256, one launch (start us, length us, event | category | flops | bytes accessed | tf_op | source)
XLA Modules:
  0.0 74.1 jit_solution(5825703510729778099)
XLA Ops:
  0.6 1.7 %pack.1 = f32[8,8,16,128]{3,2,1,0:T(8,128)} custom-call(f32[120,128]{1,0:T(8,128)} %bitcast.16, f32[120,128]{1,0:T(8,128)} %bitcast.17), custom_call_target="tpu_custom_call" | custom-call | tf_op jit(solution)/shard_map/pack/pallas_call | solution.py:37
  2.3 5.3 %all-to-all-start = ((f32[8,8,16,128]{3,2,1,0:T(8,128)}), f32[8,8,16,128]{3,2,1,0:T(8,128)}, u32[]{:S(2)}, u32[]{:S(2)}) async-start(f32[8,8,16,128]{3,2,1,0:T(8,128)} %pack.1), calls=%async_computation | async-start | bytes 1048576 | tf_op jit(solution)/shard_map/all_to_all | solution.py:313
  7.7 0.1 pad_add_fusion.me
  7.7 0.0 copy-start.1
  7.7 1.4 %copy-done.1 = f32[48,15,12,15]{0,3,2,1:T(8,128)S(1)} copy-done((f32[48,15,12,15]{0,3,2,1:T(8,128)S(1)}, f32[48,15,12,15]{0,3,2,1:T(8,128)}, u32[]{:S(2)}) %copy-start.1) | copy-done | bytes 518424
  9.1 0.0 copy-start.2
  9.1 0.7 copy-done.2
  9.8 6.3 %table.1 = bf16[4608,384]{1,0:T(8,128)(2,1)S(1)} custom-call(s32[3,48]{1,0:T(4,128)S(1)} %bitcast.15, f32[15,12,15,48]{3,2,1,0:T(8,128)S(1)} %bitcast.14), custom_call_target="tpu_custom_call" | custom-call | flops 5435817984 | bytes 4194304 | tf_op jit(solution)/shard_map/table/pallas_call | solution.py:37
  16.1 1.3 %all-to-all-done.got = f32[8,8,16,128]{3,2,1,0:T(8,128)} async-done(((f32[8,8,16,128]{3,2,1,0:T(8,128)}), f32[8,8,16,128]{3,2,1,0:T(8,128)}, u32[]{:S(2)}, u32[]{:S(2)}) %all-to-all-start) | async-done | bytes 524320 | tf_op jit(solution)/shard_map/all_to_all | solution.py:313
  17.3 0.0 copy-start
  17.3 0.9 %copy-done = f32[36,1,8,128]{3,2,1,0:T(8,128)S(1)} copy-done((f32[36,1,8,128]{3,2,1,0:T(8,128)S(1)}, f32[36,1,8,128]{3,2,1,0:T(8,128)}, u32[]{:S(2)}) %copy-start) | copy-done | bytes 147480
  18.3 1.1 %side.1 = (f32[3,168,128]{2,1,0:T(8,128)S(1)}, f32[5,40,128]{2,1,0:T(8,128)S(1)}, f32[8,128,128]{2,1,0:T(8,128)S(1)}) custom-call(s32[2]{0:T(128)S(1)} %pad_add_fusion.me, f32[8,8,16,128]{3,2,1,0:T(8,128)} %all-to-all-done.got, f32[288,128]{1,0:T(8,128)S(1)} %bitcast.13, bf16[4608,384]{1,0:T(8,128)(2,1)S(1)} %table.1), custom_call_target="tpu_custom_call" | custom-call | tf_op jit(solution)/shard_map/side/pallas_call | solution.py:37
  19.4 2.3 %collective-permute-start.1 = (f32[3,168,128]{2,1,0:T(8,128)S(1)}, f32[3,168,128]{2,1,0:T(8,128)S(1)}, u32[]{:S(2)}, u32[]{:S(2)}) collective-permute-start(f32[3,168,128]{2,1,0:T(8,128)S(1)} %get-tuple-element.19), channel_id=1, source_target_pairs={{8,16},{16,8},{24,32},{32,24},{40,48},{48,40},{56,64},{64,56},{72,... | collective-permute-start | bytes 774152 | tf_op jit(solution)/shard_map/ppermute | solution.py:288
  21.7 4.2 %collective-permute-start = (f32[3,168,128]{2,1,0:T(8,128)S(1)}, f32[3,168,128]{2,1,0:T(8,128)S(1)}, u32[]{:S(2)}, u32[]{:S(2)}) collective-permute-start(f32[3,168,128]{2,1,0:T(8,128)S(1)} %get-tuple-element.19), channel_id=1, source_target_pairs={{0,8},{8,0},{16,24},{24,16},{32,40},{40,32},{48,56},{56,48},{64,72... | collective-permute-start | bytes 774152 | tf_op jit(solution)/shard_map/ppermute | solution.py:288
  25.9 4.7 %plane.1.base = f32[3,128,128]{2,1,0:T(8,128)S(1)} custom-call(f32[8,128,128]{2,1,0:T(8,128)S(1)} %get-tuple-element.18.line, f32[5,40,128]{2,1,0:T(8,128)S(1)} %get-tuple-element.20.own, bf16[4608,384]{1,0:T(8,128)(2,1)S(1)} %table.1), custom_call_target="tpu_custom_call" | custom-call | flops 2717908992 | bytes 4194304 | tf_op jit(solution)/shard_map/plane/pallas_call | solution.py:37
  30.6 3.0 %collective-permute-done.1.side_b = f32[3,168,128]{2,1,0:T(8,128)S(1)} collective-permute-done((f32[3,168,128]{2,1,0:T(8,128)S(1)}, f32[3,168,128]{2,1,0:T(8,128)S(1)}, u32[]{:S(2)}, u32[]{:S(2)}) %collective-permute-start.1) | collective-permute-done | bytes 258080 | tf_op jit(solution)/shard_map/ppermute | solution.py:288
  33.6 0.0 collective-permute-done.side_a
  33.6 3.4 %first.1 = (f32[128,128]{1,0:T(8,128)S(1)}, f32[128,128]{1,0:T(8,128)S(1)}, f32[128,128]{1,0:T(8,128)S(1)}, f32[128,128]{1,0:T(8,128)S(1)}, f32[6,40,128]{2,1,0:T(8,128)S(1)}) custom-call(s32[2]{0:T(128)S(1)} %pad_add_fusion.me, f32[8,128,128]{2,1,0:T(8,128)S(1)} %get-tuple-element.18.line, f32[3,168,128]{2,1,0:T(8,128)S(1)} %collective-permute-done.side_a, ...), custom_call_target="tpu_custom_call" | custom-call | flops 1811939328 | bytes 4194304 | tf_op jit(solution)/shard_map/first/pallas_call | solution.py:37
  37.0 1.9 %collective-permute-start.2 = (f32[128,128]{1,0:T(8,128)S(1)}, f32[128,128]{1,0:T(8,128)S(1)}, u32[]{:S(2)}, u32[]{:S(2)}) collective-permute-start(f32[128,128]{1,0:T(8,128)S(1)} %get-tuple-element.22), channel_id=1, source_target_pairs={{0,8},{8,0},{16,24},{24,16},{32,40},{40,32},{48,56},{56,48},{64,72... | collective-permute-start | bytes 196616 | tf_op jit(solution)/shard_map/ppermute | solution.py:288
  38.9 2.9 %collective-permute-start.3 = (f32[128,128]{1,0:T(8,128)S(1)}, f32[128,128]{1,0:T(8,128)S(1)}, u32[]{:S(2)}, u32[]{:S(2)}) collective-permute-start(f32[128,128]{1,0:T(8,128)S(1)} %get-tuple-element.23), channel_id=1, source_target_pairs={{8,16},{16,8},{24,32},{32,24},{40,48},{48,40},{56,64},{64,56},{72,... | collective-permute-start | bytes 196616 | tf_op jit(solution)/shard_map/ppermute | solution.py:288
  41.9 4.6 %second.1.full = f32[128,128]{1,0:T(8,128)S(1)} custom-call(s32[2]{0:T(128)S(1)} %pad_add_fusion.me, f32[8,128,128]{2,1,0:T(8,128)S(1)} %get-tuple-element.18.line, f32[3,168,128]{2,1,0:T(8,128)S(1)} %collective-permute-done.side_a, f32[3,168,128]{2,1,0:T(8,128)S(1)} %collective-permute-done.1.side_b, f32[5,40,128]{2,1,0:T(8,128)S(1)} %get-tuple-element.20.own, ...), custom_call_target="tpu_custom_call" | custom-call | flops 2717908992 | bytes 4194304 | tf_op jit(solution)/shard_map/second/pallas_call | solution.py:37
  46.5 0.0 collective-permute-done.2.from_a
  46.5 2.2 %collective-permute-done.3.from_b = f32[128,128]{1,0:T(8,128)S(1)} collective-permute-done((f32[128,128]{1,0:T(8,128)S(1)}, f32[128,128]{1,0:T(8,128)S(1)}, u32[]{:S(2)}, u32[]{:S(2)}) %collective-permute-start.3) | collective-permute-done | bytes 65568 | tf_op jit(solution)/shard_map/ppermute | solution.py:288
  48.8 2.0 %third.1 = (f32[128,128]{1,0:T(8,128)S(1)}, f32[128,128]{1,0:T(8,128)S(1)}, f32[128,128]{1,0:T(8,128)S(1)}, f32[128,128]{1,0:T(8,128)S(1)}, f32[128,128]{1,0:T(8,128)S(1)}, /*index=5*/f32[128,128]{1,0:T(8,128)S(1)}) custom-call(s32[2]{0:T(128)S(1)} %pad_add_fusion.me, f32[128,128]{1,0:T(8,128)S(1)} %get-tuple-element.21.one, ...), custom_call_target="tpu_custom_call" | custom-call | flops 905969664 | bytes 4194304 | tf_op jit(solution)/shard_map/third/pallas_call | solution.py:37
  50.8 1.9 %collective-permute-start.4 = (f32[128,128]{1,0:T(8,128)S(1)}, f32[128,128]{1,0:T(8,128)S(1)}, u32[]{:S(2)}, u32[]{:S(2)}) collective-permute-start(f32[128,128]{1,0:T(8,128)S(1)} %get-tuple-element.28), channel_id=1, source_target_pairs={{0,8},{8,0},{16,24},{24,16},{32,40},{40,32},{48,56},{56,48},{64,72... | collective-permute-start | bytes 196616 | tf_op jit(solution)/shard_map/ppermute | solution.py:288
  52.7 4.8 %collective-permute-start.5 = (f32[128,128]{1,0:T(8,128)S(1)}, f32[128,128]{1,0:T(8,128)S(1)}, u32[]{:S(2)}, u32[]{:S(2)}) collective-permute-start(f32[128,128]{1,0:T(8,128)S(1)} %get-tuple-element.29), channel_id=1, source_target_pairs={{8,16},{16,8},{24,32},{32,24},{40,48},{48,40},{56,64},{64,56},{72,... | collective-permute-start | bytes 196616 | tf_op jit(solution)/shard_map/ppermute | solution.py:288
  57.5 0.0 collective-permute-done.4.from_a
  57.5 4.9 %collective-permute-done.5.from_b = f32[128,128]{1,0:T(8,128)S(1)} collective-permute-done((f32[128,128]{1,0:T(8,128)S(1)}, f32[128,128]{1,0:T(8,128)S(1)}, u32[]{:S(2)}, u32[]{:S(2)}) %collective-permute-start.5) | collective-permute-done | bytes 65568 | tf_op jit(solution)/shard_map/ppermute | solution.py:288
  62.5 11.0 %all_to_all.10.got = f32[8,4,16,128]{3,2,1,0:T(8,128)S(1)} all-to-all(f32[8,4,16,128]{3,2,1,0:T(8,128)S(1)} %back.1), channel_id=1, replica_groups=mesh['slab'=64,'chaos'=8] {'chaos'}, dimensions={0} | all-to-all | bytes 524288 | tf_op jit(solution)/shard_map/all_to_all | solution.py:375
  73.5 0.7 last.1
  (1 shorter events, 0.0 us)
Async XLA Ops:
  2.3 15.0 %all-to-all-start = ((f32[8,8,16,128]{3,2,1,0:T(8,128)}), f32[8,8,16,128]{3,2,1,0:T(8,128)}, u32[]{:S(2)}, u32[]{:S(2)}) async-start(f32[8,8,16,128]{3,2,1,0:T(8,128)} %pack.1), calls=%async_computation | async-start | bytes 1048576 | tf_op jit(solution)/shard_map/all_to_all | solution.py:313
  7.7 1.4 %copy-start.1 = (f32[48,15,12,15]{0,3,2,1:T(8,128)S(1)}, f32[48,15,12,15]{0,3,2,1:T(8,128)}, u32[]{:S(2)}) copy-start(f32[48,15,12,15]{0,3,2,1:T(8,128)} %param.10) | copy-start | bytes 1555204
  9.1 0.7 copy-start.2
  17.3 0.9 %copy-start = (f32[36,1,8,128]{3,2,1,0:T(8,128)S(1)}, f32[36,1,8,128]{3,2,1,0:T(8,128)}, u32[]{:S(2)}) copy-start(f32[36,1,8,128]{3,2,1,0:T(8,128)} %param.8) | copy-start | bytes 442372
  19.4 14.2 %collective-permute-start.1 = (f32[3,168,128]{2,1,0:T(8,128)S(1)}, f32[3,168,128]{2,1,0:T(8,128)S(1)}, u32[]{:S(2)}, u32[]{:S(2)}) collective-permute-start(f32[3,168,128]{2,1,0:T(8,128)S(1)} %get-tuple-element.19), channel_id=1, source_target_pairs={{8,16},{16,8},{24,32},{32,24},{40,48},{48,40},{56,64},{64,56},{72,... | collective-permute-start | bytes 774152 | tf_op jit(solution)/shard_map/ppermute | solution.py:288
  21.7 12.0 %collective-permute-start = (f32[3,168,128]{2,1,0:T(8,128)S(1)}, f32[3,168,128]{2,1,0:T(8,128)S(1)}, u32[]{:S(2)}, u32[]{:S(2)}) collective-permute-start(f32[3,168,128]{2,1,0:T(8,128)S(1)} %get-tuple-element.19), channel_id=1, source_target_pairs={{0,8},{8,0},{16,24},{24,16},{32,40},{40,32},{48,56},{56,48},{64,72... | collective-permute-start | bytes 774152 | tf_op jit(solution)/shard_map/ppermute | solution.py:288
  37.0 9.5 %collective-permute-start.2 = (f32[128,128]{1,0:T(8,128)S(1)}, f32[128,128]{1,0:T(8,128)S(1)}, u32[]{:S(2)}, u32[]{:S(2)}) collective-permute-start(f32[128,128]{1,0:T(8,128)S(1)} %get-tuple-element.22), channel_id=1, source_target_pairs={{0,8},{8,0},{16,24},{24,16},{32,40},{40,32},{48,56},{56,48},{64,72... | collective-permute-start | bytes 196616 | tf_op jit(solution)/shard_map/ppermute | solution.py:288
  38.9 9.8 %collective-permute-start.3 = (f32[128,128]{1,0:T(8,128)S(1)}, f32[128,128]{1,0:T(8,128)S(1)}, u32[]{:S(2)}, u32[]{:S(2)}) collective-permute-start(f32[128,128]{1,0:T(8,128)S(1)} %get-tuple-element.23), channel_id=1, source_target_pairs={{8,16},{16,8},{24,32},{32,24},{40,48},{48,40},{56,64},{64,56},{72,... | collective-permute-start | bytes 196616 | tf_op jit(solution)/shard_map/ppermute | solution.py:288
  50.8 6.8 %collective-permute-start.4 = (f32[128,128]{1,0:T(8,128)S(1)}, f32[128,128]{1,0:T(8,128)S(1)}, u32[]{:S(2)}, u32[]{:S(2)}) collective-permute-start(f32[128,128]{1,0:T(8,128)S(1)} %get-tuple-element.28), channel_id=1, source_target_pairs={{0,8},{8,0},{16,24},{24,16},{32,40},{40,32},{48,56},{56,48},{64,72... | collective-permute-start | bytes 196616 | tf_op jit(solution)/shard_map/ppermute | solution.py:288
  52.7 9.8 %collective-permute-start.5 = (f32[128,128]{1,0:T(8,128)S(1)}, f32[128,128]{1,0:T(8,128)S(1)}, u32[]{:S(2)}, u32[]{:S(2)}) collective-permute-start(f32[128,128]{1,0:T(8,128)S(1)} %get-tuple-element.29), channel_id=1, source_target_pairs={{8,16},{16,8},{24,32},{32,24},{40,48},{48,40},{56,64},{64,56},{72,... | collective-permute-start | bytes 196616 | tf_op jit(solution)/shard_map/ppermute | solution.py:288

commit v5 on v4

--- a/solution.py
+++ b/solution.py
@@ -285,7 +285,8 @@
     pairs_b = [(i, ((i + 1) ^ 1) - 1) for i in range(1, slabs) if ((i + 1) ^ 1) - 1 < slabs]
 
     def swap(a, b):
-        return lax.ppermute(a, "slab", pairs_a), lax.ppermute(b, "slab", pairs_b)
+        b = lax.ppermute(b, "slab", pairs_b)
+        return lax.ppermute(a, "slab", pairs_a), b
 
     def grads(tiles):
         return pltpu.VMEM((tiles, 3 * ROWS, 2 * NX), bf16)
@@ -363,14 +364,14 @@
         third_kernel,
         "third",
         (flat,) * 6,
-        (me, one, from_a, from_b, full, line, six, table),
+        (me, one, from_b, from_a, full, line, six, table),
         scratch=[single],
         specs=[SM] + [VM] * 7,
         cost=tile_flops,
     )
     from_a, from_b = swap(to_a, to_b)
     send = call(
-        back_kernel, "back", struct(NB, 4, MP, NX), (mid, rest, from_a, from_b, y_up, y_down)
+        back_kernel, "back", struct(NB, 4, MP, NX), (mid, rest, from_b, from_a, y_up, y_down)
     )
     got = lax.all_to_all(send, "chaos", 0, 0, tiled=True)
     out, residual = call(

time: 74.7 us -> 72 us (0.964)
  waiting for transfers between devices: 11.4 us -> 6.66 us
  starting transfers between devices: 23.4 us -> 25.1 us
    ppermute x6, waiting for transfers between devices: 10.1 us -> 5.38 us  [the longest x3 5.37 us: swap(): b = lax.ppermute(b, 'slab', pairs_b)]
    ppermute x6, starting transfers between devices: 18.1 us -> 19.7 us  [the longest x3 11.5 us: swap(): b = lax.ppermute(b, 'slab', pairs_b)]
  transfers between devices with their start and end apart: 7 -> 7, of which waited for: 4 -> 4; matrix products, arithmetic and copies ran while one was open for 0% -> 0% of each run, Pallas kernels for 21% -> 22%
where the time goes in v5:
time: 72 us; the launch traced here: 71.4 us
  starting transfers between devices  25.1 us (35%)
  Pallas kernels  24.6 us (34%)
  blocking collectives  11.4 us (16%)
  waiting for transfers between devices  6.66 us (9%)
  local copies, waits for them, and re-layouts  2.96 us (4%)
  between operations  0.72 us (1%)
    pallas_call x9, Pallas kernels, call(): pl.pallas_call(kernel, out_shape=outs, in_specs=specs or [VM] * len(ins),...  24.6 us
    ppermute x3, starting transfers between devices, swap(): b = lax.ppermute(b, 'slab', pairs_b)  11.5 us
    all_to_all x1, blocking collectives, body(): got = lax.all_to_all(send, 'chaos', 0, 0, tiled=True)  11.4 us
    ppermute x3, starting transfers between devices, swap(): return (lax.ppermute(a, 'slab', pairs_a), b)  8.27 us
    ppermute x3, waiting for transfers between devices, swap(): b = lax.ppermute(b, 'slab', pairs_b)  5.37 us
    all_to_all x1, starting transfers between devices, body(): got = lax.all_to_all(send, 'chaos', 0, 0, tiled=True)  5.32 us
    unnamed x6, local copies, waits for them, and re-layouts  2.96 us
  transfers between devices with their start and end apart: 7, of which 4 were waited for; matrix products, arithmetic and copies ran while one was open for 0% of the time, Pallas kernels for 22%

profile of v5, /device:TPU:256, one launch (start us, length us, event | category | flops | bytes accessed | tf_op | source)
XLA Modules:
  0.0 71.4 jit_solution(4094971742344517300)
XLA Ops:
  0.6 1.7 %pack.1 = f32[8,8,16,128]{3,2,1,0:T(8,128)} custom-call(f32[120,128]{1,0:T(8,128)} %bitcast.16, f32[120,128]{1,0:T(8,128)} %bitcast.17), custom_call_target="tpu_custom_call" | custom-call | tf_op jit(solution)/shard_map/pack/pallas_call | solution.py:37
  2.3 5.3 %all-to-all-start = ((f32[8,8,16,128]{3,2,1,0:T(8,128)}), f32[8,8,16,128]{3,2,1,0:T(8,128)}, u32[]{:S(2)}, u32[]{:S(2)}) async-start(f32[8,8,16,128]{3,2,1,0:T(8,128)} %pack.1), calls=%async_computation | async-start | bytes 1048576 | tf_op jit(solution)/shard_map/all_to_all | solution.py:314
  7.7 0.1 pad_add_fusion.me
  7.7 0.0 copy-start.1
  7.7 1.4 %copy-done.1 = f32[48,15,12,15]{0,3,2,1:T(8,128)S(1)} copy-done((f32[48,15,12,15]{0,3,2,1:T(8,128)S(1)}, f32[48,15,12,15]{0,3,2,1:T(8,128)}, u32[]{:S(2)}) %copy-start.1) | copy-done | bytes 518424
  9.1 0.0 copy-start.2
  9.1 0.7 copy-done.2
  9.8 6.3 %table.1 = bf16[4608,384]{1,0:T(8,128)(2,1)S(1)} custom-call(s32[3,48]{1,0:T(4,128)S(1)} %bitcast.15, f32[15,12,15,48]{3,2,1,0:T(8,128)S(1)} %bitcast.14), custom_call_target="tpu_custom_call" | custom-call | flops 5435817984 | bytes 4194304 | tf_op jit(solution)/shard_map/table/pallas_call | solution.py:37
  16.1 1.3 %all-to-all-done.got = f32[8,8,16,128]{3,2,1,0:T(8,128)} async-done(((f32[8,8,16,128]{3,2,1,0:T(8,128)}), f32[8,8,16,128]{3,2,1,0:T(8,128)}, u32[]{:S(2)}, u32[]{:S(2)}) %all-to-all-start) | async-done | bytes 524320 | tf_op jit(solution)/shard_map/all_to_all | solution.py:314
  17.3 0.0 copy-start
  17.3 0.9 %copy-done = f32[36,1,8,128]{3,2,1,0:T(8,128)S(1)} copy-done((f32[36,1,8,128]{3,2,1,0:T(8,128)S(1)}, f32[36,1,8,128]{3,2,1,0:T(8,128)}, u32[]{:S(2)}) %copy-start) | copy-done | bytes 147480
  18.3 1.1 %side.1 = (f32[3,168,128]{2,1,0:T(8,128)S(1)}, f32[5,40,128]{2,1,0:T(8,128)S(1)}, f32[8,128,128]{2,1,0:T(8,128)S(1)}) custom-call(s32[2]{0:T(128)S(1)} %pad_add_fusion.me, f32[8,8,16,128]{3,2,1,0:T(8,128)} %all-to-all-done.got, f32[288,128]{1,0:T(8,128)S(1)} %bitcast.13, bf16[4608,384]{1,0:T(8,128)(2,1)S(1)} %table.1), custom_call_target="tpu_custom_call" | custom-call | tf_op jit(solution)/shard_map/side/pallas_call | solution.py:37
  19.4 2.3 %collective-permute-start.1 = (f32[3,168,128]{2,1,0:T(8,128)S(1)}, f32[3,168,128]{2,1,0:T(8,128)S(1)}, u32[]{:S(2)}, u32[]{:S(2)}) collective-permute-start(f32[3,168,128]{2,1,0:T(8,128)S(1)} %get-tuple-element.19), channel_id=1, source_target_pairs={{8,16},{16,8},{24,32},{32,24},{40,48},{48,40},{56,64},{64,56},{72,... | collective-permute-start | bytes 774152 | tf_op jit(solution)/shard_map/ppermute | solution.py:288
  21.6 4.2 %collective-permute-start = (f32[3,168,128]{2,1,0:T(8,128)S(1)}, f32[3,168,128]{2,1,0:T(8,128)S(1)}, u32[]{:S(2)}, u32[]{:S(2)}) collective-permute-start(f32[3,168,128]{2,1,0:T(8,128)S(1)} %get-tuple-element.19), channel_id=1, source_target_pairs={{0,8},{8,0},{16,24},{24,16},{32,40},{40,32},{48,56},{56,48},{64,72... | collective-permute-start | bytes 774152 | tf_op jit(solution)/shard_map/ppermute | solution.py:289
  25.9 4.7 %plane.1.base = f32[3,128,128]{2,1,0:T(8,128)S(1)} custom-call(f32[8,128,128]{2,1,0:T(8,128)S(1)} %get-tuple-element.18.line, f32[5,40,128]{2,1,0:T(8,128)S(1)} %get-tuple-element.20.own, bf16[4608,384]{1,0:T(8,128)(2,1)S(1)} %table.1), custom_call_target="tpu_custom_call" | custom-call | flops 2717908992 | bytes 4194304 | tf_op jit(solution)/shard_map/plane/pallas_call | solution.py:37
  30.6 3.0 %collective-permute-done.1.side_b = f32[3,168,128]{2,1,0:T(8,128)S(1)} collective-permute-done((f32[3,168,128]{2,1,0:T(8,128)S(1)}, f32[3,168,128]{2,1,0:T(8,128)S(1)}, u32[]{:S(2)}, u32[]{:S(2)}) %collective-permute-start.1) | collective-permute-done | bytes 258080 | tf_op jit(solution)/shard_map/ppermute | solution.py:288
  33.6 0.0 collective-permute-done.side_a
  33.6 3.4 %first.1 = (f32[128,128]{1,0:T(8,128)S(1)}, f32[128,128]{1,0:T(8,128)S(1)}, f32[128,128]{1,0:T(8,128)S(1)}, f32[128,128]{1,0:T(8,128)S(1)}, f32[6,40,128]{2,1,0:T(8,128)S(1)}) custom-call(s32[2]{0:T(128)S(1)} %pad_add_fusion.me, f32[8,128,128]{2,1,0:T(8,128)S(1)} %get-tuple-element.18.line, f32[3,168,128]{2,1,0:T(8,128)S(1)} %collective-permute-done.side_a, ...), custom_call_target="tpu_custom_call" | custom-call | flops 1811939328 | bytes 4194304 | tf_op jit(solution)/shard_map/first/pallas_call | solution.py:37
  37.0 2.4 %collective-permute-start.2 = (f32[128,128]{1,0:T(8,128)S(1)}, f32[128,128]{1,0:T(8,128)S(1)}, u32[]{:S(2)}, u32[]{:S(2)}) collective-permute-start(f32[128,128]{1,0:T(8,128)S(1)} %get-tuple-element.22), channel_id=1, source_target_pairs={{8,16},{16,8},{24,32},{32,24},{40,48},{48,40},{56,64},{64,56},{72,... | collective-permute-start | bytes 196616 | tf_op jit(solution)/shard_map/ppermute | solution.py:288
  39.4 2.1 %collective-permute-start.3 = (f32[128,128]{1,0:T(8,128)S(1)}, f32[128,128]{1,0:T(8,128)S(1)}, u32[]{:S(2)}, u32[]{:S(2)}) collective-permute-start(f32[128,128]{1,0:T(8,128)S(1)} %get-tuple-element.23), channel_id=1, source_target_pairs={{0,8},{8,0},{16,24},{24,16},{32,40},{40,32},{48,56},{56,48},{64,72... | collective-permute-start | bytes 196616 | tf_op jit(solution)/shard_map/ppermute | solution.py:289
  41.6 4.6 %second.1.full = f32[128,128]{1,0:T(8,128)S(1)} custom-call(s32[2]{0:T(128)S(1)} %pad_add_fusion.me, f32[8,128,128]{2,1,0:T(8,128)S(1)} %get-tuple-element.18.line, f32[3,168,128]{2,1,0:T(8,128)S(1)} %collective-permute-done.side_a, f32[3,168,128]{2,1,0:T(8,128)S(1)} %collective-permute-done.1.side_b, f32[5,40,128]{2,1,0:T(8,128)S(1)} %get-tuple-element.20.own, ...), custom_call_target="tpu_custom_call" | custom-call | flops 2717908992 | bytes 4194304 | tf_op jit(solution)/shard_map/second/pallas_call | solution.py:37
  46.2 0.6 collective-permute-done.2.from_a
  46.8 0.0 collective-permute-done.3.from_b
  46.8 2.0 %third.1 = (f32[128,128]{1,0:T(8,128)S(1)}, f32[128,128]{1,0:T(8,128)S(1)}, f32[128,128]{1,0:T(8,128)S(1)}, f32[128,128]{1,0:T(8,128)S(1)}, f32[128,128]{1,0:T(8,128)S(1)}, /*index=5*/f32[128,128]{1,0:T(8,128)S(1)}) custom-call(s32[2]{0:T(128)S(1)} %pad_add_fusion.me, f32[128,128]{1,0:T(8,128)S(1)} %get-tuple-element.21.one, ...), custom_call_target="tpu_custom_call" | custom-call | flops 905969664 | bytes 4194304 | tf_op jit(solution)/shard_map/third/pallas_call | solution.py:37
  48.8 6.8 %collective-permute-start.4 = (f32[128,128]{1,0:T(8,128)S(1)}, f32[128,128]{1,0:T(8,128)S(1)}, u32[]{:S(2)}, u32[]{:S(2)}) collective-permute-start(f32[128,128]{1,0:T(8,128)S(1)} %get-tuple-element.28), channel_id=1, source_target_pairs={{8,16},{16,8},{24,32},{32,24},{40,48},{48,40},{56,64},{64,56},{72,... | collective-permute-start | bytes 196616 | tf_op jit(solution)/shard_map/ppermute | solution.py:288
  55.6 1.9 %collective-permute-start.5 = (f32[128,128]{1,0:T(8,128)S(1)}, f32[128,128]{1,0:T(8,128)S(1)}, u32[]{:S(2)}, u32[]{:S(2)}) collective-permute-start(f32[128,128]{1,0:T(8,128)S(1)} %get-tuple-element.29), channel_id=1, source_target_pairs={{0,8},{8,0},{16,24},{24,16},{32,40},{40,32},{48,56},{56,48},{64,72... | collective-permute-start | bytes 196616 | tf_op jit(solution)/shard_map/ppermute | solution.py:289
  57.5 1.8 %collective-permute-done.4.from_a = f32[128,128]{1,0:T(8,128)S(1)} collective-permute-done((f32[128,128]{1,0:T(8,128)S(1)}, f32[128,128]{1,0:T(8,128)S(1)}, u32[]{:S(2)}, u32[]{:S(2)}) %collective-permute-start.4) | collective-permute-done | bytes 65568 | tf_op jit(solution)/shard_map/ppermute | solution.py:288
  59.3 0.0 collective-permute-done.5.from_b
  59.4 11.4 %all_to_all.10.got = f32[8,4,16,128]{3,2,1,0:T(8,128)S(1)} all-to-all(f32[8,4,16,128]{3,2,1,0:T(8,128)S(1)} %back.1), channel_id=1, replica_groups=mesh['slab'=64,'chaos'=8] {'chaos'}, dimensions={0} | all-to-all | bytes 524288 | tf_op jit(solution)/shard_map/all_to_all | solution.py:376
  70.8 0.7 last.1
  (1 shorter events, 0.0 us)
Async XLA Ops:
  2.3 15.0 %all-to-all-start = ((f32[8,8,16,128]{3,2,1,0:T(8,128)}), f32[8,8,16,128]{3,2,1,0:T(8,128)}, u32[]{:S(2)}, u32[]{:S(2)}) async-start(f32[8,8,16,128]{3,2,1,0:T(8,128)} %pack.1), calls=%async_computation | async-start | bytes 1048576 | tf_op jit(solution)/shard_map/all_to_all | solution.py:314
  7.7 1.4 %copy-start.1 = (f32[48,15,12,15]{0,3,2,1:T(8,128)S(1)}, f32[48,15,12,15]{0,3,2,1:T(8,128)}, u32[]{:S(2)}) copy-start(f32[48,15,12,15]{0,3,2,1:T(8,128)} %param.10) | copy-start | bytes 1555204
  9.1 0.7 copy-start.2
  17.3 0.9 %copy-start = (f32[36,1,8,128]{3,2,1,0:T(8,128)S(1)}, f32[36,1,8,128]{3,2,1,0:T(8,128)}, u32[]{:S(2)}) copy-start(f32[36,1,8,128]{3,2,1,0:T(8,128)} %param.8) | copy-start | bytes 442372
  19.4 14.2 %collective-permute-start.1 = (f32[3,168,128]{2,1,0:T(8,128)S(1)}, f32[3,168,128]{2,1,0:T(8,128)S(1)}, u32[]{:S(2)}, u32[]{:S(2)}) collective-permute-start(f32[3,168,128]{2,1,0:T(8,128)S(1)} %get-tuple-element.19), channel_id=1, source_target_pairs={{8,16},{16,8},{24,32},{32,24},{40,48},{48,40},{56,64},{64,56},{72,... | collective-permute-start | bytes 774152 | tf_op jit(solution)/shard_map/ppermute | solution.py:288
  21.6 12.0 %collective-permute-start = (f32[3,168,128]{2,1,0:T(8,128)S(1)}, f32[3,168,128]{2,1,0:T(8,128)S(1)}, u32[]{:S(2)}, u32[]{:S(2)}) collective-permute-start(f32[3,168,128]{2,1,0:T(8,128)S(1)} %get-tuple-element.19), channel_id=1, source_target_pairs={{0,8},{8,0},{16,24},{24,16},{32,40},{40,32},{48,56},{56,48},{64,72... | collective-permute-start | bytes 774152 | tf_op jit(solution)/shard_map/ppermute | solution.py:289
  37.0 9.8 %collective-permute-start.2 = (f32[128,128]{1,0:T(8,128)S(1)}, f32[128,128]{1,0:T(8,128)S(1)}, u32[]{:S(2)}, u32[]{:S(2)}) collective-permute-start(f32[128,128]{1,0:T(8,128)S(1)} %get-tuple-element.22), channel_id=1, source_target_pairs={{8,16},{16,8},{24,32},{32,24},{40,48},{48,40},{56,64},{64,56},{72,... | collective-permute-start | bytes 196616 | tf_op jit(solution)/shard_map/ppermute | solution.py:288
  39.4 7.4 %collective-permute-start.3 = (f32[128,128]{1,0:T(8,128)S(1)}, f32[128,128]{1,0:T(8,128)S(1)}, u32[]{:S(2)}, u32[]{:S(2)}) collective-permute-start(f32[128,128]{1,0:T(8,128)S(1)} %get-tuple-element.23), channel_id=1, source_target_pairs={{0,8},{8,0},{16,24},{24,16},{32,40},{40,32},{48,56},{56,48},{64,72... | collective-permute-start | bytes 196616 | tf_op jit(solution)/shard_map/ppermute | solution.py:289
  48.8 10.5 %collective-permute-start.4 = (f32[128,128]{1,0:T(8,128)S(1)}, f32[128,128]{1,0:T(8,128)S(1)}, u32[]{:S(2)}, u32[]{:S(2)}) collective-permute-start(f32[128,128]{1,0:T(8,128)S(1)} %get-tuple-element.28), channel_id=1, source_target_pairs={{8,16},{16,8},{24,32},{32,24},{40,48},{48,40},{56,64},{64,56},{72,... | collective-permute-start | bytes 196616 | tf_op jit(solution)/shard_map/ppermute | solution.py:288
  55.6 3.7 %collective-permute-start.5 = (f32[128,128]{1,0:T(8,128)S(1)}, f32[128,128]{1,0:T(8,128)S(1)}, u32[]{:S(2)}, u32[]{:S(2)}) collective-permute-start(f32[128,128]{1,0:T(8,128)S(1)} %get-tuple-element.29), channel_id=1, source_target_pairs={{0,8},{8,0},{16,24},{24,16},{32,40},{40,32},{48,56},{56,48},{64,72... | collective-permute-start | bytes 196616 | tf_op jit(solution)/shard_map/ppermute | solution.py:289

commit v6 on v5

--- a/solution.py
+++ b/solution.py
@@ -250,15 +250,22 @@
     full[...] = rest[...] + (y[:, :NX] + y[:, NX:])
 
 
-def third_kernel(
-    me, one, from_a, from_b, full, line, six, table, mid, first_out, second_out, y_up, y_down, rest, single
-):
+def third_kernel(me, one, from_a, from_b, full, six, table, mid, first_out, second_out, single):
     odd = me[1] == 1
     v = one[...] + RELAX * (full[...] + (from_a[...] + from_b[...]))
     mid[...] = v
-    y_up[...], y_down[...], rest[...] = row_sums(
-        odd, v, line[6], table, single, six, first_out, second_out
-    )
+    put_columns(single, 0, [v])
+    zp, zm = sums(table, single, 0, NX, six, (4, 5))
+    first_out[...] = jnp.where(odd, zm, zp)
+    second_out[...] = jnp.where(odd, zp, zm)
+
+
+def fourth_kernel(mid, to_a, to_b, line, six, table, y_up, y_down, rest, single):
+    put_columns(single, 0, [mid[...]])
+    xp, xm, yp, ym = sums(table, single, 0, NX, six, (0, 1, 2, 3))
+    y_up[...] = yp
+    y_down[...] = ym
+    rest[...] = line[6] - along_x(xp, xm) - ((yp + ym) + (to_a[...] + to_b[...]))
 
 
 def back_kernel(mid, rest, from_a, from_b, y_up, y_down, send):
@@ -360,16 +367,24 @@
         specs=[SM] + [VM] * 7,
         cost=3 * tile_flops,
     )
-    mid, to_a, to_b, y_up, y_down, rest = call(
+    mid, to_a, to_b = call(
         third_kernel,
         "third",
-        (flat,) * 6,
-        (me, one, from_b, from_a, full, line, six, table),
+        (flat,) * 3,
+        (me, one, from_b, from_a, full, six, table),
         scratch=[single],
-        specs=[SM] + [VM] * 7,
+        specs=[SM] + [VM] * 6,
         cost=tile_flops,
     )
     from_a, from_b = swap(to_a, to_b)
+    y_up, y_down, rest = call(
+        fourth_kernel,
+        "fourth",
+        (flat,) * 3,
+        (mid, to_b, to_a, line, six, table),
+        scratch=[single],
+        cost=tile_flops,
+    )
     send = call(
         back_kernel, "back", struct(NB, 4, MP, NX), (mid, rest, from_b, from_a, y_up, y_down)
     )

time: 72 us -> 71.5 us (level)
  waiting for transfers between devices: 6.66 us -> 5.74 us
    ppermute x3, waiting for transfers between devices: 5.37 us -> 4.46 us  [swap(): b = lax.ppermute(b, 'slab', pairs_b)]
    pallas_call x9 -> x10, Pallas kernels: 24.6 us -> 25 us  [call(): pl.pallas_call(kernel, out_shape=outs, in_specs=specs or [VM] * len(ins),...]
  transfers between devices with their start and end apart: 7 -> 7, of which waited for: 4 -> 4; matrix products, arithmetic and copies ran while one was open for 0% -> 0% of each run, Pallas kernels for 22% -> 23%
where the time goes in v6:
time: 71.5 us; the launch traced here: 70.9 us
  Pallas kernels  25 us (35%)
  starting transfers between devices  25 us (35%)
  blocking collectives  11.4 us (16%)
  waiting for transfers between devices  5.74 us (8%)
  local copies, waits for them, and re-layouts  2.96 us (4%)
  between operations  0.74 us (1%)
    pallas_call x10, Pallas kernels, call(): pl.pallas_call(kernel, out_shape=outs, in_specs=specs or [VM] * len(ins),...  25 us
    ppermute x3, starting transfers between devices, swap(): b = lax.ppermute(b, 'slab', pairs_b)  11.4 us
    all_to_all x1, blocking collectives, body(): got = lax.all_to_all(send, 'chaos', 0, 0, tiled=True)  11.4 us
    ppermute x3, starting transfers between devices, swap(): return (lax.ppermute(a, 'slab', pairs_a), b)  8.27 us
    all_to_all x1, starting transfers between devices, body(): got = lax.all_to_all(send, 'chaos', 0, 0, tiled=True)  5.32 us
    ppermute x3, waiting for transfers between devices, swap(): b = lax.ppermute(b, 'slab', pairs_b)  4.46 us
    unnamed x6, local copies, waits for them, and re-layouts  2.96 us
  transfers between devices with their start and end apart: 7, of which 4 were waited for; matrix products, arithmetic and copies ran while one was open for 0% of the time, Pallas kernels for 23%

profile of v6, /device:TPU:256, one launch (start us, length us, event | category | flops | bytes accessed | tf_op | source)
XLA Modules:
  0.0 70.9 jit_solution(5308561601233393719)
XLA Ops:
  0.6 1.7 %pack.1 = f32[8,8,16,128]{3,2,1,0:T(8,128)} custom-call(f32[120,128]{1,0:T(8,128)} %bitcast.16, f32[120,128]{1,0:T(8,128)} %bitcast.17), custom_call_target="tpu_custom_call" | custom-call | tf_op jit(solution)/shard_map/pack/pallas_call | solution.py:37
  2.3 5.3 %all-to-all-start = ((f32[8,8,16,128]{3,2,1,0:T(8,128)}), f32[8,8,16,128]{3,2,1,0:T(8,128)}, u32[]{:S(2)}, u32[]{:S(2)}) async-start(f32[8,8,16,128]{3,2,1,0:T(8,128)} %pack.1), calls=%async_computation | async-start | bytes 1048576 | tf_op jit(solution)/shard_map/all_to_all | solution.py:321
  7.7 0.1 pad_add_fusion.me
  7.7 0.0 copy-start.1
  7.7 1.4 %copy-done.1 = f32[48,15,12,15]{0,3,2,1:T(8,128)S(1)} copy-done((f32[48,15,12,15]{0,3,2,1:T(8,128)S(1)}, f32[48,15,12,15]{0,3,2,1:T(8,128)}, u32[]{:S(2)}) %copy-start.1) | copy-done | bytes 518424
  9.1 0.0 copy-start.2
  9.1 0.7 copy-done.2
  9.8 6.3 %table.1 = bf16[4608,384]{1,0:T(8,128)(2,1)S(1)} custom-call(s32[3,48]{1,0:T(4,128)S(1)} %bitcast.15, f32[15,12,15,48]{3,2,1,0:T(8,128)S(1)} %bitcast.14), custom_call_target="tpu_custom_call" | custom-call | flops 5435817984 | bytes 4194304 | tf_op jit(solution)/shard_map/table/pallas_call | solution.py:37
  16.1 1.3 %all-to-all-done.got = f32[8,8,16,128]{3,2,1,0:T(8,128)} async-done(((f32[8,8,16,128]{3,2,1,0:T(8,128)}), f32[8,8,16,128]{3,2,1,0:T(8,128)}, u32[]{:S(2)}, u32[]{:S(2)}) %all-to-all-start) | async-done | bytes 524320 | tf_op jit(solution)/shard_map/all_to_all | solution.py:321
  17.3 0.0 copy-start
  17.3 0.9 %copy-done = f32[36,1,8,128]{3,2,1,0:T(8,128)S(1)} copy-done((f32[36,1,8,128]{3,2,1,0:T(8,128)S(1)}, f32[36,1,8,128]{3,2,1,0:T(8,128)}, u32[]{:S(2)}) %copy-start) | copy-done | bytes 147480
  18.2 1.1 %side.1 = (f32[3,168,128]{2,1,0:T(8,128)S(1)}, f32[5,40,128]{2,1,0:T(8,128)S(1)}, f32[8,128,128]{2,1,0:T(8,128)S(1)}) custom-call(s32[2]{0:T(128)S(1)} %pad_add_fusion.me, f32[8,8,16,128]{3,2,1,0:T(8,128)} %all-to-all-done.got, f32[288,128]{1,0:T(8,128)S(1)} %bitcast.13, bf16[4608,384]{1,0:T(8,128)(2,1)S(1)} %table.1), custom_call_target="tpu_custom_call" | custom-call | tf_op jit(solution)/shard_map/side/pallas_call | solution.py:37
  19.4 2.3 %collective-permute-start.1 = (f32[3,168,128]{2,1,0:T(8,128)S(1)}, f32[3,168,128]{2,1,0:T(8,128)S(1)}, u32[]{:S(2)}, u32[]{:S(2)}) collective-permute-start(f32[3,168,128]{2,1,0:T(8,128)S(1)} %get-tuple-element.19), channel_id=1, source_target_pairs={{8,16},{16,8},{24,32},{32,24},{40,48},{48,40},{56,64},{64,56},{72,... | collective-permute-start | bytes 774152 | tf_op jit(solution)/shard_map/ppermute | solution.py:295
  21.6 4.3 %collective-permute-start = (f32[3,168,128]{2,1,0:T(8,128)S(1)}, f32[3,168,128]{2,1,0:T(8,128)S(1)}, u32[]{:S(2)}, u32[]{:S(2)}) collective-permute-start(f32[3,168,128]{2,1,0:T(8,128)S(1)} %get-tuple-element.19), channel_id=1, source_target_pairs={{0,8},{8,0},{16,24},{24,16},{32,40},{40,32},{48,56},{56,48},{64,72... | collective-permute-start | bytes 774152 | tf_op jit(solution)/shard_map/ppermute | solution.py:296
  25.9 4.5 %plane.1.base = f32[3,128,128]{2,1,0:T(8,128)S(1)} custom-call(f32[8,128,128]{2,1,0:T(8,128)S(1)} %get-tuple-element.18.line, f32[5,40,128]{2,1,0:T(8,128)S(1)} %get-tuple-element.20.own, bf16[4608,384]{1,0:T(8,128)(2,1)S(1)} %table.1), custom_call_target="tpu_custom_call" | custom-call | flops 2717908992 | bytes 4194304 | tf_op jit(solution)/shard_map/plane/pallas_call | solution.py:37
  30.4 3.2 %collective-permute-done.1.side_b = f32[3,168,128]{2,1,0:T(8,128)S(1)} collective-permute-done((f32[3,168,128]{2,1,0:T(8,128)S(1)}, f32[3,168,128]{2,1,0:T(8,128)S(1)}, u32[]{:S(2)}, u32[]{:S(2)}) %collective-permute-start.1) | collective-permute-done | bytes 258080 | tf_op jit(solution)/shard_map/ppermute | solution.py:295
  33.6 0.0 collective-permute-done.side_a
  33.6 3.3 %first.1 = (f32[128,128]{1,0:T(8,128)S(1)}, f32[128,128]{1,0:T(8,128)S(1)}, f32[128,128]{1,0:T(8,128)S(1)}, f32[128,128]{1,0:T(8,128)S(1)}, f32[6,40,128]{2,1,0:T(8,128)S(1)}) custom-call(s32[2]{0:T(128)S(1)} %pad_add_fusion.me, f32[8,128,128]{2,1,0:T(8,128)S(1)} %get-tuple-element.18.line, f32[3,168,128]{2,1,0:T(8,128)S(1)} %collective-permute-done.side_a, ...), custom_call_target="tpu_custom_call" | custom-call | flops 1811939328 | bytes 4194304 | tf_op jit(solution)/shard_map/first/pallas_call | solution.py:37
  36.9 2.4 %collective-permute-start.2 = (f32[128,128]{1,0:T(8,128)S(1)}, f32[128,128]{1,0:T(8,128)S(1)}, u32[]{:S(2)}, u32[]{:S(2)}) collective-permute-start(f32[128,128]{1,0:T(8,128)S(1)} %get-tuple-element.22), channel_id=1, source_target_pairs={{8,16},{16,8},{24,32},{32,24},{40,48},{48,40},{56,64},{64,56},{72,... | collective-permute-start | bytes 196616 | tf_op jit(solution)/shard_map/ppermute | solution.py:295
  39.3 2.1 %collective-permute-start.3 = (f32[128,128]{1,0:T(8,128)S(1)}, f32[128,128]{1,0:T(8,128)S(1)}, u32[]{:S(2)}, u32[]{:S(2)}) collective-permute-start(f32[128,128]{1,0:T(8,128)S(1)} %get-tuple-element.23), channel_id=1, source_target_pairs={{0,8},{8,0},{16,24},{24,16},{32,40},{40,32},{48,56},{56,48},{64,72... | collective-permute-start | bytes 196616 | tf_op jit(solution)/shard_map/ppermute | solution.py:296
  41.5 4.6 %second.1.full = f32[128,128]{1,0:T(8,128)S(1)} custom-call(s32[2]{0:T(128)S(1)} %pad_add_fusion.me, f32[8,128,128]{2,1,0:T(8,128)S(1)} %get-tuple-element.18.line, f32[3,168,128]{2,1,0:T(8,128)S(1)} %collective-permute-done.side_a, f32[3,168,128]{2,1,0:T(8,128)S(1)} %collective-permute-done.1.side_b, f32[5,40,128]{2,1,0:T(8,128)S(1)} %get-tuple-element.20.own, ...), custom_call_target="tpu_custom_call" | custom-call | flops 2717908992 | bytes 4194304 | tf_op jit(solution)/shard_map/second/pallas_call | solution.py:37
  46.1 0.6 collective-permute-done.2.from_a
  46.7 0.0 collective-permute-done.3.from_b
  46.7 1.6 %third.1 = (f32[128,128]{1,0:T(8,128)S(1)}, f32[128,128]{1,0:T(8,128)S(1)}, f32[128,128]{1,0:T(8,128)S(1)}) custom-call(s32[2]{0:T(128)S(1)} %pad_add_fusion.me, f32[128,128]{1,0:T(8,128)S(1)} %get-tuple-element.21.one, f32[128,128]{1,0:T(8,128)S(1)} %collective-permute-done.2.from_a, f32[128,128]{1,0:T(8,128)S(1)} %collective-permute-done.3.from_b, ...), custom_call_target="tpu_custom_call" | custom-call | flops 905969664 | bytes 4194304 | tf_op jit(solution)/shard_map/third/pallas_call | solution.py:37
  48.4 6.7 %collective-permute-start.4 = (f32[128,128]{1,0:T(8,128)S(1)}, f32[128,128]{1,0:T(8,128)S(1)}, u32[]{:S(2)}, u32[]{:S(2)}) collective-permute-start(f32[128,128]{1,0:T(8,128)S(1)} %get-tuple-element.27.to_a), channel_id=1, source_target_pairs={{8,16},{16,8},{24,32},{32,24},{40,48},{48,40},{56,64},{64,56},{72,... | collective-permute-start | bytes 196616 | tf_op jit(solution)/shard_map/ppermute | solution.py:295
  55.1 1.9 %collective-permute-start.5 = (f32[128,128]{1,0:T(8,128)S(1)}, f32[128,128]{1,0:T(8,128)S(1)}, u32[]{:S(2)}, u32[]{:S(2)}) collective-permute-start(f32[128,128]{1,0:T(8,128)S(1)} %get-tuple-element.28.to_b), channel_id=1, source_target_pairs={{0,8},{8,0},{16,24},{24,16},{32,40},{40,32},{48,56},{56,48},{64,72... | collective-permute-start | bytes 196616 | tf_op jit(solution)/shard_map/ppermute | solution.py:296
  57.0 1.2 %fourth.1 = (f32[128,128]{1,0:T(8,128)S(1)}, f32[128,128]{1,0:T(8,128)S(1)}, f32[128,128]{1,0:T(8,128)S(1)}) custom-call(f32[128,128]{1,0:T(8,128)S(1)} %get-tuple-element.26.mid, f32[128,128]{1,0:T(8,128)S(1)} %get-tuple-element.27.to_a, f32[128,128]{1,0:T(8,128)S(1)} %get-tuple-element.28.to_b, f32[8,128,128]{2,1,0:T(8,128)S(1)} %get-tuple-element.18.line, ...), custom_call_target="tpu_custom_call" | custom-call | flops 905969664 | bytes 4194304 | tf_op jit(solution)/shard_map/fourth/pallas_call | solution.py:37
  58.2 0.6 collective-permute-done.4.from_a
  58.8 0.0 collective-permute-done.5.from_b
  58.9 11.4 %all_to_all.10.got = f32[8,4,16,128]{3,2,1,0:T(8,128)S(1)} all-to-all(f32[8,4,16,128]{3,2,1,0:T(8,128)S(1)} %back.1), channel_id=1, replica_groups=mesh['slab'=64,'chaos'=8] {'chaos'}, dimensions={0} | all-to-all | bytes 524288 | tf_op jit(solution)/shard_map/all_to_all | solution.py:391
  70.3 0.7 last.1
  (1 shorter events, 0.0 us)
Async XLA Ops:
  2.3 15.0 %all-to-all-start = ((f32[8,8,16,128]{3,2,1,0:T(8,128)}), f32[8,8,16,128]{3,2,1,0:T(8,128)}, u32[]{:S(2)}, u32[]{:S(2)}) async-start(f32[8,8,16,128]{3,2,1,0:T(8,128)} %pack.1), calls=%async_computation | async-start | bytes 1048576 | tf_op jit(solution)/shard_map/all_to_all | solution.py:321
  7.7 1.4 %copy-start.1 = (f32[48,15,12,15]{0,3,2,1:T(8,128)S(1)}, f32[48,15,12,15]{0,3,2,1:T(8,128)}, u32[]{:S(2)}) copy-start(f32[48,15,12,15]{0,3,2,1:T(8,128)} %param.10) | copy-start | bytes 1555204
  9.1 0.7 copy-start.2
  17.3 0.9 %copy-start = (f32[36,1,8,128]{3,2,1,0:T(8,128)S(1)}, f32[36,1,8,128]{3,2,1,0:T(8,128)}, u32[]{:S(2)}) copy-start(f32[36,1,8,128]{3,2,1,0:T(8,128)} %param.8) | copy-start | bytes 442372
  19.4 14.2 %collective-permute-start.1 = (f32[3,168,128]{2,1,0:T(8,128)S(1)}, f32[3,168,128]{2,1,0:T(8,128)S(1)}, u32[]{:S(2)}, u32[]{:S(2)}) collective-permute-start(f32[3,168,128]{2,1,0:T(8,128)S(1)} %get-tuple-element.19), channel_id=1, source_target_pairs={{8,16},{16,8},{24,32},{32,24},{40,48},{48,40},{56,64},{64,56},{72,... | collective-permute-start | bytes 774152 | tf_op jit(solution)/shard_map/ppermute | solution.py:295
  21.6 12.0 %collective-permute-start = (f32[3,168,128]{2,1,0:T(8,128)S(1)}, f32[3,168,128]{2,1,0:T(8,128)S(1)}, u32[]{:S(2)}, u32[]{:S(2)}) collective-permute-start(f32[3,168,128]{2,1,0:T(8,128)S(1)} %get-tuple-element.19), channel_id=1, source_target_pairs={{0,8},{8,0},{16,24},{24,16},{32,40},{40,32},{48,56},{56,48},{64,72... | collective-permute-start | bytes 774152 | tf_op jit(solution)/shard_map/ppermute | solution.py:296
  36.9 9.8 %collective-permute-start.2 = (f32[128,128]{1,0:T(8,128)S(1)}, f32[128,128]{1,0:T(8,128)S(1)}, u32[]{:S(2)}, u32[]{:S(2)}) collective-permute-start(f32[128,128]{1,0:T(8,128)S(1)} %get-tuple-element.22), channel_id=1, source_target_pairs={{8,16},{16,8},{24,32},{32,24},{40,48},{48,40},{56,64},{64,56},{72,... | collective-permute-start | bytes 196616 | tf_op jit(solution)/shard_map/ppermute | solution.py:295
  39.3 7.4 %collective-permute-start.3 = (f32[128,128]{1,0:T(8,128)S(1)}, f32[128,128]{1,0:T(8,128)S(1)}, u32[]{:S(2)}, u32[]{:S(2)}) collective-permute-start(f32[128,128]{1,0:T(8,128)S(1)} %get-tuple-element.23), channel_id=1, source_target_pairs={{0,8},{8,0},{16,24},{24,16},{32,40},{40,32},{48,56},{56,48},{64,72... | collective-permute-start | bytes 196616 | tf_op jit(solution)/shard_map/ppermute | solution.py:296
  48.4 10.5 %collective-permute-start.4 = (f32[128,128]{1,0:T(8,128)S(1)}, f32[128,128]{1,0:T(8,128)S(1)}, u32[]{:S(2)}, u32[]{:S(2)}) collective-permute-start(f32[128,128]{1,0:T(8,128)S(1)} %get-tuple-element.27.to_a), channel_id=1, source_target_pairs={{8,16},{16,8},{24,32},{32,24},{40,48},{48,40},{56,64},{64,56},{72,... | collective-permute-start | bytes 196616 | tf_op jit(solution)/shard_map/ppermute | solution.py:295
  55.1 3.7 %collective-permute-start.5 = (f32[128,128]{1,0:T(8,128)S(1)}, f32[128,128]{1,0:T(8,128)S(1)}, u32[]{:S(2)}, u32[]{:S(2)}) collective-permute-start(f32[128,128]{1,0:T(8,128)S(1)} %get-tuple-element.28.to_b), channel_id=1, source_target_pairs={{0,8},{8,0},{16,24},{24,16},{32,40},{40,32},{48,56},{56,48},{64,72... | collective-permute-start | bytes 196616 | tf_op jit(solution)/shard_map/ppermute | solution.py:296

commit v7 on v6

--- a/solution.py
+++ b/solution.py
@@ -106,7 +106,7 @@
             send[(y + 1 - p) % NB, 5 + p] = r
 
 
-def side_kernel(me, got, coef, table, side, own, rows):
+def side_kernel(me, got, coef, table, side, own):
     del table
     for q in range(5):
         row = lax.rem(me[0] + q + NB - 2, NB)
@@ -116,12 +116,15 @@
         own[q] = c
         if 1 <= q <= 3:
             side[q - 1, ROWS:, :] = c
+    for q in range(1, 4):
+        for b in range(NB):
+            side[q - 1, b * MP : (b + 1) * MP, :] = got[b, q]
+
+
+def line_kernel(got, rows):
     for q in range(8):
         for b in range(NB):
-            x = got[b, q]
-            rows[q, b * MP : (b + 1) * MP, :] = x
-            if 1 <= q <= 3:
-                side[q - 1, b * MP : (b + 1) * MP, :] = x
+            rows[q, b * MP : (b + 1) * MP, :] = got[b, q]
 
 
 def put_columns(grad, tile, columns):
@@ -332,14 +335,15 @@
         specs=[SM, VM],
         cost=6 * tile_flops,
     )
-    side, own, line = call(
+    side, own = call(
         side_kernel,
         "side",
-        (struct(3, ROWS + CP, NX), struct(5, CP, NX), struct(8, ROWS, NX)),
+        (struct(3, ROWS + CP, NX), struct(5, CP, NX)),
         (me, got, coef.reshape(NK * NB, NX), table),
         specs=[SM, VM, VM, ANY],
     )
     side_a, side_b = swap(side, side)
+    line = call(line_kernel, "line", struct(8, ROWS, NX), (got,), cost=tile_flops)
     base = call(
         plane_kernel,
         "plane",

time: 71.5 us -> 71.5 us (level)
  waiting for transfers between devices: 5.74 us -> 4.03 us
  Pallas kernels: 25 us -> 26.1 us
    ppermute x3, waiting for transfers between devices: 4.46 us -> 2.75 us  [swap(): b = lax.ppermute(b, 'slab', pairs_b)]
    pallas_call x10 -> x11, Pallas kernels: 25 us -> 26.1 us  [call(): pl.pallas_call(kernel, out_shape=outs, in_specs=specs or [VM] * len(ins),...]
  transfers between devices with their start and end apart: 7 -> 7, of which waited for: 4 -> 3; matrix products, arithmetic and copies ran while one was open for 0% -> 0% of each run, Pallas kernels for 23% -> 25%
where the time goes in v7:
time: 71.5 us; the launch traced here: 70.9 us
  Pallas kernels  26.1 us (37%)
  starting transfers between devices  25.6 us (36%)
  blocking collectives  11.4 us (16%)
  waiting for transfers between devices  4.03 us (6%)
  local copies, waits for them, and re-layouts  2.96 us (4%)
  between operations  0.76 us (1%)
    pallas_call x11, Pallas kernels, call(): pl.pallas_call(kernel, out_shape=outs, in_specs=specs or [VM] * len(ins),...  26.1 us
    ppermute x3, starting transfers between devices, swap(): b = lax.ppermute(b, 'slab', pairs_b)  12 us
    all_to_all x1, blocking collectives, body(): got = lax.all_to_all(send, 'chaos', 0, 0, tiled=True)  11.4 us
    ppermute x3, starting transfers between devices, swap(): return (lax.ppermute(a, 'slab', pairs_a), b)  8.27 us
    all_to_all x1, starting transfers between devices, body(): got = lax.all_to_all(send, 'chaos', 0, 0, tiled=True)  5.32 us
    unnamed x6, local copies, waits for them, and re-layouts  2.96 us
    ppermute x3, waiting for transfers between devices, swap(): b = lax.ppermute(b, 'slab', pairs_b)  2.75 us
  transfers between devices with their start and end apart: 7, of which 3 were waited for; matrix products, arithmetic and copies ran while one was open for 0% of the time, Pallas kernels for 25%

profile of v7, /device:TPU:256, one launch (start us, length us, event | category | flops | bytes accessed | tf_op | source)
XLA Modules:
  0.0 70.9 jit_solution(16467672252486503901)
XLA Ops:
  0.6 1.7 %pack.1 = f32[8,8,16,128]{3,2,1,0:T(8,128)} custom-call(f32[120,128]{1,0:T(8,128)} %bitcast.16, f32[120,128]{1,0:T(8,128)} %bitcast.17), custom_call_target="tpu_custom_call" | custom-call | tf_op jit(solution)/shard_map/pack/pallas_call | solution.py:37
  2.3 5.3 %all-to-all-start = ((f32[8,8,16,128]{3,2,1,0:T(8,128)}), f32[8,8,16,128]{3,2,1,0:T(8,128)}, u32[]{:S(2)}, u32[]{:S(2)}) async-start(f32[8,8,16,128]{3,2,1,0:T(8,128)} %pack.1), calls=%async_computation | async-start | bytes 1048576 | tf_op jit(solution)/shard_map/all_to_all | solution.py:324
  7.7 0.1 pad_add_fusion.me
  7.7 0.0 copy-start.1
  7.7 1.4 %copy-done.1 = f32[48,15,12,15]{0,3,2,1:T(8,128)S(1)} copy-done((f32[48,15,12,15]{0,3,2,1:T(8,128)S(1)}, f32[48,15,12,15]{0,3,2,1:T(8,128)}, u32[]{:S(2)}) %copy-start.1) | copy-done | bytes 518424
  9.1 0.0 copy-start.2
  9.1 0.7 copy-done.2
  9.8 6.3 %table.1 = bf16[4608,384]{1,0:T(8,128)(2,1)S(1)} custom-call(s32[3,48]{1,0:T(4,128)S(1)} %bitcast.15, f32[15,12,15,48]{3,2,1,0:T(8,128)S(1)} %bitcast.14), custom_call_target="tpu_custom_call" | custom-call | flops 5435817984 | bytes 4194304 | tf_op jit(solution)/shard_map/table/pallas_call | solution.py:37
  16.1 1.3 %all-to-all-done.got = f32[8,8,16,128]{3,2,1,0:T(8,128)} async-done(((f32[8,8,16,128]{3,2,1,0:T(8,128)}), f32[8,8,16,128]{3,2,1,0:T(8,128)}, u32[]{:S(2)}, u32[]{:S(2)}) %all-to-all-start) | async-done | bytes 524320 | tf_op jit(solution)/shard_map/all_to_all | solution.py:324
  17.3 0.0 copy-start
  17.3 0.9 %copy-done = f32[36,1,8,128]{3,2,1,0:T(8,128)S(1)} copy-done((f32[36,1,8,128]{3,2,1,0:T(8,128)S(1)}, f32[36,1,8,128]{3,2,1,0:T(8,128)}, u32[]{:S(2)}) %copy-start) | copy-done | bytes 147480
  18.2 1.1 %side.1 = (f32[3,168,128]{2,1,0:T(8,128)S(1)}, f32[5,40,128]{2,1,0:T(8,128)S(1)}) custom-call(s32[2]{0:T(128)S(1)} %pad_add_fusion.me, f32[8,8,16,128]{3,2,1,0:T(8,128)} %all-to-all-done.got, f32[288,128]{1,0:T(8,128)S(1)} %bitcast.13, bf16[4608,384]{1,0:T(8,128)(2,1)S(1)} %table.1), custom_call_target="tpu_custom_call" | custom-call | tf_op jit(solution)/shard_map/side/pallas_call | solution.py:37
  19.3 2.3 %collective-permute-start.1 = (f32[3,168,128]{2,1,0:T(8,128)S(1)}, f32[3,168,128]{2,1,0:T(8,128)S(1)}, u32[]{:S(2)}, u32[]{:S(2)}) collective-permute-start(f32[3,168,128]{2,1,0:T(8,128)S(1)} %get-tuple-element.17), channel_id=1, source_target_pairs={{8,16},{16,8},{24,32},{32,24},{40,48},{48,40},{56,64},{64,56},{72,... | collective-permute-start | bytes 774152 | tf_op jit(solution)/shard_map/ppermute | solution.py:298
  21.6 4.2 %collective-permute-start = (f32[3,168,128]{2,1,0:T(8,128)S(1)}, f32[3,168,128]{2,1,0:T(8,128)S(1)}, u32[]{:S(2)}, u32[]{:S(2)}) collective-permute-start(f32[3,168,128]{2,1,0:T(8,128)S(1)} %get-tuple-element.17), channel_id=1, source_target_pairs={{0,8},{8,0},{16,24},{24,16},{32,40},{40,32},{48,56},{56,48},{64,72... | collective-permute-start | bytes 774152 | tf_op jit(solution)/shard_map/ppermute | solution.py:299
  25.9 1.1 %line.1 = f32[8,128,128]{2,1,0:T(8,128)S(1)} custom-call(f32[8,8,16,128]{3,2,1,0:T(8,128)} %all-to-all-done.got), custom_call_target="tpu_custom_call" | custom-call | flops 905969664 | bytes 4194304 | tf_op jit(solution)/shard_map/line/pallas_call | solution.py:37
  27.0 4.5 %plane.1.base = f32[3,128,128]{2,1,0:T(8,128)S(1)} custom-call(f32[8,128,128]{2,1,0:T(8,128)S(1)} %line.1, f32[5,40,128]{2,1,0:T(8,128)S(1)} %get-tuple-element.18.own, bf16[4608,384]{1,0:T(8,128)(2,1)S(1)} %table.1), custom_call_target="tpu_custom_call" | custom-call | flops 2717908992 | bytes 4194304 | tf_op jit(solution)/shard_map/plane/pallas_call | solution.py:37
  31.4 2.1 %collective-permute-done.1.side_b = f32[3,168,128]{2,1,0:T(8,128)S(1)} collective-permute-done((f32[3,168,128]{2,1,0:T(8,128)S(1)}, f32[3,168,128]{2,1,0:T(8,128)S(1)}, u32[]{:S(2)}, u32[]{:S(2)}) %collective-permute-start.1) | collective-permute-done | bytes 258080 | tf_op jit(solution)/shard_map/ppermute | solution.py:298
  33.6 0.0 collective-permute-done.side_a
  33.6 3.3 %first.1 = (f32[128,128]{1,0:T(8,128)S(1)}, f32[128,128]{1,0:T(8,128)S(1)}, f32[128,128]{1,0:T(8,128)S(1)}, f32[128,128]{1,0:T(8,128)S(1)}, f32[6,40,128]{2,1,0:T(8,128)S(1)}) custom-call(s32[2]{0:T(128)S(1)} %pad_add_fusion.me, f32[8,128,128]{2,1,0:T(8,128)S(1)} %line.1, f32[3,168,128]{2,1,0:T(8,128)S(1)} %collective-permute-done.side_a, ...), custom_call_target="tpu_custom_call" | custom-call | flops 1811939328 | bytes 4194304 | tf_op jit(solution)/shard_map/first/pallas_call | solution.py:37
  36.9 3.1 %collective-permute-start.2 = (f32[128,128]{1,0:T(8,128)S(1)}, f32[128,128]{1,0:T(8,128)S(1)}, u32[]{:S(2)}, u32[]{:S(2)}) collective-permute-start(f32[128,128]{1,0:T(8,128)S(1)} %get-tuple-element.20), channel_id=1, source_target_pairs={{8,16},{16,8},{24,32},{32,24},{40,48},{48,40},{56,64},{64,56},{72,... | collective-permute-start | bytes 196616 | tf_op jit(solution)/shard_map/ppermute | solution.py:298
  40.0 2.1 %collective-permute-start.3 = (f32[128,128]{1,0:T(8,128)S(1)}, f32[128,128]{1,0:T(8,128)S(1)}, u32[]{:S(2)}, u32[]{:S(2)}) collective-permute-start(f32[128,128]{1,0:T(8,128)S(1)} %get-tuple-element.21), channel_id=1, source_target_pairs={{0,8},{8,0},{16,24},{24,16},{32,40},{40,32},{48,56},{56,48},{64,72... | collective-permute-start | bytes 196616 | tf_op jit(solution)/shard_map/ppermute | solution.py:299
  42.1 4.6 %second.1.full = f32[128,128]{1,0:T(8,128)S(1)} custom-call(s32[2]{0:T(128)S(1)} %pad_add_fusion.me, f32[8,128,128]{2,1,0:T(8,128)S(1)} %line.1, f32[3,168,128]{2,1,0:T(8,128)S(1)} %collective-permute-done.side_a, f32[3,168,128]{2,1,0:T(8,128)S(1)} %collective-permute-done.1.side_b, f32[5,40,128]{2,1,0:T(8,128)S(1)} %get-tuple-element.18.own, ...), custom_call_target="tpu_custom_call" | custom-call | flops 2717908992 | bytes 4194304 | tf_op jit(solution)/shard_map/second/pallas_call | solution.py:37
  46.7 0.0 collective-permute-done.2.from_a
  46.7 0.0 collective-permute-done.3.from_b
  46.7 1.6 %third.1 = (f32[128,128]{1,0:T(8,128)S(1)}, f32[128,128]{1,0:T(8,128)S(1)}, f32[128,128]{1,0:T(8,128)S(1)}) custom-call(s32[2]{0:T(128)S(1)} %pad_add_fusion.me, f32[128,128]{1,0:T(8,128)S(1)} %get-tuple-element.19.one, f32[128,128]{1,0:T(8,128)S(1)} %collective-permute-done.2.from_a, f32[128,128]{1,0:T(8,128)S(1)} %collective-permute-done.3.from_b, ...), custom_call_target="tpu_custom_call" | custom-call | flops 905969664 | bytes 4194304 | tf_op jit(solution)/shard_map/third/pallas_call | solution.py:37
  48.4 6.7 %collective-permute-start.4 = (f32[128,128]{1,0:T(8,128)S(1)}, f32[128,128]{1,0:T(8,128)S(1)}, u32[]{:S(2)}, u32[]{:S(2)}) collective-permute-start(f32[128,128]{1,0:T(8,128)S(1)} %get-tuple-element.25.to_a), channel_id=1, source_target_pairs={{8,16},{16,8},{24,32},{32,24},{40,48},{48,40},{56,64},{64,56},{72,... | collective-permute-start | bytes 196616 | tf_op jit(solution)/shard_map/ppermute | solution.py:298
  55.1 1.9 %collective-permute-start.5 = (f32[128,128]{1,0:T(8,128)S(1)}, f32[128,128]{1,0:T(8,128)S(1)}, u32[]{:S(2)}, u32[]{:S(2)}) collective-permute-start(f32[128,128]{1,0:T(8,128)S(1)} %get-tuple-element.26.to_b), channel_id=1, source_target_pairs={{0,8},{8,0},{16,24},{24,16},{32,40},{40,32},{48,56},{56,48},{64,72... | collective-permute-start | bytes 196616 | tf_op jit(solution)/shard_map/ppermute | solution.py:299
  57.0 1.2 %fourth.1 = (f32[128,128]{1,0:T(8,128)S(1)}, f32[128,128]{1,0:T(8,128)S(1)}, f32[128,128]{1,0:T(8,128)S(1)}) custom-call(f32[128,128]{1,0:T(8,128)S(1)} %get-tuple-element.24.mid, f32[128,128]{1,0:T(8,128)S(1)} %get-tuple-element.25.to_a, f32[128,128]{1,0:T(8,128)S(1)} %get-tuple-element.26.to_b, f32[8,128,128]{2,1,0:T(8,128)S(1)} %line.1, ...), custom_call_target="tpu_custom_call" | custom-call | flops 905969664 | bytes 4194304 | tf_op jit(solution)/shard_map/fourth/pallas_call | solution.py:37
  58.2 0.6 collective-permute-done.4.from_a
  58.8 0.0 collective-permute-done.5.from_b
  58.9 11.4 %all_to_all.10.got = f32[8,4,16,128]{3,2,1,0:T(8,128)S(1)} all-to-all(f32[8,4,16,128]{3,2,1,0:T(8,128)S(1)} %back.1), channel_id=1, replica_groups=mesh['slab'=64,'chaos'=8] {'chaos'}, dimensions={0} | all-to-all | bytes 524288 | tf_op jit(solution)/shard_map/all_to_all | solution.py:395
  70.3 0.7 last.1
  (1 shorter events, 0.0 us)
Async XLA Ops:
  2.3 15.0 %all-to-all-start = ((f32[8,8,16,128]{3,2,1,0:T(8,128)}), f32[8,8,16,128]{3,2,1,0:T(8,128)}, u32[]{:S(2)}, u32[]{:S(2)}) async-start(f32[8,8,16,128]{3,2,1,0:T(8,128)} %pack.1), calls=%async_computation | async-start | bytes 1048576 | tf_op jit(solution)/shard_map/all_to_all | solution.py:324
  7.7 1.4 %copy-start.1 = (f32[48,15,12,15]{0,3,2,1:T(8,128)S(1)}, f32[48,15,12,15]{0,3,2,1:T(8,128)}, u32[]{:S(2)}) copy-start(f32[48,15,12,15]{0,3,2,1:T(8,128)} %param.10) | copy-start | bytes 1555204
  9.1 0.7 copy-start.2
  17.3 0.9 %copy-start = (f32[36,1,8,128]{3,2,1,0:T(8,128)S(1)}, f32[36,1,8,128]{3,2,1,0:T(8,128)}, u32[]{:S(2)}) copy-start(f32[36,1,8,128]{3,2,1,0:T(8,128)} %param.8) | copy-start | bytes 442372
  19.3 14.2 %collective-permute-start.1 = (f32[3,168,128]{2,1,0:T(8,128)S(1)}, f32[3,168,128]{2,1,0:T(8,128)S(1)}, u32[]{:S(2)}, u32[]{:S(2)}) collective-permute-start(f32[3,168,128]{2,1,0:T(8,128)S(1)} %get-tuple-element.17), channel_id=1, source_target_pairs={{8,16},{16,8},{24,32},{32,24},{40,48},{48,40},{56,64},{64,56},{72,... | collective-permute-start | bytes 774152 | tf_op jit(solution)/shard_map/ppermute | solution.py:298
  21.6 12.0 %collective-permute-start = (f32[3,168,128]{2,1,0:T(8,128)S(1)}, f32[3,168,128]{2,1,0:T(8,128)S(1)}, u32[]{:S(2)}, u32[]{:S(2)}) collective-permute-start(f32[3,168,128]{2,1,0:T(8,128)S(1)} %get-tuple-element.17), channel_id=1, source_target_pairs={{0,8},{8,0},{16,24},{24,16},{32,40},{40,32},{48,56},{56,48},{64,72... | collective-permute-start | bytes 774152 | tf_op jit(solution)/shard_map/ppermute | solution.py:299
  36.9 9.8 %collective-permute-start.2 = (f32[128,128]{1,0:T(8,128)S(1)}, f32[128,128]{1,0:T(8,128)S(1)}, u32[]{:S(2)}, u32[]{:S(2)}) collective-permute-start(f32[128,128]{1,0:T(8,128)S(1)} %get-tuple-element.20), channel_id=1, source_target_pairs={{8,16},{16,8},{24,32},{32,24},{40,48},{48,40},{56,64},{64,56},{72,... | collective-permute-start | bytes 196616 | tf_op jit(solution)/shard_map/ppermute | solution.py:298
  40.0 6.8 %collective-permute-start.3 = (f32[128,128]{1,0:T(8,128)S(1)}, f32[128,128]{1,0:T(8,128)S(1)}, u32[]{:S(2)}, u32[]{:S(2)}) collective-permute-start(f32[128,128]{1,0:T(8,128)S(1)} %get-tuple-element.21), channel_id=1, source_target_pairs={{0,8},{8,0},{16,24},{24,16},{32,40},{40,32},{48,56},{56,48},{64,72... | collective-permute-start | bytes 196616 | tf_op jit(solution)/shard_map/ppermute | solution.py:299
  48.4 10.4 %collective-permute-start.4 = (f32[128,128]{1,0:T(8,128)S(1)}, f32[128,128]{1,0:T(8,128)S(1)}, u32[]{:S(2)}, u32[]{:S(2)}) collective-permute-start(f32[128,128]{1,0:T(8,128)S(1)} %get-tuple-element.25.to_a), channel_id=1, source_target_pairs={{8,16},{16,8},{24,32},{32,24},{40,48},{48,40},{56,64},{64,56},{72,... | collective-permute-start | bytes 196616 | tf_op jit(solution)/shard_map/ppermute | solution.py:298
  55.1 3.7 %collective-permute-start.5 = (f32[128,128]{1,0:T(8,128)S(1)}, f32[128,128]{1,0:T(8,128)S(1)}, u32[]{:S(2)}, u32[]{:S(2)}) collective-permute-start(f32[128,128]{1,0:T(8,128)S(1)} %get-tuple-element.26.to_b), channel_id=1, source_target_pairs={{0,8},{8,0},{16,24},{24,16},{32,40},{40,32},{48,56},{56,48},{64,72... | collective-permute-start | bytes 196616 | tf_op jit(solution)/shard_map/ppermute | solution.py:299
